TPU v7x, 32 devices: a whole 2x2x4 slice. The times are simulated.
32 devices in a mesh: groups: 2 (over x), leaf: 16 (over z, y, core).
Axes of the slice: x: 2, y: 2, z: 4, core: 2. Of those that a mesh axis runs over, the one named last changes fastest.
Arguments:
- queries: bfloat16 [8192, 2560], P(('groups', 'leaf')), parts along dimension 0, may hold values from -5 to 5
- keys: bfloat16 [8192, 512], P(('groups', 'leaf')), parts along dimension 0, may hold values from -5 to 5
- values: bfloat16 [8192, 512], P(('groups', 'leaf')), parts along dimension 0, may hold values from -6 to 6
- saved_out: bfloat16 [8192, 2560], P(('groups', 'leaf')), parts along dimension 0, may hold values from -3 to 3
- grad_out: bfloat16 [8192, 2560], P(('groups', 'leaf')), parts along dimension 0, may hold values from -60 to 60
- parents: int32 [32], P('groups'), parts along dimension 0, may hold values from -1 to 15, as said below
- assignment: int32 [32], P('groups'), parts along dimension 0, may hold values from 0 to 15, each once
- lengths: int32 [32], P('groups'), parts along dimension 0, may hold values from 64 to 256, as said below
Outputs:
- query_grad: bfloat16 [8192, 2560], P(('groups', 'leaf')), parts along dimension 0
- key_grad: bfloat16 [8192, 512], P(('groups', 'leaf')), parts along dimension 0
- value_grad: bfloat16 [8192, 512], P(('groups', 'leaf')), parts along dimension 0
There are 2 independent parts, one for each index of `groups`. A program takes and returns all parts, laid end to end along the dimension named above; each array names one. Nothing has to cross between parts.
Inputs may be any that keep to these rules, and one draw needn't show every extreme that they name: parents[s] is the segment that segment s continues, -1 for segment 0 alone; segments 0 to 1 are the root prompt, each continuing the one before; every chain of ancestors holds at most 5 segments, and some segment's holds exactly that many. lengths[s] counts the live tokens of segment s from its start; the root prompt's segments are full.
All inputs are finite; a program needn't handle non-finite values.
Results may differ from a plain program's by a relative error of at most 0.0052.
Values may be sent and summed in bfloat16 or wider, within the bound.
No kernel may reach another device: no remote copies, remote signals or barrier semaphores. Data moves between devices by JAX's collectives and lax.ppermute only.
A program may use at most 128 MiB of HBM per device.

v0:
```python
import functools
import math

import jax
import jax.numpy as jnp
from jax import lax
from jax.experimental import pallas as pl
from jax.experimental.pallas import tpu as pltpu
from jax.sharding import PartitionSpec as P

HQ = 20
HK = 4
DH = 128
PER = HQ // HK
HALF = HK // 2
WIDE = PER * DH
ANCESTORS = 5
SLOTS = ANCESTORS + 1
OWN = 1 << 20
SCALE = 1.0 / math.sqrt(DH)
EXP_SCALE = SCALE / math.log(2.0)
NN = (((1,), (0,)), ((), ()))
SMEM = pl.BlockSpec(memory_space=pltpu.SMEM)
HBM = pl.BlockSpec(memory_space=pl.ANY)
VMEM = pl.BlockSpec(memory_space=pltpu.VMEM)


def dot(a, b):
    return lax.dot_general(a, b, NN, preferred_element_type=jnp.float32)


def ring_order(chips):
    if chips == 8:
        return [0, 2, 4, 6, 7, 5, 3, 1]
    return list(range(chips))


def walk(device, me, places, parents, assignment, lengths, owner, plan, side):
    chips = places.shape[0]
    here = places[me // 2]

    def place(held):
        at = places[held // 2] - here
        at = jnp.where(at < 0, at + chips, at)
        return side * 2 * chips + at * 2 + jnp.where(held % 2 == me % 2, 0, 1)

    def clear(at, carry):
        plan[side * 2 * chips + at] = 0
        return carry

    lax.fori_loop(0, 2 * chips, clear, 0)
    segment = assignment[device]
    plan[place(device)] = OWN
    up = parents[segment]
    for _ in range(ANCESTORS):
        at = jnp.maximum(up, 0)

        @pl.when(up >= 0)
        def _():
            plan[place(owner[at])] = lengths[at]

        up = jnp.where(up >= 0, parents[at], -1)


def run_copies(pairs, sems):
    copies = [pltpu.make_async_copy(a, b, sems.at[i]) for i, (a, b) in enumerate(pairs)]
    for copy in copies:
        copy.start()
    return copies


def column_of(me, head, h):
    return pl.multiple_of(((me % 2 * HALF + head) * PER + h) * DH, DH)


def seen_keys(rows, sees):
    lane_at = lax.broadcasted_iota(jnp.int32, (1, rows), 1)
    key_at = lax.broadcasted_iota(jnp.int32, (rows, 1), 0)
    return key_at <= jnp.where(sees == OWN, lane_at, sees - 1)


def measure_blocks(plan, offsets, kv_ref, qt_ref, top_ref, sum_ref):
    rows = kv_ref.shape[1] // 2
    chips = plan.shape[0] // 4
    for slot, offset in enumerate(offsets):
        def visit(i, carry):
            half, side = i // 2, i % 2
            sees = plan[side * 2 * chips + offset * 2 + half]

            @pl.when(sees > 0)
            def _():
                seen = seen_keys(rows, sees)
                keys = kv_ref[slot, pl.ds(pl.multiple_of(half * rows, rows), rows), :DH]
                for h in range(PER):
                    at = (side, slice(None), slice(h * rows, (h + 1) * rows))
                    s = jnp.where(seen, dot(keys, qt_ref[at]), -1e30)
                    old = top_ref[at]
                    top = jnp.maximum(old, jnp.max(s, axis=0, keepdims=True))
                    total = jnp.sum(jnp.exp2((s - top) * EXP_SCALE), axis=0, keepdims=True)
                    top_ref[at] = top
                    sum_ref[at] = sum_ref[at] * jnp.exp2((old - top) * EXP_SCALE) + total

            return carry

        lax.fori_loop(0, 4, visit, 0)


def prepare_kernel(head, me_ref, places, parents, assignment, lengths, queries, grads, saved, other, block, *refs):
    (plan, qt_ref, gt_ref, gm_ref, qm_ref, delta_ref, top_ref, sum_ref,
     owner, q_ref, g_ref, o_ref, kv_ref, sems) = refs
    rows = queries.shape[0]
    me = me_ref[0]
    column = pl.multiple_of((me % 2 * HALF + head) * WIDE, WIDE)
    pairs = [(block, kv_ref.at[0])]
    for at, (array, held) in enumerate(zip((queries, grads, saved), (q_ref, g_ref, o_ref))):
        pairs.append((array.at[:, pl.ds(column, WIDE)], held.at[0]))
        first = (at * HALF + head) * WIDE
        pairs.append((other.at[:, first:first + WIDE], held.at[1]))
    copies = run_copies(pairs, sems)

    def invert(d, carry):
        owner[assignment[d]] = d
        return carry

    lax.fori_loop(0, assignment.shape[0], invert, 0)
    walk(me, me, places, parents, assignment, lengths, owner, plan, 0)
    walk(me + 1 - me % 2 * 2, me, places, parents, assignment, lengths, owner, plan, 1)
    row_at = lax.broadcasted_iota(jnp.int32, (rows, 1), 0)
    top_ref[...] = jnp.full(top_ref.shape, -1e30, top_ref.dtype)
    sum_ref[...] = jnp.zeros_like(sum_ref)
    for copy in copies:
        copy.wait()
    for side, device in enumerate((me, me + 1 - me % 2 * 2)):
        live = row_at < lengths[assignment[device]]
        for h in range(PER):
            lanes = slice(h * rows, (h + 1) * rows)
            cols = slice(h * DH, (h + 1) * DH)
            masked = jnp.where(live, g_ref[side, :, cols], jnp.zeros((), g_ref.dtype))
            query = q_ref[side, :, cols]
            gm_ref[side, lanes, :] = masked
            qm_ref[side, lanes, :] = query
            gt_ref[side, :, lanes] = masked.T
            qt_ref[side, :, lanes] = query.T
            terms = masked.astype(jnp.float32) * o_ref[side, :, cols].astype(jnp.float32)
            delta_ref[side, :, lanes] = jnp.sum(terms.T, axis=0, keepdims=True)
    measure_blocks(plan, [0], kv_ref, qt_ref, top_ref, sum_ref)


def row_stats(rows):
    return jax.ShapeDtypeStruct((2, 1, PER * rows), jnp.float32)


def prepare(head, tables, mine, other, block):
    rows = other.shape[0]
    chips = tables[1].shape[0]
    bf16 = jnp.bfloat16
    return pl.pallas_call(
        functools.partial(prepare_kernel, head),
        in_specs=[SMEM] * 5 + [HBM] * 5,
        out_specs=[SMEM] + [VMEM] * 7,
        out_shape=[
            jax.ShapeDtypeStruct((4 * chips,), jnp.int32),
            jax.ShapeDtypeStruct((2, DH, PER * rows), bf16),
            jax.ShapeDtypeStruct((2, DH, PER * rows), bf16),
            jax.ShapeDtypeStruct((2, PER * rows, DH), bf16),
            jax.ShapeDtypeStruct((2, PER * rows, DH), bf16),
            row_stats(rows),
            row_stats(rows),
            row_stats(rows),
        ],
        scratch_shapes=[pltpu.SMEM(tables[3].shape, jnp.int32)]
        + [pltpu.VMEM((2, rows, WIDE), bf16)] * 3
        + [pltpu.VMEM((1, 2 * rows, 2 * DH), bf16), pltpu.SemaphoreType.DMA((7,))],
        compiler_params=pltpu.CompilerParams(vmem_limit_bytes=16 << 20),
        cost_estimate=pl.CostEstimate(flops=0, bytes_accessed=12 << 20, transcendentals=0),
    )(*tables, *mine, other, block)


def measure_kernel(offsets, plan, qt_ref, top_in, sum_in, *refs):
    count = len(offsets)
    blocks, (top_ref, sum_ref, kv_ref, sems) = refs[:count], refs[count:]
    copies = run_copies([(held, kv_ref.at[i]) for i, held in enumerate(blocks)], sems)
    top_ref[...] = top_in[...]
    sum_ref[...] = sum_in[...]
    for copy in copies:
        copy.wait()
    measure_blocks(plan, offsets, kv_ref, qt_ref, top_ref, sum_ref)


def measure(offsets, prepared, stats, blocks):
    rows = blocks[0].shape[0] // 2
    plan, qt = prepared[:2]
    return pl.pallas_call(
        functools.partial(measure_kernel, offsets),
        in_specs=[SMEM] + [VMEM] * 3 + [HBM] * len(blocks),
        out_specs=[VMEM] * 2,
        out_shape=[row_stats(rows)] * 2,
        scratch_shapes=[
            pltpu.VMEM((len(offsets), 2 * rows, 2 * DH), jnp.bfloat16),
            pltpu.SemaphoreType.DMA((len(blocks),)),
        ],
        compiler_params=pltpu.CompilerParams(vmem_limit_bytes=12 << 20),
        cost_estimate=pl.CostEstimate(flops=0, bytes_accessed=8 << 20, transcendentals=0),
    )(plan, qt, *stats, *blocks)


def grads_kernel(chips, offsets, first, last, plan, *refs):
    far = chips // 2
    shared = []
    for head in range(HALF):
        shared.append(refs[:6 + first])
        refs = refs[6 + first:]
    blocks = []
    for head in range(HALF):
        blocks.append(refs[:len(offsets) + first])
        refs = refs[len(offsets) + first:]
    carried = None
    if not first:
        carried, refs = refs[0], refs[1:]
    terms, refs = refs[:HALF], refs[HALF:]
    if first:
        ups, downs, refs = refs[:HALF], refs[HALF:2 * HALF], refs[2 * HALF:]
        lse_out, refs = refs[:HALF], refs[HALF:]
    outs, refs = refs[:2 if last else 1], refs[2 if last else 1:]
    (kv_ref, acc_ref, stage_ref, zero_ref, p_ref, ds_ref, sum_ref, dqt_ref, offset_ref,
     sems, kv_sems, out_sems, zero_sems) = refs
    lse_ref = lse_out if first else [head[5] for head in shared]
    if not last:
        dqt_ref = outs[0]
    rows = acc_ref.shape[1]
    slots = stage_ref.shape[0]

    pairs = []
    for head in range(HALF):
        for slot, offset in enumerate(offsets):
            offset_ref[slot] = offset
            if offset == far:
                pairs.append((blocks[head][0], kv_ref.at[slot, head, :rows]))
                pairs.append((blocks[head][1], kv_ref.at[slot, head, rows:]))
            else:
                pltpu.make_async_copy(
                    blocks[head][slot + first], kv_ref.at[slot, head], kv_sems.at[slot, head]
                ).start()
    copies = run_copies(pairs, sems)
    zero_ref[...] = jnp.zeros_like(zero_ref)

    def sees(side, i):
        return plan[side * 2 * chips + offset_ref[i // 2] * 2 + i % 2]

    def seen(i):
        return (sees(0, i) > 0) | (sees(1, i) > 0)

    def send(i, sources, sem_of):
        at_block, half = i // 2, i % 2
        here = pl.ds(pl.multiple_of(half * rows, rows), rows)
        for head in range(HALF):
            def put(target):
                pltpu.make_async_copy(sources[head], target, sem_of(head)).start()

            if not first:
                put(terms[head].at[at_block, here])
                continue

            @pl.when(i >= 2)
            def _():
                put(terms[head].at[at_block, here])

            @pl.when(i == 0)
            def _():
                put(ups[head])

            @pl.when(i == 1)
            def _():
                put(downs[head])

    def sent(sem_of):
        for head in range(HALF):
            pltpu.make_async_copy(zero_ref, terms[head].at[0, :rows], sem_of(head)).wait()

    def send_zeros(i, carry):
        @pl.when(jnp.logical_not(seen(i)))
        def _():
            send(i, [zero_ref] * HALF, lambda head: zero_sems.at[i, head])

        return carry

    lax.fori_loop(0, 2 * len(offsets), send_zeros, 0)
    dqt_ref[...] = jnp.zeros_like(dqt_ref) if first else carried[...]
    for copy in copies:
        copy.wait()
    if first:
        for head in range(HALF):
            top_ref, total_ref = lse_out[head], sum_ref.at[head]
            top_ref[...] = shared[head][5][...]
            total_ref[...] = shared[head][6][...]
            measure_blocks(plan, [far], kv_ref.at[:, head], shared[head][0], top_ref, total_ref)
            top_ref[...] = top_ref[...] * EXP_SCALE + jnp.log2(total_ref[...])

    def visit(i, done):
        at_block, half = i // 2, i % 2
        here = pl.ds(pl.multiple_of(half * rows, rows), rows)

        @pl.when((half == 0) & (offset_ref[at_block] != far))
        def _():
            for head in range(HALF):
                pltpu.make_async_copy(
                    blocks[head][-1], kv_ref.at[at_block, head], kv_sems.at[at_block, head]
                ).wait()

        def look(side, carry):
            @pl.when(sees(side, i) > 0)
            def _():
                allowed = seen_keys(rows, sees(side, i))
                for head in range(HALF):
                    qt_ref, gt_ref, gm_ref, qm_ref, delta_ref = shared[head][:5]
                    k = kv_ref[at_block, head, here, :DH]
                    v = kv_ref[at_block, head, here, DH:]
                    for h in range(PER):
                        lanes = slice(h * rows, (h + 1) * rows)
                        part = (side, slice(None), lanes)
                        s = dot(k, qt_ref[part]) * EXP_SCALE - lse_ref[head][part]
                        p = jnp.where(allowed, jnp.exp2(s), 0.0)
                        ds = p * (dot(v, gt_ref[part]) - delta_ref[part])
                        p_ref[head, :, lanes] = p.astype(p_ref.dtype)
                        ds_ref[head, :, lanes] = ds.astype(ds_ref.dtype)
                    acc_ref[head, :, DH:] += dot(p_ref[head], gm_ref[side])
                    acc_ref[head, :, :DH] += dot(ds_ref[head], qm_ref[side])
                    dqt_ref[head, side] += dot(k.T, ds_ref[head])

            return carry

        @pl.when(seen(i))
        def _():
            slot = done % slots

            @pl.when(done >= slots)
            def _():
                sent(lambda head: out_sems.at[slot, head])

            acc_ref[...] = jnp.zeros_like(acc_ref)
            lax.fori_loop(0, 2, look, 0)
            for head in range(HALF):
                stage_ref[slot, head, :, :DH] = (acc_ref[head, :, :DH] * SCALE).astype(stage_ref.dtype)
                stage_ref[slot, head, :, DH:] = acc_ref[head, :, DH:].astype(stage_ref.dtype)
            send(i, [stage_ref.at[slot, head] for head in range(HALF)], lambda head: out_sems.at[slot, head])

        return done + seen(i).astype(jnp.int32)

    done = lax.fori_loop(0, 2 * len(offsets), visit, jnp.int32(0))
    if last:
        for side, dq_ref in enumerate(outs):
            for head in range(HALF):
                for h in range(PER):
                    dq = (dqt_ref[head, side, :, h * rows:(h + 1) * rows] * SCALE).astype(dq_ref.dtype)
                    dq_ref[:, (head * PER + h) * DH:(head * PER + h + 1) * DH] = dq.T

    def zeros_sent(i, carry):
        @pl.when(jnp.logical_not(seen(i)))
        def _():
            sent(lambda head: zero_sems.at[i, head])

        return carry

    lax.fori_loop(0, 2 * len(offsets), zeros_sent, 0)
    for slot in range(slots):
        @pl.when(done > slot)
        def _():
            sent(lambda head: out_sems.at[slot, head])


def gradients(prepared, stats, offsets, blocks, carried, last):
    plan = prepared[0][0]
    chips = plan.shape[0] // 4
    rows = blocks[0][-1].shape[0] // 2
    first = carried is None
    bf16, f32 = jnp.bfloat16, jnp.float32
    shared = [(*prepared[head][1:6], *stats[head]) for head in range(HALF)]
    arrays = [a for head in shared for a in head] + [a for head in blocks for a in head]
    arrays += [] if first else [carried]
    dense = jax.ShapeDtypeStruct((len(offsets), 2 * rows, 2 * DH), bf16)
    piece = jax.ShapeDtypeStruct((rows, 2 * DH), bf16)
    query = jax.ShapeDtypeStruct((rows, HALF * WIDE), bf16)
    sums = jax.ShapeDtypeStruct((HALF, 2, DH, PER * rows), f32)
    out_shape, out_specs = [dense] * HALF, [HBM] * HALF
    if first:
        out_shape += [piece] * (2 * HALF) + [row_stats(rows)] * HALF
        out_specs += [HBM] * (2 * HALF) + [VMEM] * HALF
    out_shape += [query] * 2 if last else [sums]
    out_specs += [VMEM] * (2 if last else 1)
    flat = sum(len(head) for head in shared)
    in_specs = [SMEM] + [VMEM] * flat + [HBM] * (len(arrays) - flat)
    if not first:
        in_specs[-1] = VMEM
    return pl.pallas_call(
        functools.partial(grads_kernel, chips, tuple(offsets), first, last),
        in_specs=in_specs,
        out_specs=out_specs,
        out_shape=out_shape,
        scratch_shapes=[
            pltpu.VMEM((len(offsets), HALF, 2 * rows, 2 * DH), bf16),
            pltpu.VMEM((HALF, rows, 2 * DH), f32),
            pltpu.VMEM((4, HALF, rows, 2 * DH), bf16),
            pltpu.VMEM((rows, 2 * DH), bf16),
            pltpu.VMEM((HALF, rows, PER * rows), bf16),
            pltpu.VMEM((HALF, rows, PER * rows), bf16),
            pltpu.VMEM((HALF, 2, 1, PER * rows), f32),
            pltpu.VMEM((HALF, 2, DH, PER * rows) if last else (8, DH), f32),
            pltpu.SMEM((len(offsets),), jnp.int32),
            pltpu.SemaphoreType.DMA((2 * HALF,)),
            pltpu.SemaphoreType.DMA((len(offsets), HALF)),
            pltpu.SemaphoreType.DMA((4, HALF)),
            pltpu.SemaphoreType.DMA((2 * len(offsets), HALF)),
        ],
        compiler_params=pltpu.CompilerParams(vmem_limit_bytes=(24 << 20) + (len(offsets) << 19)),
        cost_estimate=pl.CostEstimate(flops=8 << 30, bytes_accessed=16 << 20, transcendentals=0),
    )(plan, *arrays)


def wide(x):
    return x.astype(jnp.float32)


def local(queries, keys, values, saved_out, grad_out, parents, assignment, lengths):
    rows = keys.shape[0]
    chips = lax.axis_size("leaf") // 2
    order = ring_order(chips)
    ahead = [(order[i], order[(i + 1) % chips]) for i in range(chips)]
    right = [(2 * a + c, 2 * b + c) for a, b in ahead for c in range(2)]
    left = [(b, a) for a, b in right]
    swap = [(2 * a + c, 2 * a + 1 - c) for a in range(chips) for c in range(2)]
    places = jnp.asarray([order.index(chip) for chip in range(chips)], jnp.int32)
    index = lax.axis_index("leaf").astype(jnp.int32)
    core = index % 2
    me = index.reshape(1)
    tables = (me, places, parents, assignment, lengths)

    def part(array, which, width):
        return lax.dynamic_slice(array, (0, which * width), (rows, width))

    def heads_of(which):
        pieces = [part(array, which * HALF + head, DH) for head in range(HALF) for array in (keys, values)]
        return jnp.concatenate(pieces, axis=1)

    kept = heads_of(core)
    got = lax.ppermute(heads_of(1 - core), "leaf", swap)
    own = []
    for head in range(HALF):
        cols = slice(head * 2 * DH, (head + 1) * 2 * DH)
        own.append(jnp.concatenate([kept[:, cols], got[:, cols]], axis=0))
    mine = (queries, grad_out, saved_out)
    late = lax.optimization_barrier((*mine, got))[:3]
    other = jnp.concatenate([part(array, 1 - core, HALF * WIDE) for array in late], axis=1)
    other = lax.ppermute(other, "leaf", swap)

    def shift(arrays, ring):
        return [lax.ppermute(array, "leaf", ring) for array in arrays]

    far = chips // 2
    prepared, stats = [None] * HALF, [None] * HALF
    blocks, halves = [], []
    streams = [(block, block) for block in own]
    blocks = [{0: block} for block in own]
    for step in range(1, far):
        for head in range(HALF):
            up, down = streams[head]
            up, down = lax.ppermute(up, "leaf", right), lax.ppermute(down, "leaf", left)
            blocks[head][chips - step], blocks[head][step] = up, down
            if step == 1:
                prepared[head] = prepare(head, tables, mine, other, own[head])
                stats[head] = prepared[head][6:]
            else:
                met = (step - 1, chips - step + 1)
                stats[head] = measure(met, prepared[head], stats[head], [blocks[head][at] for at in met])
            stats[head], streams[head] = lax.optimization_barrier((stats[head], (up, down)))
    for head in range(HALF):
        up, down = streams[head]
        halves.append([lax.ppermute(up[:rows], "leaf", right), lax.ppermute(down[rows:], "leaf", left)])
        met = (far - 1, far + 1)
        stats[head] = measure(met, prepared[head], stats[head], [blocks[head][at] for at in met])

    offsets = [far]
    for step in range(1, far - 1):
        offsets += [far + step, far - step]
    arrays = [halves[head] + [blocks[head][at] for at in offsets[1:]] for head in range(HALF)]
    *terms, carried = gradients(prepared, stats, offsets, arrays, None, False)
    lse = [[a] for a in terms[3 * HALF:]]
    by_offset = {at: [terms[head][slot] for head in range(HALF)] for slot, at in enumerate(offsets)}
    ups = [jnp.pad(wide(a), ((0, rows), (0, 0))) for a in shift(terms[HALF:2 * HALF], right)]
    downs = [jnp.pad(wide(a), ((rows, 0), (0, 0))) for a in shift(terms[2 * HALF:3 * HALF], left)]

    def add(sums, at):
        return [(a + wide(b)).astype(jnp.bfloat16) for a, b in zip(sums, by_offset[at])]

    later = {far - 1: [chips - 1, 1], max(far - 2, 1): [0]}
    ours = theirs = None
    for step in range(far - 1, 0, -1):
        ups, downs = add(ups, step), add(downs, chips - step)
        if step in later:
            last = 0 in later[step]
            (lse, carried), ups, downs = lax.optimization_barrier(((lse, carried), ups, downs))
            arrays = [[blocks[head][at] for at in later[step]] for head in range(HALF)]
            *terms, lead = gradients(prepared, lse, later[step], arrays, carried, last)
            for slot, at in enumerate(later[step]):
                by_offset[at] = [terms[head][slot] for head in range(HALF)]
            if last:
                ours, theirs = terms[HALF], lax.ppermute(lead, "leaf", swap)
            else:
                carried = lead
        ups = [wide(a) for a in shift(ups, right)]
        downs = [wide(a) for a in shift(downs, left)]
    kept, got = [], []
    for head in range(HALF):
        summed = (wide(by_offset[0][head]) + ups[head] + downs[head]).astype(jnp.bfloat16)
        kept.append(summed[:rows])
        got.append(lax.ppermute(summed[rows:], "leaf", swap))

    def whole(kept, got):
        low = [jnp.where(core == 0, a, b) for a, b in zip(kept, got)]
        high = [jnp.where(core == 0, b, a) for a, b in zip(kept, got)]
        return jnp.concatenate(low + high, axis=1)

    key_grad = whole([a[:, :DH] for a in kept], [a[:, :DH] for a in got])
    value_grad = whole([a[:, DH:] for a in kept], [a[:, DH:] for a in got])
    return (whole([ours], [theirs]), key_grad, value_grad)


def solution(mesh):
    tokens = P(("groups", "leaf"), None)
    tables = P("groups")
    return jax.shard_map(
        local,
        mesh=mesh,
        in_specs=(tokens,) * 5 + (tables,) * 3,
        out_specs=(tokens,) * 3,
        check_vma=False,
    )
```

profile of v0, /device:TPU:3, one launch (start us, length us, event | category | flops | bytes accessed | tf_op | source)
XLA Modules:
  0.0 128.2 jit_solution(12694039321173318223)
XLA Ops:
  8.4 4.6 %shard_map.116 = (s32[32]{0:T(128)S(1)}, bf16[2,128,1280]{2,1,0:T(8,128)(2,1)S(1)}, bf16[2,128,1280]{2,1,0:T(8,128)(2,1)S(1)}, bf16[2,1280,128]{2,1,0:T(8,128)(2...) custom-call(s32[1]{0:T(128)} %bitcast.me_ref, ...), custom_call_target="tpu_custom_call" | custom-call | bytes 12582912 | tf_op jit(solution)/shard_map/pallas_call | solution.py:157
  15.0 4.6 %shard_map.112 = (s32[32]{0:T(128)S(1)}, bf16[2,128,1280]{2,1,0:T(8,128)(2,1)S(1)}, bf16[2,128,1280]{2,1,0:T(8,128)(2,1)S(1)}, bf16[2,1280,128]{2,1,0:T(8,128)(2...) custom-call(s32[1]{0:T(128)} %bitcast.me_ref, ...), custom_call_target="tpu_custom_call" | custom-call | bytes 12582912 | tf_op jit(solution)/shard_map/pallas_call | solution.py:157
  21.2 1.8 %shard_map.117 = (f32[2,1,1280]{2,1,0:T(1,128)S(1)}, f32[2,1,1280]{2,1,0:T(1,128)S(1)}) custom-call(s32[32]{0:T(128)S(1)} %get-tuple-element.120.plan, bf16[2,128,1280]{2,1,0:T(8,128)(2,1)S(1)} %get-tuple-element.115.qt_ref.refs_7_.refs_6_, f32[2,1,1280]{2,1,0:T(1,128)S(1)} %get-tuple-element.123.top_in, f32[2,1,1280]{2,1,0:T(1,128)S(1)} %get-tuple-element.124.sum_in, ...), custom_call_target="tpu_custom_call" | custom-call | bytes 8388608 | tf_op jit(solution)/shard_map/pallas_call | solution.py:193
  26.3 1.8 %shard_map.113 = (f32[2,1,1280]{2,1,0:T(1,128)S(1)}, f32[2,1,1280]{2,1,0:T(1,128)S(1)}) custom-call(s32[32]{0:T(128)S(1)} %get-tuple-element.91.plan, bf16[2,128,1280]{2,1,0:T(8,128)(2,1)S(1)} %get-tuple-element.92.qt_ref.refs_0_, f32[2,1,1280]{2,1,0:T(1,128)S(1)} %get-tuple-element.99.top_in, f32[2,1,1280]{2,1,0:T(1,128)S(1)} %get-tuple-element.100.sum_in, ...), custom_call_target="tpu_custom_call" | custom-call | bytes 8388608 | tf_op jit(solution)/shard_map/pallas_call | solution.py:193
  31.2 1.8 %shard_map.118 = (f32[2,1,1280]{2,1,0:T(1,128)S(1)}, f32[2,1,1280]{2,1,0:T(1,128)S(1)}) custom-call(s32[32]{0:T(128)S(1)} %get-tuple-element.120.plan, bf16[2,128,1280]{2,1,0:T(8,128)(2,1)S(1)} %get-tuple-element.115.qt_ref.refs_7_.refs_6_, f32[2,1,1280]{2,1,0:T(1,128)S(1)} %get-tuple-element.129.top_in, f32[2,1,1280]{2,1,0:T(1,128)S(1)} %get-tuple-element.130.sum_in, ...), custom_call_target="tpu_custom_call" | custom-call | bytes 8388608 | tf_op jit(solution)/shard_map/pallas_call | solution.py:193
  33.0 1.8 %shard_map.114 = (f32[2,1,1280]{2,1,0:T(1,128)S(1)}, f32[2,1,1280]{2,1,0:T(1,128)S(1)}) custom-call(s32[32]{0:T(128)S(1)} %get-tuple-element.91.plan, bf16[2,128,1280]{2,1,0:T(8,128)(2,1)S(1)} %get-tuple-element.92.qt_ref.refs_0_, f32[2,1,1280]{2,1,0:T(1,128)S(1)} %get-tuple-element.105.top_in, f32[2,1,1280]{2,1,0:T(1,128)S(1)} %get-tuple-element.106.sum_in, ...), custom_call_target="tpu_custom_call" | custom-call | bytes 8388608 | tf_op jit(solution)/shard_map/pallas_call | solution.py:193
  36.9 3.0 %collective-permute-done.6.refs_1_.refs_16_ = bf16[512,256]{1,0:T(8,128)(2,1)S(1)} collective-permute-done((bf16[512,256]{1,0:T(8,128)(2,1)S(1)}, bf16[512,256]{1,0:T(8,128)(2,1)S(1)}, u32[]{:S(2)}, u32[]{:S(2)}) %collective-permute-start.6) | collective-permute-done | bytes 262176 | tf_op jit(solution)/shard_map/ppermute | solution.py:466
  42.7 2.3 %shard_map.119 = (f32[2,1,1280]{2,1,0:T(1,128)S(1)}, f32[2,1,1280]{2,1,0:T(1,128)S(1)}) custom-call(s32[32]{0:T(128)S(1)} %get-tuple-element.120.plan, bf16[2,128,1280]{2,1,0:T(8,128)(2,1)S(1)} %get-tuple-element.115.qt_ref.refs_7_.refs_6_, f32[2,1,1280]{2,1,0:T(1,128)S(1)} %get-tuple-element.135.top_in, f32[2,1,1280]{2,1,0:T(1,128)S(1)} %get-tuple-element.136.sum_in, ...), custom_call_target="tpu_custom_call" | custom-call | bytes 8388608 | tf_op jit(solution)/shard_map/pallas_call | solution.py:193
  45.1 2.3 %shard_map.115 = (f32[2,1,1280]{2,1,0:T(1,128)S(1)}, f32[2,1,1280]{2,1,0:T(1,128)S(1)}) custom-call(s32[32]{0:T(128)S(1)} %get-tuple-element.91.plan, bf16[2,128,1280]{2,1,0:T(8,128)(2,1)S(1)} %get-tuple-element.92.qt_ref.refs_0_, f32[2,1,1280]{2,1,0:T(1,128)S(1)} %get-tuple-element.111.top_in, f32[2,1,1280]{2,1,0:T(1,128)S(1)} %get-tuple-element.112.sum_in, ...), custom_call_target="tpu_custom_call" | custom-call | bytes 8388608 | tf_op jit(solution)/shard_map/pallas_call | solution.py:193
  47.5 15.8 %shard_map.120 = (bf16[5,512,256]{2,1,0:T(8,128)(2,1)S(1)}, bf16[5,512,256]{2,1,0:T(8,128)(2,1)S(1)}, bf16[256,256]{1,0:T(8,128)(2,1)S(1)}, bf16[256,256]{1,0:T(...) custom-call(s32[32]{0:T(128)S(1)} %get-tuple-element.91.plan, ...), custom_call_target="tpu_custom_call" | custom-call | flops 8589934592 | bytes 16777216 | tf_op jit(solution)/shard_map/pallas_call | solution.py:394
  63.4 1.5 %collective-permute-start.21 = (bf16[256,256]{1,0:T(8,128)(2,1)S(1)}, bf16[256,256]{1,0:T(8,128)(2,1)S(1)}, u32[]{:S(2)}, u32[]{:S(2)}) collective-permute-start(bf16[256,256]{1,0:T(8,128)(2,1)S(1)} %get-tuple-element.151), channel_id=1, source_target_pairs={{4,0},{5,1},{8,4},{9,5},{12,8},{13,9},{14,12},{15,13},{10,14},{11,... | collective-permute-start | bytes 393224 | tf_op jit(solution)/shard_map/ppermute | solution.py:456
  64.9 4.8 %collective-permute-start.20 = (bf16[256,256]{1,0:T(8,128)(2,1)S(1)}, bf16[256,256]{1,0:T(8,128)(2,1)S(1)}, u32[]{:S(2)}, u32[]{:S(2)}) collective-permute-start(bf16[256,256]{1,0:T(8,128)(2,1)S(1)} %get-tuple-element.150), channel_id=1, source_target_pairs={{4,0},{5,1},{8,4},{9,5},{12,8},{13,9},{14,12},{15,13},{10,14},{11,... | collective-permute-start | bytes 393224 | tf_op jit(solution)/shard_map/ppermute | solution.py:456
  69.8 3.5 %collective-permute-done.18 = bf16[256,256]{1,0:T(8,128)(2,1)S(1)} collective-permute-done((bf16[256,256]{1,0:T(8,128)(2,1)S(1)}, bf16[256,256]{1,0:T(8,128)(2,1)S(1)}, u32[]{:S(2)}, u32[]{:S(2)}) %collective-permute-start.18) | collective-permute-done | bytes 131104 | tf_op jit(solution)/shard_map/ppermute | solution.py:456
  73.5 4.7 %collective-permute-start.25 = (bf16[512,256]{1,0:T(8,128)(2,1)S(1)}, bf16[512,256]{1,0:T(8,128)(2,1)S(1)}, u32[]{:S(2)}, u32[]{:S(2)}) collective-permute-start(bf16[512,256]{1,0:T(8,128)(2,1)S(1)} %get-tuple-element.159), channel_id=1, source_target_pairs={{4,0},{5,1},{8,4},{9,5},{12,8},{13,9},{14,12},{15,13},{10,14},{11,... | collective-permute-start | bytes 786440 | tf_op jit(solution)/shard_map/ppermute | solution.py:456
  80.0 6.3 %shard_map.121 = (bf16[2,512,256]{2,1,0:T(8,128)(2,1)S(1)}, bf16[2,512,256]{2,1,0:T(8,128)(2,1)S(1)}, f32[2,2,128,1280]{3,2,1,0:T(8,128)S(1)}) custom-call(s32[32]{0:T(128)S(1)} %get-tuple-element.91.plan, bf16[2,128,1280]{2,1,0:T(8,128)(2,1)S(1)} %get-tuple-element.92.qt_ref.refs_0_, bf16[2,128,1280]{2,1,0:T(8,128)(2,1)S(1)} %get-tuple-element.93.refs_1_, ...), custom_call_target="tpu_custom_call" | custom-call | flops 8589934592 | bytes 16777216 | tf_op jit(solution)/shard_map/pallas_call | solution.py:394
  89.1 3.7 %collective-permute-start.32 = (bf16[512,256]{1,0:T(8,128)(2,1)S(1)}, bf16[512,256]{1,0:T(8,128)(2,1)S(1)}, u32[]{:S(2)}, u32[]{:S(2)}) collective-permute-start(bf16[512,256]{1,0:T(8,128)(2,1)S(1)} %get-tuple-element.170), channel_id=1, source_target_pairs={{0,4},{1,5},{4,8},{5,9},{8,12},{9,13},{12,14},{13,15},{14,10},{15,... | collective-permute-start | bytes 786440 | tf_op jit(solution)/shard_map/ppermute | solution.py:456
  92.8 7.7 %shard_map.122 = (bf16[1,512,256]{2,1,0:T(8,128)(2,1)S(1)}, bf16[1,512,256]{2,1,0:T(8,128)(2,1)S(1)}, bf16[256,1280]{1,0:T(8,128)(2,1)S(1)}, bf16[256,1280]{1,0:T(8,128)(2,1)S(1)}) custom-call(s32[32]{0:T(128)S(1)} %get-tuple-element.91.plan, bf16[2,128,1280]{2,1,0:T(8,128)(2,1)S(1)} %get-tuple-element.92.qt_ref.refs_0_, ...), custom_call_target="tpu_custom_call" | custom-call | flops 8589934592 | bytes 16777216 | tf_op jit(solution)/shard_map/pallas_call | solution.py:394
  100.5 7.0 %collective-permute-start.26 = (bf16[256,1280]{1,0:T(8,128)(2,1)S(1)}, bf16[256,1280]{1,0:T(8,128)(2,1)S(1)}, u32[]{:S(2)}, u32[]{:S(2)}) collective-permute-start(bf16[256,1280]{1,0:T(8,128)(2,1)S(1)} %get-tuple-element.164), channel_id=1, source_target_pairs={{0,1},{1,0},{2,3},{3,2},{4,5},{5,4},{6,7},{7,6},{8,9},{9,8},{10,11... | collective-permute-start | bytes 1966088 | tf_op jit(solution)/shard_map/ppermute | solution.py:506
  107.7 1.8 %collective-permute-start.28 = (bf16[512,256]{1,0:T(8,128)(2,1)S(1)}, bf16[512,256]{1,0:T(8,128)(2,1)S(1)}, u32[]{:S(2)}, u32[]{:S(2)}) collective-permute-start(bf16[512,256]{1,0:T(8,128)(2,1)S(1)} %get-tuple-element.183), channel_id=1, source_target_pairs={{0,4},{1,5},{4,8},{5,9},{8,12},{9,13},{12,14},{13,15},{14,10},{15,... | collective-permute-start | bytes 786440 | tf_op jit(solution)/shard_map/ppermute | solution.py:456
  110.4 1.7 %collective-permute-start.33 = (bf16[512,256]{1,0:T(8,128)(2,1)}, bf16[512,256]{1,0:T(8,128)(2,1)}, u32[]{:S(2)}, u32[]{:S(2)}) collective-permute-start(bf16[512,256]{1,0:T(8,128)(2,1)} %get-tuple-element.185), channel_id=1, source_target_pairs={{0,4},{1,5},{4,8},{5,9},{8,12},{9,13},{12,14},{13,15},{14,10},{15,... | collective-permute-start | bytes 786440 | tf_op jit(solution)/shard_map/ppermute | solution.py:456
  112.2 3.5 %collective-permute-done.28 = bf16[512,256]{1,0:T(8,128)(2,1)S(1)} collective-permute-done((bf16[512,256]{1,0:T(8,128)(2,1)S(1)}, bf16[512,256]{1,0:T(8,128)(2,1)S(1)}, u32[]{:S(2)}, u32[]{:S(2)}) %collective-permute-start.28) | collective-permute-done | bytes 262176 | tf_op jit(solution)/shard_map/ppermute | solution.py:456
  115.6 2.1 %collective-permute-done.30 = bf16[512,256]{1,0:T(8,128)(2,1)S(1)} collective-permute-done((bf16[512,256]{1,0:T(8,128)(2,1)S(1)}, bf16[512,256]{1,0:T(8,128)(2,1)S(1)}, u32[]{:S(2)}, u32[]{:S(2)}) %collective-permute-start.30) | collective-permute-done | bytes 262176 | tf_op jit(solution)/shard_map/ppermute | solution.py:456
  119.0 2.3 %collective-permute-done.33 = bf16[512,256]{1,0:T(8,128)(2,1)} collective-permute-done((bf16[512,256]{1,0:T(8,128)(2,1)}, bf16[512,256]{1,0:T(8,128)(2,1)}, u32[]{:S(2)}, u32[]{:S(2)}) %collective-permute-start.33) | collective-permute-done | bytes 262176 | tf_op jit(solution)/shard_map/ppermute | solution.py:456
  121.3 2.0 %collective-permute-done.35 = bf16[512,256]{1,0:T(8,128)(2,1)} collective-permute-done((bf16[512,256]{1,0:T(8,128)(2,1)}, bf16[512,256]{1,0:T(8,128)(2,1)}, u32[]{:S(2)}, u32[]{:S(2)}) %collective-permute-start.35) | collective-permute-done | bytes 262176 | tf_op jit(solution)/shard_map/ppermute | solution.py:456
  (104 shorter events, 34.5 us)
Async XLA Ops:
  6.3 13.3 %collective-permute-start.2 = (bf16[512,256]{1,0:T(8,128)(2,1)S(1)}, bf16[512,256]{1,0:T(8,128)(2,1)S(1)}, u32[]{:S(2)}, u32[]{:S(2)}) collective-permute-start(bf16[512,256]{1,0:T(8,128)(2,1)S(1)} %pad_maximum_fusion.3.block.refs_12_), channel_id=1, source_target_pairs={{0,4},{1,5},{4,8},{5,9},{8,12},{9,13},{12,14},{13,15},{14,10},{15,... | collective-permute-start | bytes 786440 | tf_op jit(solution)/shard_map/ppermute | solution.py:466
  7.7 12.0 %collective-permute-start.3 = (bf16[512,256]{1,0:T(8,128)(2,1)S(1)}, bf16[512,256]{1,0:T(8,128)(2,1)S(1)}, u32[]{:S(2)}, u32[]{:S(2)}) collective-permute-start(bf16[512,256]{1,0:T(8,128)(2,1)S(1)} %pad_maximum_fusion.3.block.refs_12_), channel_id=1, source_target_pairs={{4,0},{5,1},{8,4},{9,5},{12,8},{13,9},{14,12},{15,13},{10,14},{11,... | collective-permute-start | bytes 786440 | tf_op jit(solution)/shard_map/ppermute | solution.py:466
  13.6 10.3 %collective-permute-start.10 = (bf16[512,256]{1,0:T(8,128)(2,1)S(1)}, bf16[512,256]{1,0:T(8,128)(2,1)S(1)}, u32[]{:S(2)}, u32[]{:S(2)}) collective-permute-start(bf16[512,256]{1,0:T(8,128)(2,1)S(1)} %collective-permute-done.8.refs_1_.refs_14_), channel_id=1, source_target_pairs={{0,4},{1,5},{4,8},{5,9},{8,12},{9,13},{12,14},{13,15},{14,10},{15,... | collective-permute-start | bytes 786440 | tf_op jit(solution)/shard_map/ppermute | solution.py:466
  14.9 9.9 %collective-permute-start.11 = (bf16[512,256]{1,0:T(8,128)(2,1)S(1)}, bf16[512,256]{1,0:T(8,128)(2,1)S(1)}, u32[]{:S(2)}, u32[]{:S(2)}) collective-permute-start(bf16[512,256]{1,0:T(8,128)(2,1)S(1)} %collective-permute-done.9.refs_0_.refs_15_), channel_id=1, source_target_pairs={{4,0},{5,1},{8,4},{9,5},{12,8},{13,9},{14,12},{15,13},{10,14},{11,... | collective-permute-start | bytes 786440 | tf_op jit(solution)/shard_map/ppermute | solution.py:466
  19.7 9.0 %collective-permute-start.4 = (bf16[512,256]{1,0:T(8,128)(2,1)S(1)}, bf16[512,256]{1,0:T(8,128)(2,1)S(1)}, u32[]{:S(2)}, u32[]{:S(2)}) collective-permute-start(bf16[512,256]{1,0:T(8,128)(2,1)S(1)} %collective-permute-done.2.refs_1_.refs_12_), channel_id=1, source_target_pairs={{0,4},{1,5},{4,8},{5,9},{8,12},{9,13},{12,14},{13,15},{14,10},{15,... | collective-permute-start | bytes 786440 | tf_op jit(solution)/shard_map/ppermute | solution.py:466
  21.0 8.7 %collective-permute-start.5 = (bf16[512,256]{1,0:T(8,128)(2,1)S(1)}, bf16[512,256]{1,0:T(8,128)(2,1)S(1)}, u32[]{:S(2)}, u32[]{:S(2)}) collective-permute-start(bf16[512,256]{1,0:T(8,128)(2,1)S(1)} %collective-permute-done.3.refs_0_.refs_13_), channel_id=1, source_target_pairs={{4,0},{5,1},{8,4},{9,5},{12,8},{13,9},{14,12},{15,13},{10,14},{11,... | collective-permute-start | bytes 786440 | tf_op jit(solution)/shard_map/ppermute | solution.py:466
  24.8 10.0 %collective-permute-start.12 = (bf16[512,256]{1,0:T(8,128)(2,1)S(1)}, bf16[512,256]{1,0:T(8,128)(2,1)S(1)}, u32[]{:S(2)}, u32[]{:S(2)}) collective-permute-start(bf16[512,256]{1,0:T(8,128)(2,1)S(1)} %collective-permute-done.10.refs_1_.refs_24_), channel_id=1, source_target_pairs={{0,4},{1,5},{4,8},{5,9},{8,12},{9,13},{12,14},{13,15},{14,10},{15,... | collective-permute-start | bytes 786440 | tf_op jit(solution)/shard_map/ppermute | solution.py:466
  26.1 9.3 %collective-permute-start.13 = (bf16[512,256]{1,0:T(8,128)(2,1)S(1)}, bf16[512,256]{1,0:T(8,128)(2,1)S(1)}, u32[]{:S(2)}, u32[]{:S(2)}) collective-permute-start(bf16[512,256]{1,0:T(8,128)(2,1)S(1)} %collective-permute-done.11.refs_0_.refs_25_), channel_id=1, source_target_pairs={{4,0},{5,1},{8,4},{9,5},{12,8},{13,9},{14,12},{15,13},{10,14},{11,... | collective-permute-start | bytes 786440 | tf_op jit(solution)/shard_map/ppermute | solution.py:466
  29.7 10.2 %collective-permute-start.6 = (bf16[512,256]{1,0:T(8,128)(2,1)S(1)}, bf16[512,256]{1,0:T(8,128)(2,1)S(1)}, u32[]{:S(2)}, u32[]{:S(2)}) collective-permute-start(bf16[512,256]{1,0:T(8,128)(2,1)S(1)} %collective-permute-done.4.refs_1_.refs_18_), channel_id=1, source_target_pairs={{0,4},{1,5},{4,8},{5,9},{8,12},{9,13},{12,14},{13,15},{14,10},{15,... | collective-permute-start | bytes 786440 | tf_op jit(solution)/shard_map/ppermute | solution.py:466
  31.0 9.9 %collective-permute-start.7 = (bf16[512,256]{1,0:T(8,128)(2,1)S(1)}, bf16[512,256]{1,0:T(8,128)(2,1)S(1)}, u32[]{:S(2)}, u32[]{:S(2)}) collective-permute-start(bf16[512,256]{1,0:T(8,128)(2,1)S(1)} %collective-permute-done.5.refs_0_.refs_19_), channel_id=1, source_target_pairs={{4,0},{5,1},{8,4},{9,5},{12,8},{13,9},{14,12},{15,13},{10,14},{11,... | collective-permute-start | bytes 786440 | tf_op jit(solution)/shard_map/ppermute | solution.py:466
  35.4 12.1 %collective-permute-start.16 = (bf16[256,256]{1,0:T(8,128)(2,1)S(1)}, bf16[256,256]{1,0:T(8,128)(2,1)S(1)}, u32[]{:S(2)}, u32[]{:S(2)}) collective-permute-start(bf16[256,256]{1,0:T(8,128)(2,1)S(1)} %slice.98), channel_id=1, source_target_pairs={{0,4},{1,5},{4,8},{5,9},{8,12},{9,13},{12,14},{13,15},{14,10},{15,... | collective-permute-start | bytes 393224 | tf_op jit(solution)/shard_map/ppermute | solution.py:477
  36.7 10.7 %collective-permute-start.17 = (bf16[256,256]{1,0:T(8,128)(2,1)S(1)}, bf16[256,256]{1,0:T(8,128)(2,1)S(1)}, u32[]{:S(2)}, u32[]{:S(2)}) collective-permute-start(bf16[256,256]{1,0:T(8,128)(2,1)S(1)} %slice.99), channel_id=1, source_target_pairs={{4,0},{5,1},{8,4},{9,5},{12,8},{13,9},{14,12},{15,13},{10,14},{11,... | collective-permute-start | bytes 393224 | tf_op jit(solution)/shard_map/ppermute | solution.py:477
  64.9 8.5 %collective-permute-start.18 = (bf16[256,256]{1,0:T(8,128)(2,1)S(1)}, bf16[256,256]{1,0:T(8,128)(2,1)S(1)}, u32[]{:S(2)}, u32[]{:S(2)}) collective-permute-start(bf16[256,256]{1,0:T(8,128)(2,1)S(1)} %get-tuple-element.146), channel_id=1, source_target_pairs={{0,4},{1,5},{4,8},{5,9},{8,12},{9,13},{12,14},{13,15},{14,10},{15,... | collective-permute-start | bytes 393224 | tf_op jit(solution)/shard_map/ppermute | solution.py:456
  73.4 13.0 %collective-permute-start.23 = (bf16[512,256]{1,0:T(8,128)(2,1)S(1)}, bf16[512,256]{1,0:T(8,128)(2,1)S(1)}, u32[]{:S(2)}, u32[]{:S(2)}) collective-permute-start(bf16[512,256]{1,0:T(8,128)(2,1)S(1)} %get-tuple-element.157), channel_id=1, source_target_pairs={{0,4},{1,5},{4,8},{5,9},{8,12},{9,13},{12,14},{13,15},{14,10},{15,... | collective-permute-start | bytes 786440 | tf_op jit(solution)/shard_map/ppermute | solution.py:456
  73.5 12.9 %collective-permute-start.25 = (bf16[512,256]{1,0:T(8,128)(2,1)S(1)}, bf16[512,256]{1,0:T(8,128)(2,1)S(1)}, u32[]{:S(2)}, u32[]{:S(2)}) collective-permute-start(bf16[512,256]{1,0:T(8,128)(2,1)S(1)} %get-tuple-element.159), channel_id=1, source_target_pairs={{4,0},{5,1},{8,4},{9,5},{12,8},{13,9},{14,12},{15,13},{10,14},{11,... | collective-permute-start | bytes 786440 | tf_op jit(solution)/shard_map/ppermute | solution.py:456
  78.1 8.4 %collective-permute-start.22 = (bf16[512,256]{1,0:T(8,128)(2,1)S(1)}, bf16[512,256]{1,0:T(8,128)(2,1)S(1)}, u32[]{:S(2)}, u32[]{:S(2)}) collective-permute-start(bf16[512,256]{1,0:T(8,128)(2,1)S(1)} %get-tuple-element.156), channel_id=1, source_target_pairs={{0,4},{1,5},{4,8},{5,9},{8,12},{9,13},{12,14},{13,15},{14,10},{15,... | collective-permute-start | bytes 786440 | tf_op jit(solution)/shard_map/ppermute | solution.py:456
  87.6 19.9 %collective-permute-start.27 = (bf16[512,256]{1,0:T(8,128)(2,1)S(1)}, bf16[512,256]{1,0:T(8,128)(2,1)S(1)}, u32[]{:S(2)}, u32[]{:S(2)}) collective-permute-start(bf16[512,256]{1,0:T(8,128)(2,1)S(1)} %get-tuple-element.166), channel_id=1, source_target_pairs={{0,4},{1,5},{4,8},{5,9},{8,12},{9,13},{12,14},{13,15},{14,10},{15,... | collective-permute-start | bytes 786440 | tf_op jit(solution)/shard_map/ppermute | solution.py:456
  88.8 18.7 %collective-permute-start.29 = (bf16[512,256]{1,0:T(8,128)(2,1)S(1)}, bf16[512,256]{1,0:T(8,128)(2,1)S(1)}, u32[]{:S(2)}, u32[]{:S(2)}) collective-permute-start(bf16[512,256]{1,0:T(8,128)(2,1)S(1)} %get-tuple-element.168), channel_id=1, source_target_pairs={{4,0},{5,1},{8,4},{9,5},{12,8},{13,9},{14,12},{15,13},{10,14},{11,... | collective-permute-start | bytes 786440 | tf_op jit(solution)/shard_map/ppermute | solution.py:456
  89.1 20.4 %collective-permute-start.32 = (bf16[512,256]{1,0:T(8,128)(2,1)S(1)}, bf16[512,256]{1,0:T(8,128)(2,1)S(1)}, u32[]{:S(2)}, u32[]{:S(2)}) collective-permute-start(bf16[512,256]{1,0:T(8,128)(2,1)S(1)} %get-tuple-element.170), channel_id=1, source_target_pairs={{0,4},{1,5},{4,8},{5,9},{8,12},{9,13},{12,14},{13,15},{14,10},{15,... | collective-permute-start | bytes 786440 | tf_op jit(solution)/shard_map/ppermute | solution.py:456
  92.8 16.7 %collective-permute-start.34 = (bf16[512,256]{1,0:T(8,128)(2,1)S(1)}, bf16[512,256]{1,0:T(8,128)(2,1)S(1)}, u32[]{:S(2)}, u32[]{:S(2)}) collective-permute-start(bf16[512,256]{1,0:T(8,128)(2,1)S(1)} %get-tuple-element.172), channel_id=1, source_target_pairs={{4,0},{5,1},{8,4},{9,5},{12,8},{13,9},{14,12},{15,13},{10,14},{11,... | collective-permute-start | bytes 786440 | tf_op jit(solution)/shard_map/ppermute | solution.py:456
  100.5 24.9 %collective-permute-start.26 = (bf16[256,1280]{1,0:T(8,128)(2,1)S(1)}, bf16[256,1280]{1,0:T(8,128)(2,1)S(1)}, u32[]{:S(2)}, u32[]{:S(2)}) collective-permute-start(bf16[256,1280]{1,0:T(8,128)(2,1)S(1)} %get-tuple-element.164), channel_id=1, source_target_pairs={{0,1},{1,0},{2,3},{3,2},{4,5},{5,4},{6,7},{7,6},{8,9},{9,8},{10,11... | collective-permute-start | bytes 1966088 | tf_op jit(solution)/shard_map/ppermute | solution.py:506
  110.4 10.9 %collective-permute-start.33 = (bf16[512,256]{1,0:T(8,128)(2,1)}, bf16[512,256]{1,0:T(8,128)(2,1)}, u32[]{:S(2)}, u32[]{:S(2)}) collective-permute-start(bf16[512,256]{1,0:T(8,128)(2,1)} %get-tuple-element.185), channel_id=1, source_target_pairs={{0,4},{1,5},{4,8},{5,9},{8,12},{9,13},{12,14},{13,15},{14,10},{15,... | collective-permute-start | bytes 786440 | tf_op jit(solution)/shard_map/ppermute | solution.py:456
  112.1 11.2 %collective-permute-start.35 = (bf16[512,256]{1,0:T(8,128)(2,1)}, bf16[512,256]{1,0:T(8,128)(2,1)}, u32[]{:S(2)}, u32[]{:S(2)}) collective-permute-start(bf16[512,256]{1,0:T(8,128)(2,1)} %get-tuple-element.186), channel_id=1, source_target_pairs={{4,0},{5,1},{8,4},{9,5},{12,8},{13,9},{14,12},{15,13},{10,14},{11,... | collective-permute-start | bytes 786440 | tf_op jit(solution)/shard_map/ppermute | solution.py:456
  117.9 8.8 %collective-permute-start.31 = (bf16[256,256]{1,0:T(8,128)(2,1)S(1)}, bf16[256,256]{1,0:T(8,128)(2,1)S(1)}, u32[]{:S(2)}, u32[]{:S(2)}) collective-permute-start(bf16[256,256]{1,0:T(8,128)(2,1)S(1)} %slice.125), channel_id=1, source_target_pairs={{0,1},{1,0},{2,3},{3,2},{4,5},{5,4},{6,7},{7,6},{8,9},{9,8},{10,11... | collective-permute-start | bytes 393224 | tf_op jit(solution)/shard_map/ppermute | solution.py:515
  (20 other events, 105.4 us)
where the time goes:
time: 130 us; the launch traced here: 128 us
  Pallas kernels  51 us (39%)
  starting transfers between devices  44.3 us (34%)
  waiting for transfers between devices  24.5 us (19%)
  other arithmetic  5.71 us (4%)
  local copies, waits for them, and re-layouts  1.56 us (1%)
    pallas_call x3, Pallas kernels, gradients(): pl.pallas_call(functools.partial(grads_kernel, chips, tuple(offsets), fir...  29.9 us
    ppermute x16, starting transfers between devices, shift(): return [lax.ppermute(array, 'leaf', ring) for array in arrays]  21.8 us
    ppermute x16, waiting for transfers between devices, shift(): return [lax.ppermute(array, 'leaf', ring) for array in arrays]  14.3 us
    pallas_call x6, Pallas kernels, measure(): pl.pallas_call(functools.partial(measure_kernel, offsets), in_specs=[SMEM...  11.9 us
    pallas_call x2, Pallas kernels, prepare(): pl.pallas_call(functools.partial(prepare_kernel, head), in_specs=[SMEM] *...  9.23 us
    ppermute x6, starting transfers between devices, local(): lax.ppermute(up, 'leaf', right)  7.94 us
    ppermute x1, starting transfers between devices, local(): ours, theirs = (terms[HALF], lax.ppermute(lead, 'leaf', swap))  7.02 us
    ppermute x6, waiting for transfers between devices, local(): lax.ppermute(up, 'leaf', right)  4.45 us
  transfers between devices with their start and end apart: 37, of which 16 were waited for; matrix products, arithmetic and copies ran while one was open for 3% of the time, Pallas kernels for 27%

commit v1 on v0

--- a/solution.py
+++ b/solution.py
@@ -479,7 +479,7 @@
         stats[head] = measure(met, prepared[head], stats[head], [blocks[head][at] for at in met])
 
     offsets = [far]
-    for step in range(1, far - 1):
+    for step in range(1, far - 2):
         offsets += [far + step, far - step]
     arrays = [halves[head] + [blocks[head][at] for at in offsets[1:]] for head in range(HALF)]
     *terms, carried = gradients(prepared, stats, offsets, arrays, None, False)
@@ -491,13 +491,14 @@
     def add(sums, at):
         return [(a + wide(b)).astype(jnp.bfloat16) for a, b in zip(sums, by_offset[at])]
 
-    later = {far - 1: [chips - 1, 1], max(far - 2, 1): [0]}
+    later = {3: [chips - 2, 2], 2: [chips - 1, 1], 1: [0]}
     ours = theirs = None
     for step in range(far - 1, 0, -1):
         ups, downs = add(ups, step), add(downs, chips - step)
         if step in later:
             last = 0 in later[step]
-            (lse, carried), ups, downs = lax.optimization_barrier(((lse, carried), ups, downs))
+            (lse, carried), held = lax.optimization_barrier(((lse, carried), (ups[1:], downs[1:])))
+            ups, downs = ups[:1] + held[0], downs[:1] + held[1]
             arrays = [[blocks[head][at] for at in later[step]] for head in range(HALF)]
             *terms, lead = gradients(prepared, lse, later[step], arrays, carried, last)
             for slot, at in enumerate(later[step]):

time: 130 us -> 133 us (1.023)
  the two profiles are of different devices: /device:TPU:3 before, /device:TPU:15 now
where the time goes in v1:
time: 133 us
  starting transfers between devices  51.5 us (39%)
  Pallas kernels  45.8 us (34%)
  waiting for transfers between devices  15.9 us (12%)
  local copies, waits for them, and re-layouts  13.1 us (10%)
  other arithmetic  4.82 us (4%)
  between operations  1.5 us (1%)
    pallas_call x4, Pallas kernels, gradients(): pl.pallas_call(functools.partial(grads_kernel, chips, tuple(offsets), fir...  31 us
    ppermute x16, starting transfers between devices, shift(): return [lax.ppermute(array, 'leaf', ring) for array in arrays]  27.8 us
    ppermute x6, waiting for transfers between devices, local(): lax.ppermute(up, 'leaf', right)  11 us
    unnamed x106, local copies, waits for them, and re-layouts  10.9 us
    pallas_call x2, Pallas kernels, prepare(): pl.pallas_call(functools.partial(prepare_kernel, head), in_specs=[SMEM] *...  9.22 us
    ppermute x1, starting transfers between devices, local(): ours, theirs = (terms[HALF], lax.ppermute(lead, 'leaf', swap))  8.89 us
    ppermute x6, starting transfers between devices, local(): lax.ppermute(down, 'leaf', left)  8.09 us
    pallas_call x6, Pallas kernels, measure(): pl.pallas_call(functools.partial(measure_kernel, offsets), in_specs=[SMEM...  5.61 us
  transfers between devices with their start and end apart: 37, of which 10 were waited for; matrix products, arithmetic and copies ran while one was open for 3% of the time, Pallas kernels for 22%

profile of v1, /device:TPU:15, one launch (start us, length us, event | category | flops | bytes accessed | tf_op | source)
XLA Modules:
  0.0 132.6 jit_solution(17183310065940196949)
XLA Ops:
  0.7 1.9 %constant_dynamic-slice_fusion = (bf16[256,128]{1,0:T(8,128)(2,1)}, bf16[256,128]{1,0:T(8,128)(2,1)S(1)}, bf16[256,128]{1,0:T(8,128)(2,1)S(1)}, bf16[256,128]{1,...) fusion(bf16[256,512]{1,0:T(8,128)(2,1)} %param.11, ...), kind=kLoop, calls=%fused_computation.47 | loop fusion | bytes 1048592 | tf_op jit(solution)/shard_map/dynamic_slice | solution.py:438
  9.0 4.6 %shard_map.116 = (s32[32]{0:T(128)S(1)}, bf16[2,128,1280]{2,1,0:T(8,128)(2,1)S(1)}, bf16[2,128,1280]{2,1,0:T(8,128)(2,1)S(1)}, bf16[2,1280,128]{2,1,0:T(8,128)(2...) custom-call(s32[1]{0:T(128)} %bitcast.me_ref, ...), custom_call_target="tpu_custom_call" | custom-call | bytes 12582912 | tf_op jit(solution)/shard_map/pallas_call | solution.py:157
  15.3 4.6 %shard_map.112 = (s32[32]{0:T(128)S(1)}, bf16[2,128,1280]{2,1,0:T(8,128)(2,1)S(1)}, bf16[2,128,1280]{2,1,0:T(8,128)(2,1)S(1)}, bf16[2,1280,128]{2,1,0:T(8,128)(2...) custom-call(s32[1]{0:T(128)} %bitcast.me_ref, ...), custom_call_target="tpu_custom_call" | custom-call | bytes 12582912 | tf_op jit(solution)/shard_map/pallas_call | solution.py:157
  22.8 1.7 %collective-permute-done.10.refs_1_.refs_14_ = bf16[512,256]{1,0:T(8,128)(2,1)S(1)} collective-permute-done((bf16[512,256]{1,0:T(8,128)(2,1)S(1)}, bf16[512,256]{1,0:T(8,128)(2,1)S(1)}, u32[]{:S(2)}, u32[]{:S(2)}) %collective-permute-start.10) | collective-permute-done | bytes 262176 | tf_op jit(solution)/shard_map/ppermute | solution.py:466
  27.3 2.8 %collective-permute-done.4.refs_1_.refs_12_ = bf16[512,256]{1,0:T(8,128)(2,1)S(1)} collective-permute-done((bf16[512,256]{1,0:T(8,128)(2,1)S(1)}, bf16[512,256]{1,0:T(8,128)(2,1)S(1)}, u32[]{:S(2)}, u32[]{:S(2)}) %collective-permute-start.4) | collective-permute-done | bytes 262176 | tf_op jit(solution)/shard_map/ppermute | solution.py:466
  33.2 2.5 %collective-permute-done.12.refs_1_.refs_20_ = bf16[512,256]{1,0:T(8,128)(2,1)S(1)} collective-permute-done((bf16[512,256]{1,0:T(8,128)(2,1)S(1)}, bf16[512,256]{1,0:T(8,128)(2,1)S(1)}, u32[]{:S(2)}, u32[]{:S(2)}) %collective-permute-start.12) | collective-permute-done | bytes 262176 | tf_op jit(solution)/shard_map/ppermute | solution.py:466
  37.3 4.0 %collective-permute-done.6.refs_1_.refs_16_ = bf16[512,256]{1,0:T(8,128)(2,1)S(1)} collective-permute-done((bf16[512,256]{1,0:T(8,128)(2,1)S(1)}, bf16[512,256]{1,0:T(8,128)(2,1)S(1)}, u32[]{:S(2)}, u32[]{:S(2)}) %collective-permute-start.6) | collective-permute-done | bytes 262176 | tf_op jit(solution)/shard_map/ppermute | solution.py:466
  41.6 2.1 %collective-permute-start.15 = (bf16[256,256]{1,0:T(8,128)(2,1)S(1)}, bf16[256,256]{1,0:T(8,128)(2,1)S(1)}, u32[]{:S(2)}, u32[]{:S(2)}) collective-permute-start(bf16[256,256]{1,0:T(8,128)(2,1)S(1)} %slice.97), channel_id=1, source_target_pairs={{4,0},{5,1},{8,4},{9,5},{12,8},{13,9},{14,12},{15,13},{10,14},{11,... | collective-permute-start | bytes 393224 | tf_op jit(solution)/shard_map/ppermute | solution.py:477
  46.4 16.0 %shard_map.120 = (bf16[3,512,256]{2,1,0:T(8,128)(2,1)S(1)}, bf16[3,512,256]{2,1,0:T(8,128)(2,1)S(1)}, bf16[256,256]{1,0:T(8,128)(2,1)}, bf16[256,256]{1,0:T(8,12...) custom-call(s32[32]{0:T(128)S(1)} %get-tuple-element.95.plan, ...), custom_call_target="tpu_custom_call" | custom-call | flops 8589934592 | bytes 16777216 | tf_op jit(solution)/shard_map/pallas_call | solution.py:394
  63.1 1.5 %copy-done.43 = f32[2,2,128,1280]{3,2,1,0:T(8,128)} copy-done((f32[2,2,128,1280]{3,2,1,0:T(8,128)}, f32[2,2,128,1280]{3,2,1,0:T(8,128)S(1)}, u32[]{:S(2)}) %copy-start.43) | copy-done | bytes 2621464
  65.8 1.5 %collective-permute-start.29 = (bf16[256,256]{1,0:T(8,128)(2,1)}, bf16[256,256]{1,0:T(8,128)(2,1)}, u32[]{:S(2)}, u32[]{:S(2)}) collective-permute-start(bf16[256,256]{1,0:T(8,128)(2,1)} %get-tuple-element.177), channel_id=1, source_target_pairs={{4,0},{5,1},{8,4},{9,5},{12,8},{13,9},{14,12},{15,13},{10,14},{11,... | collective-permute-start | bytes 393224 | tf_op jit(solution)/shard_map/ppermute | solution.py:456
  67.3 1.5 %collective-permute-start.19 = (bf16[256,256]{1,0:T(8,128)(2,1)S(1)}, bf16[256,256]{1,0:T(8,128)(2,1)S(1)}, u32[]{:S(2)}, u32[]{:S(2)}) collective-permute-start(bf16[256,256]{1,0:T(8,128)(2,1)S(1)} %get-tuple-element.152), channel_id=1, source_target_pairs={{4,0},{5,1},{8,4},{9,5},{12,8},{13,9},{14,12},{15,13},{10,14},{11,... | collective-permute-start | bytes 393224 | tf_op jit(solution)/shard_map/ppermute | solution.py:456
  71.0 1.5 %collective-permute-start.30 = (bf16[512,256]{1,0:T(8,128)(2,1)S(1)}, bf16[512,256]{1,0:T(8,128)(2,1)S(1)}, u32[]{:S(2)}, u32[]{:S(2)}) collective-permute-start(bf16[512,256]{1,0:T(8,128)(2,1)S(1)} %get-tuple-element.184), channel_id=1, source_target_pairs={{4,0},{5,1},{8,4},{9,5},{12,8},{13,9},{14,12},{15,13},{10,14},{11,... | collective-permute-start | bytes 786440 | tf_op jit(solution)/shard_map/ppermute | solution.py:456
  72.7 1.5 %collective-permute-start.21 = (bf16[512,256]{1,0:T(8,128)(2,1)S(1)}, bf16[512,256]{1,0:T(8,128)(2,1)S(1)}, u32[]{:S(2)}, u32[]{:S(2)}) collective-permute-start(bf16[512,256]{1,0:T(8,128)(2,1)S(1)} %get-tuple-element.159), channel_id=1, source_target_pairs={{4,0},{5,1},{8,4},{9,5},{12,8},{13,9},{14,12},{15,13},{10,14},{11,... | collective-permute-start | bytes 786440 | tf_op jit(solution)/shard_map/ppermute | solution.py:456
  79.6 1.7 %copy-done.44 = f32[2,2,128,1280]{3,2,1,0:T(8,128)S(1)} copy-done((f32[2,2,128,1280]{3,2,1,0:T(8,128)S(1)}, f32[2,2,128,1280]{3,2,1,0:T(8,128)}, u32[]{:S(2)}) %copy-start.44) | copy-done | bytes 2621464
  81.4 2.7 %shard_map.121 = (bf16[2,512,256]{2,1,0:T(8,128)(2,1)S(1)}, bf16[2,512,256]{2,1,0:T(8,128)(2,1)S(1)}, f32[2,2,128,1280]{3,2,1,0:T(8,128)S(1)}) custom-call(s32[32]{0:T(128)S(1)} %get-tuple-element.95.plan, bf16[2,128,1280]{2,1,0:T(8,128)(2,1)S(1)} %copy-done.4, bf16[2,128,1280]{2,1,0:T(8,128)(2,1)S(1)} %copy-done.34, bf16[2,1280,128]{2,1,0:T(8,128)(2,1)S(1)} %copy-done.37, ...), custom_call_target="tpu_custom_call" | custom-call | flops 8589934592 | bytes 16777216 | tf_op jit(solution)/shard_map/pallas_call | solution.py:394
  84.3 2.0 %collective-permute-start.27 = (bf16[512,256]{1,0:T(8,128)(2,1)S(1)}, bf16[512,256]{1,0:T(8,128)(2,1)S(1)}, u32[]{:S(2)}, u32[]{:S(2)}) collective-permute-start(bf16[512,256]{1,0:T(8,128)(2,1)S(1)} %get-tuple-element.189), channel_id=1, source_target_pairs={{0,4},{1,5},{4,8},{5,9},{8,12},{9,13},{12,14},{13,15},{14,10},{15,... | collective-permute-start | bytes 786440 | tf_op jit(solution)/shard_map/ppermute | solution.py:456
  86.5 9.2 %collective-permute-start.22 = (bf16[512,256]{1,0:T(8,128)(2,1)S(1)}, bf16[512,256]{1,0:T(8,128)(2,1)S(1)}, u32[]{:S(2)}, u32[]{:S(2)}) collective-permute-start(bf16[512,256]{1,0:T(8,128)(2,1)S(1)} %get-tuple-element.164), channel_id=1, source_target_pairs={{0,4},{1,5},{4,8},{5,9},{8,12},{9,13},{12,14},{13,15},{14,10},{15,... | collective-permute-start | bytes 786440 | tf_op jit(solution)/shard_map/ppermute | solution.py:456
  95.6 3.8 %collective-permute-start.23 = (bf16[512,256]{1,0:T(8,128)(2,1)S(1)}, bf16[512,256]{1,0:T(8,128)(2,1)S(1)}, u32[]{:S(2)}, u32[]{:S(2)}) collective-permute-start(bf16[512,256]{1,0:T(8,128)(2,1)S(1)} %get-tuple-element.166), channel_id=1, source_target_pairs={{4,0},{5,1},{8,4},{9,5},{12,8},{13,9},{14,12},{15,13},{10,14},{11,... | collective-permute-start | bytes 786440 | tf_op jit(solution)/shard_map/ppermute | solution.py:456
  99.5 4.6 %shard_map.122 = (bf16[2,512,256]{2,1,0:T(8,128)(2,1)S(1)}, bf16[2,512,256]{2,1,0:T(8,128)(2,1)S(1)}, f32[2,2,128,1280]{3,2,1,0:T(8,128)S(1)}) custom-call(s32[32]{0:T(128)S(1)} %get-tuple-element.95.plan, bf16[2,128,1280]{2,1,0:T(8,128)(2,1)S(1)} %copy-done.4, bf16[2,128,1280]{2,1,0:T(8,128)(2,1)S(1)} %copy-done.35, bf16[2,1280,128]{2,1,0:T(8,128)(2,1)S(1)} %copy-done.37, ...), custom_call_target="tpu_custom_call" | custom-call | flops 8589934592 | bytes 16777216 | tf_op jit(solution)/shard_map/pallas_call | solution.py:394
  104.3 5.1 %collective-permute-start.32 = (bf16[512,256]{1,0:T(8,128)(2,1)S(1)}, bf16[512,256]{1,0:T(8,128)(2,1)S(1)}, u32[]{:S(2)}, u32[]{:S(2)}) collective-permute-start(bf16[512,256]{1,0:T(8,128)(2,1)S(1)} %get-tuple-element.188), channel_id=1, source_target_pairs={{4,0},{5,1},{8,4},{9,5},{12,8},{13,9},{14,12},{15,13},{10,14},{11,... | collective-permute-start | bytes 786440 | tf_op jit(solution)/shard_map/ppermute | solution.py:456
  109.7 1.5 %collective-permute-start.35 = (bf16[512,256]{1,0:T(8,128)(2,1)S(1)}, bf16[512,256]{1,0:T(8,128)(2,1)S(1)}, u32[]{:S(2)}, u32[]{:S(2)}) collective-permute-start(bf16[512,256]{1,0:T(8,128)(2,1)S(1)} %get-tuple-element.180), channel_id=1, source_target_pairs={{4,0},{5,1},{8,4},{9,5},{12,8},{13,9},{14,12},{15,13},{10,14},{11,... | collective-permute-start | bytes 786440 | tf_op jit(solution)/shard_map/ppermute | solution.py:456
  111.1 7.7 %shard_map.123 = (bf16[1,512,256]{2,1,0:T(8,128)(2,1)S(1)}, bf16[1,512,256]{2,1,0:T(8,128)(2,1)S(1)}, bf16[256,1280]{1,0:T(8,128)(2,1)S(1)}, bf16[256,1280]{1,0:T(8,128)(2,1)S(1)}) custom-call(s32[32]{0:T(128)S(1)} %get-tuple-element.95.plan, bf16[2,128,1280]{2,1,0:T(8,128)(2,1)S(1)} %copy-done.4, bf16[2,128,1280]{2,1,0:T(8,128)(2,1)S(1)} %copy-done.35, ...), custom_call_target="tpu_custom_call" | custom-call | flops 8589934592 | bytes 16777216 | tf_op jit(solution)/shard_map/pallas_call | solution.py:394
  118.8 8.9 %collective-permute-start.24 = (bf16[256,1280]{1,0:T(8,128)(2,1)S(1)}, bf16[256,1280]{1,0:T(8,128)(2,1)S(1)}, u32[]{:S(2)}, u32[]{:S(2)}) collective-permute-start(bf16[256,1280]{1,0:T(8,128)(2,1)S(1)} %get-tuple-element.171), channel_id=1, source_target_pairs={{0,1},{1,0},{2,3},{3,2},{4,5},{5,4},{6,7},{7,6},{8,9},{9,8},{10,11... | collective-permute-start | bytes 1966088 | tf_op jit(solution)/shard_map/ppermute | solution.py:507
  (197 shorter events, 36.2 us)
Async XLA Ops:
  7.2 12.7 %collective-permute-start.2 = (bf16[512,256]{1,0:T(8,128)(2,1)S(1)}, bf16[512,256]{1,0:T(8,128)(2,1)S(1)}, u32[]{:S(2)}, u32[]{:S(2)}) collective-permute-start(bf16[512,256]{1,0:T(8,128)(2,1)S(1)} %pad_maximum_fusion.3.block.refs_12_), channel_id=1, source_target_pairs={{0,4},{1,5},{4,8},{5,9},{8,12},{9,13},{12,14},{13,15},{14,10},{15,... | collective-permute-start | bytes 786440 | tf_op jit(solution)/shard_map/ppermute | solution.py:466
  7.4 12.5 %collective-permute-start.3 = (bf16[512,256]{1,0:T(8,128)(2,1)S(1)}, bf16[512,256]{1,0:T(8,128)(2,1)S(1)}, u32[]{:S(2)}, u32[]{:S(2)}) collective-permute-start(bf16[512,256]{1,0:T(8,128)(2,1)S(1)} %pad_maximum_fusion.3.block.refs_12_), channel_id=1, source_target_pairs={{4,0},{5,1},{8,4},{9,5},{12,8},{13,9},{14,12},{15,13},{10,14},{11,... | collective-permute-start | bytes 786440 | tf_op jit(solution)/shard_map/ppermute | solution.py:466
  13.7 10.7 %collective-permute-start.10 = (bf16[512,256]{1,0:T(8,128)(2,1)S(1)}, bf16[512,256]{1,0:T(8,128)(2,1)S(1)}, u32[]{:S(2)}, u32[]{:S(2)}) collective-permute-start(bf16[512,256]{1,0:T(8,128)(2,1)S(1)} %collective-permute-done.8.refs_1_.refs_14_), channel_id=1, source_target_pairs={{0,4},{1,5},{4,8},{5,9},{8,12},{9,13},{12,14},{13,15},{14,10},{15,... | collective-permute-start | bytes 786440 | tf_op jit(solution)/shard_map/ppermute | solution.py:466
  13.8 10.7 %collective-permute-start.11 = (bf16[512,256]{1,0:T(8,128)(2,1)S(1)}, bf16[512,256]{1,0:T(8,128)(2,1)S(1)}, u32[]{:S(2)}, u32[]{:S(2)}) collective-permute-start(bf16[512,256]{1,0:T(8,128)(2,1)S(1)} %collective-permute-done.9.refs_0_.refs_15_), channel_id=1, source_target_pairs={{4,0},{5,1},{8,4},{9,5},{12,8},{13,9},{14,12},{15,13},{10,14},{11,... | collective-permute-start | bytes 786440 | tf_op jit(solution)/shard_map/ppermute | solution.py:466
  20.0 10.1 %collective-permute-start.4 = (bf16[512,256]{1,0:T(8,128)(2,1)S(1)}, bf16[512,256]{1,0:T(8,128)(2,1)S(1)}, u32[]{:S(2)}, u32[]{:S(2)}) collective-permute-start(bf16[512,256]{1,0:T(8,128)(2,1)S(1)} %collective-permute-done.2.refs_1_.refs_12_), channel_id=1, source_target_pairs={{0,4},{1,5},{4,8},{5,9},{8,12},{9,13},{12,14},{13,15},{14,10},{15,... | collective-permute-start | bytes 786440 | tf_op jit(solution)/shard_map/ppermute | solution.py:466
  20.0 10.1 %collective-permute-start.5 = (bf16[512,256]{1,0:T(8,128)(2,1)S(1)}, bf16[512,256]{1,0:T(8,128)(2,1)S(1)}, u32[]{:S(2)}, u32[]{:S(2)}) collective-permute-start(bf16[512,256]{1,0:T(8,128)(2,1)S(1)} %collective-permute-done.3.refs_0_.refs_13_), channel_id=1, source_target_pairs={{4,0},{5,1},{8,4},{9,5},{12,8},{13,9},{14,12},{15,13},{10,14},{11,... | collective-permute-start | bytes 786440 | tf_op jit(solution)/shard_map/ppermute | solution.py:466
  24.5 11.2 %collective-permute-start.12 = (bf16[512,256]{1,0:T(8,128)(2,1)S(1)}, bf16[512,256]{1,0:T(8,128)(2,1)S(1)}, u32[]{:S(2)}, u32[]{:S(2)}) collective-permute-start(bf16[512,256]{1,0:T(8,128)(2,1)S(1)} %collective-permute-done.10.refs_1_.refs_14_), channel_id=1, source_target_pairs={{0,4},{1,5},{4,8},{5,9},{8,12},{9,13},{12,14},{13,15},{14,10},{15,... | collective-permute-start | bytes 786440 | tf_op jit(solution)/shard_map/ppermute | solution.py:466
  24.7 11.0 %collective-permute-start.13 = (bf16[512,256]{1,0:T(8,128)(2,1)S(1)}, bf16[512,256]{1,0:T(8,128)(2,1)S(1)}, u32[]{:S(2)}, u32[]{:S(2)}) collective-permute-start(bf16[512,256]{1,0:T(8,128)(2,1)S(1)} %collective-permute-done.11.refs_0_.refs_15_), channel_id=1, source_target_pairs={{4,0},{5,1},{8,4},{9,5},{12,8},{13,9},{14,12},{15,13},{10,14},{11,... | collective-permute-start | bytes 786440 | tf_op jit(solution)/shard_map/ppermute | solution.py:466
  30.1 11.2 %collective-permute-start.6 = (bf16[512,256]{1,0:T(8,128)(2,1)S(1)}, bf16[512,256]{1,0:T(8,128)(2,1)S(1)}, u32[]{:S(2)}, u32[]{:S(2)}) collective-permute-start(bf16[512,256]{1,0:T(8,128)(2,1)S(1)} %collective-permute-done.4.refs_1_.refs_12_), channel_id=1, source_target_pairs={{0,4},{1,5},{4,8},{5,9},{8,12},{9,13},{12,14},{13,15},{14,10},{15,... | collective-permute-start | bytes 786440 | tf_op jit(solution)/shard_map/ppermute | solution.py:466
  30.3 11.0 %collective-permute-start.7 = (bf16[512,256]{1,0:T(8,128)(2,1)S(1)}, bf16[512,256]{1,0:T(8,128)(2,1)S(1)}, u32[]{:S(2)}, u32[]{:S(2)}) collective-permute-start(bf16[512,256]{1,0:T(8,128)(2,1)S(1)} %collective-permute-done.5.refs_0_.refs_13_), channel_id=1, source_target_pairs={{4,0},{5,1},{8,4},{9,5},{12,8},{13,9},{14,12},{15,13},{10,14},{11,... | collective-permute-start | bytes 786440 | tf_op jit(solution)/shard_map/ppermute | solution.py:466
  35.7 9.5 %collective-permute-start.16 = (bf16[256,256]{1,0:T(8,128)(2,1)S(1)}, bf16[256,256]{1,0:T(8,128)(2,1)S(1)}, u32[]{:S(2)}, u32[]{:S(2)}) collective-permute-start(bf16[256,256]{1,0:T(8,128)(2,1)S(1)} %slice.98), channel_id=1, source_target_pairs={{0,4},{1,5},{4,8},{5,9},{8,12},{9,13},{12,14},{13,15},{14,10},{15,... | collective-permute-start | bytes 393224 | tf_op jit(solution)/shard_map/ppermute | solution.py:477
  71.0 13.2 %collective-permute-start.26 = (bf16[512,256]{1,0:T(8,128)(2,1)S(1)}, bf16[512,256]{1,0:T(8,128)(2,1)S(1)}, u32[]{:S(2)}, u32[]{:S(2)}) collective-permute-start(bf16[512,256]{1,0:T(8,128)(2,1)S(1)} %get-tuple-element.183), channel_id=1, source_target_pairs={{0,4},{1,5},{4,8},{5,9},{8,12},{9,13},{12,14},{13,15},{14,10},{15,... | collective-permute-start | bytes 786440 | tf_op jit(solution)/shard_map/ppermute | solution.py:456
  71.0 13.1 %collective-permute-start.30 = (bf16[512,256]{1,0:T(8,128)(2,1)S(1)}, bf16[512,256]{1,0:T(8,128)(2,1)S(1)}, u32[]{:S(2)}, u32[]{:S(2)}) collective-permute-start(bf16[512,256]{1,0:T(8,128)(2,1)S(1)} %get-tuple-element.184), channel_id=1, source_target_pairs={{4,0},{5,1},{8,4},{9,5},{12,8},{13,9},{14,12},{15,13},{10,14},{11,... | collective-permute-start | bytes 786440 | tf_op jit(solution)/shard_map/ppermute | solution.py:456
  72.6 13.7 %collective-permute-start.20 = (bf16[512,256]{1,0:T(8,128)(2,1)S(1)}, bf16[512,256]{1,0:T(8,128)(2,1)S(1)}, u32[]{:S(2)}, u32[]{:S(2)}) collective-permute-start(bf16[512,256]{1,0:T(8,128)(2,1)S(1)} %get-tuple-element.157), channel_id=1, source_target_pairs={{0,4},{1,5},{4,8},{5,9},{8,12},{9,13},{12,14},{13,15},{14,10},{15,... | collective-permute-start | bytes 786440 | tf_op jit(solution)/shard_map/ppermute | solution.py:456
  72.7 13.6 %collective-permute-start.21 = (bf16[512,256]{1,0:T(8,128)(2,1)S(1)}, bf16[512,256]{1,0:T(8,128)(2,1)S(1)}, u32[]{:S(2)}, u32[]{:S(2)}) collective-permute-start(bf16[512,256]{1,0:T(8,128)(2,1)S(1)} %get-tuple-element.159), channel_id=1, source_target_pairs={{4,0},{5,1},{8,4},{9,5},{12,8},{13,9},{14,12},{15,13},{10,14},{11,... | collective-permute-start | bytes 786440 | tf_op jit(solution)/shard_map/ppermute | solution.py:456
  84.3 19.8 %collective-permute-start.27 = (bf16[512,256]{1,0:T(8,128)(2,1)S(1)}, bf16[512,256]{1,0:T(8,128)(2,1)S(1)}, u32[]{:S(2)}, u32[]{:S(2)}) collective-permute-start(bf16[512,256]{1,0:T(8,128)(2,1)S(1)} %get-tuple-element.189), channel_id=1, source_target_pairs={{0,4},{1,5},{4,8},{5,9},{8,12},{9,13},{12,14},{13,15},{14,10},{15,... | collective-permute-start | bytes 786440 | tf_op jit(solution)/shard_map/ppermute | solution.py:456
  86.3 17.8 %collective-permute-start.31 = (bf16[512,256]{1,0:T(8,128)(2,1)S(1)}, bf16[512,256]{1,0:T(8,128)(2,1)S(1)}, u32[]{:S(2)}, u32[]{:S(2)}) collective-permute-start(bf16[512,256]{1,0:T(8,128)(2,1)S(1)} %get-tuple-element.190), channel_id=1, source_target_pairs={{4,0},{5,1},{8,4},{9,5},{12,8},{13,9},{14,12},{15,13},{10,14},{11,... | collective-permute-start | bytes 786440 | tf_op jit(solution)/shard_map/ppermute | solution.py:456
  86.5 23.0 %collective-permute-start.22 = (bf16[512,256]{1,0:T(8,128)(2,1)S(1)}, bf16[512,256]{1,0:T(8,128)(2,1)S(1)}, u32[]{:S(2)}, u32[]{:S(2)}) collective-permute-start(bf16[512,256]{1,0:T(8,128)(2,1)S(1)} %get-tuple-element.164), channel_id=1, source_target_pairs={{0,4},{1,5},{4,8},{5,9},{8,12},{9,13},{12,14},{13,15},{14,10},{15,... | collective-permute-start | bytes 786440 | tf_op jit(solution)/shard_map/ppermute | solution.py:456
  95.6 13.8 %collective-permute-start.23 = (bf16[512,256]{1,0:T(8,128)(2,1)S(1)}, bf16[512,256]{1,0:T(8,128)(2,1)S(1)}, u32[]{:S(2)}, u32[]{:S(2)}) collective-permute-start(bf16[512,256]{1,0:T(8,128)(2,1)S(1)} %get-tuple-element.166), channel_id=1, source_target_pairs={{4,0},{5,1},{8,4},{9,5},{12,8},{13,9},{14,12},{15,13},{10,14},{11,... | collective-permute-start | bytes 786440 | tf_op jit(solution)/shard_map/ppermute | solution.py:456
  104.3 23.5 %collective-permute-start.28 = (bf16[512,256]{1,0:T(8,128)(2,1)S(1)}, bf16[512,256]{1,0:T(8,128)(2,1)S(1)}, u32[]{:S(2)}, u32[]{:S(2)}) collective-permute-start(bf16[512,256]{1,0:T(8,128)(2,1)S(1)} %get-tuple-element.187), channel_id=1, source_target_pairs={{0,4},{1,5},{4,8},{5,9},{8,12},{9,13},{12,14},{13,15},{14,10},{15,... | collective-permute-start | bytes 786440 | tf_op jit(solution)/shard_map/ppermute | solution.py:456
  104.3 23.4 %collective-permute-start.32 = (bf16[512,256]{1,0:T(8,128)(2,1)S(1)}, bf16[512,256]{1,0:T(8,128)(2,1)S(1)}, u32[]{:S(2)}, u32[]{:S(2)}) collective-permute-start(bf16[512,256]{1,0:T(8,128)(2,1)S(1)} %get-tuple-element.188), channel_id=1, source_target_pairs={{4,0},{5,1},{8,4},{9,5},{12,8},{13,9},{14,12},{15,13},{10,14},{11,... | collective-permute-start | bytes 786440 | tf_op jit(solution)/shard_map/ppermute | solution.py:456
  109.6 18.3 %collective-permute-start.34 = (bf16[512,256]{1,0:T(8,128)(2,1)S(1)}, bf16[512,256]{1,0:T(8,128)(2,1)S(1)}, u32[]{:S(2)}, u32[]{:S(2)}) collective-permute-start(bf16[512,256]{1,0:T(8,128)(2,1)S(1)} %get-tuple-element.179), channel_id=1, source_target_pairs={{0,4},{1,5},{4,8},{5,9},{8,12},{9,13},{12,14},{13,15},{14,10},{15,... | collective-permute-start | bytes 786440 | tf_op jit(solution)/shard_map/ppermute | solution.py:456
  109.7 18.3 %collective-permute-start.35 = (bf16[512,256]{1,0:T(8,128)(2,1)S(1)}, bf16[512,256]{1,0:T(8,128)(2,1)S(1)}, u32[]{:S(2)}, u32[]{:S(2)}) collective-permute-start(bf16[512,256]{1,0:T(8,128)(2,1)S(1)} %get-tuple-element.180), channel_id=1, source_target_pairs={{4,0},{5,1},{8,4},{9,5},{12,8},{13,9},{14,12},{15,13},{10,14},{11,... | collective-permute-start | bytes 786440 | tf_op jit(solution)/shard_map/ppermute | solution.py:456
  118.8 12.5 %collective-permute-start.24 = (bf16[256,1280]{1,0:T(8,128)(2,1)S(1)}, bf16[256,1280]{1,0:T(8,128)(2,1)S(1)}, u32[]{:S(2)}, u32[]{:S(2)}) collective-permute-start(bf16[256,1280]{1,0:T(8,128)(2,1)S(1)} %get-tuple-element.171), channel_id=1, source_target_pairs={{0,1},{1,0},{2,3},{3,2},{4,5},{5,4},{6,7},{7,6},{8,9},{9,8},{10,11... | collective-permute-start | bytes 1966088 | tf_op jit(solution)/shard_map/ppermute | solution.py:507
  (66 other events, 587.3 us)

commit v2 on v1

--- a/solution.py
+++ b/solution.py
@@ -171,7 +171,7 @@
         scratch_shapes=[pltpu.SMEM(tables[3].shape, jnp.int32)]
         + [pltpu.VMEM((2, rows, WIDE), bf16)] * 3
         + [pltpu.VMEM((1, 2 * rows, 2 * DH), bf16), pltpu.SemaphoreType.DMA((7,))],
-        compiler_params=pltpu.CompilerParams(vmem_limit_bytes=16 << 20),
+        compiler_params=pltpu.CompilerParams(vmem_limit_bytes=8 << 20),
         cost_estimate=pl.CostEstimate(flops=0, bytes_accessed=12 << 20, transcendentals=0),
     )(*tables, *mine, other, block)
 
@@ -199,7 +199,7 @@
             pltpu.VMEM((len(offsets), 2 * rows, 2 * DH), jnp.bfloat16),
             pltpu.SemaphoreType.DMA((len(blocks),)),
         ],
-        compiler_params=pltpu.CompilerParams(vmem_limit_bytes=12 << 20),
+        compiler_params=pltpu.CompilerParams(vmem_limit_bytes=6 << 20),
         cost_estimate=pl.CostEstimate(flops=0, bytes_accessed=8 << 20, transcendentals=0),
     )(plan, qt, *stats, *blocks)
 
@@ -411,7 +411,7 @@
             pltpu.SemaphoreType.DMA((4, HALF)),
             pltpu.SemaphoreType.DMA((2 * len(offsets), HALF)),
         ],
-        compiler_params=pltpu.CompilerParams(vmem_limit_bytes=(24 << 20) + (len(offsets) << 19)),
+        compiler_params=pltpu.CompilerParams(vmem_limit_bytes=(13 << 20) + (len(offsets) << 19)),
         cost_estimate=pl.CostEstimate(flops=8 << 30, bytes_accessed=16 << 20, transcendentals=0),
     )(plan, *arrays)
 

time: 133 us -> 132 us (level)
  the two profiles are of different devices: /device:TPU:15 before, /device:TPU:31 now
where the time goes in v2:
time: 132 us; the launch traced here: 131 us
  starting transfers between devices  61.1 us (46%)
  Pallas kernels  34.1 us (26%)
  waiting for transfers between devices  16.4 us (12%)
  local copies, waits for them, and re-layouts  13.1 us (10%)
  other arithmetic  4.82 us (4%)
  between operations  1.49 us (1%)
    ppermute x16, starting transfers between devices, shift(): return [lax.ppermute(array, 'leaf', ring) for array in arrays]  38.2 us
    pallas_call x4, Pallas kernels, gradients(): pl.pallas_call(functools.partial(grads_kernel, chips, tuple(offsets), fir...  19.2 us
    unnamed x106, local copies, waits for them, and re-layouts  10.9 us
    ppermute x6, waiting for transfers between devices, local(): lax.ppermute(up, 'leaf', right)  10.7 us
    pallas_call x2, Pallas kernels, prepare(): pl.pallas_call(functools.partial(prepare_kernel, head), in_specs=[SMEM] *...  9.23 us
    ppermute x6, starting transfers between devices, local(): lax.ppermute(down, 'leaf', left)  8.09 us
    ppermute x1, starting transfers between devices, local(): ours, theirs = (terms[HALF], lax.ppermute(lead, 'leaf', swap))  7.36 us
    pallas_call x6, Pallas kernels, measure(): pl.pallas_call(functools.partial(measure_kernel, offsets), in_specs=[SMEM...  5.61 us
  transfers between devices with their start and end apart: 37, of which 12 were waited for; matrix products, arithmetic and copies ran while one was open for 3% of the time, Pallas kernels for 21%

profile of v2, /device:TPU:31, one launch (start us, length us, event | category | flops | bytes accessed | tf_op | source)
XLA Modules:
  0.0 131.0 jit_solution(906631057638505055)
XLA Ops:
  0.7 1.9 %constant_dynamic-slice_fusion = (bf16[256,128]{1,0:T(8,128)(2,1)}, bf16[256,128]{1,0:T(8,128)(2,1)S(1)}, bf16[256,128]{1,0:T(8,128)(2,1)S(1)}, bf16[256,128]{1,...) fusion(bf16[256,512]{1,0:T(8,128)(2,1)} %param.11, ...), kind=kLoop, calls=%fused_computation.47 | loop fusion | bytes 1048592 | tf_op jit(solution)/shard_map/dynamic_slice | solution.py:438
  9.0 4.6 %shard_map.116 = (s32[32]{0:T(128)S(1)}, bf16[2,128,1280]{2,1,0:T(8,128)(2,1)S(1)}, bf16[2,128,1280]{2,1,0:T(8,128)(2,1)S(1)}, bf16[2,1280,128]{2,1,0:T(8,128)(2...) custom-call(s32[1]{0:T(128)} %bitcast.me_ref, ...), custom_call_target="tpu_custom_call" | custom-call | bytes 12582912 | tf_op jit(solution)/shard_map/pallas_call | solution.py:157
  13.8 1.5 %collective-permute-start.11 = (bf16[512,256]{1,0:T(8,128)(2,1)S(1)}, bf16[512,256]{1,0:T(8,128)(2,1)S(1)}, u32[]{:S(2)}, u32[]{:S(2)}) collective-permute-start(bf16[512,256]{1,0:T(8,128)(2,1)S(1)} %collective-permute-done.9.refs_0_.refs_15_), channel_id=1, source_target_pairs={{4,0},{5,1},{8,4},{9,5},{12,8},{13,9},{14,12},{15,13},{10,14},{11,... | collective-permute-start | bytes 786440 | tf_op jit(solution)/shard_map/ppermute | solution.py:466
  15.3 4.6 %shard_map.112 = (s32[32]{0:T(128)S(1)}, bf16[2,128,1280]{2,1,0:T(8,128)(2,1)S(1)}, bf16[2,128,1280]{2,1,0:T(8,128)(2,1)S(1)}, bf16[2,1280,128]{2,1,0:T(8,128)(2...) custom-call(s32[1]{0:T(128)} %bitcast.me_ref, ...), custom_call_target="tpu_custom_call" | custom-call | bytes 12582912 | tf_op jit(solution)/shard_map/pallas_call | solution.py:157
  22.3 2.2 %collective-permute-done.10.refs_1_.refs_14_ = bf16[512,256]{1,0:T(8,128)(2,1)S(1)} collective-permute-done((bf16[512,256]{1,0:T(8,128)(2,1)S(1)}, bf16[512,256]{1,0:T(8,128)(2,1)S(1)}, u32[]{:S(2)}, u32[]{:S(2)}) %collective-permute-start.10) | collective-permute-done | bytes 262176 | tf_op jit(solution)/shard_map/ppermute | solution.py:466
  26.8 3.3 %collective-permute-done.4.refs_1_.refs_12_ = bf16[512,256]{1,0:T(8,128)(2,1)S(1)} collective-permute-done((bf16[512,256]{1,0:T(8,128)(2,1)S(1)}, bf16[512,256]{1,0:T(8,128)(2,1)S(1)}, u32[]{:S(2)}, u32[]{:S(2)}) %collective-permute-start.4) | collective-permute-done | bytes 262176 | tf_op jit(solution)/shard_map/ppermute | solution.py:466
  33.2 2.5 %collective-permute-done.12.refs_1_.refs_20_ = bf16[512,256]{1,0:T(8,128)(2,1)S(1)} collective-permute-done((bf16[512,256]{1,0:T(8,128)(2,1)S(1)}, bf16[512,256]{1,0:T(8,128)(2,1)S(1)}, u32[]{:S(2)}, u32[]{:S(2)}) %collective-permute-start.12) | collective-permute-done | bytes 262176 | tf_op jit(solution)/shard_map/ppermute | solution.py:466
  36.0 2.7 %collective-permute-start.17 = (bf16[256,256]{1,0:T(8,128)(2,1)S(1)}, bf16[256,256]{1,0:T(8,128)(2,1)S(1)}, u32[]{:S(2)}, u32[]{:S(2)}) collective-permute-start(bf16[256,256]{1,0:T(8,128)(2,1)S(1)} %slice.99), channel_id=1, source_target_pairs={{4,0},{5,1},{8,4},{9,5},{12,8},{13,9},{14,12},{15,13},{10,14},{11,... | collective-permute-start | bytes 393224 | tf_op jit(solution)/shard_map/ppermute | solution.py:477
  38.7 2.6 %collective-permute-done.6.refs_1_.refs_16_ = bf16[512,256]{1,0:T(8,128)(2,1)S(1)} collective-permute-done((bf16[512,256]{1,0:T(8,128)(2,1)S(1)}, bf16[512,256]{1,0:T(8,128)(2,1)S(1)}, u32[]{:S(2)}, u32[]{:S(2)}) %collective-permute-start.6) | collective-permute-done | bytes 262176 | tf_op jit(solution)/shard_map/ppermute | solution.py:466
  41.6 1.5 %collective-permute-start.15 = (bf16[256,256]{1,0:T(8,128)(2,1)S(1)}, bf16[256,256]{1,0:T(8,128)(2,1)S(1)}, u32[]{:S(2)}, u32[]{:S(2)}) collective-permute-start(bf16[256,256]{1,0:T(8,128)(2,1)S(1)} %slice.97), channel_id=1, source_target_pairs={{4,0},{5,1},{8,4},{9,5},{12,8},{13,9},{14,12},{15,13},{10,14},{11,... | collective-permute-start | bytes 393224 | tf_op jit(solution)/shard_map/ppermute | solution.py:477
  46.3 6.1 %shard_map.120 = (bf16[3,512,256]{2,1,0:T(8,128)(2,1)S(1)}, bf16[3,512,256]{2,1,0:T(8,128)(2,1)S(1)}, bf16[256,256]{1,0:T(8,128)(2,1)}, bf16[256,256]{1,0:T(8,12...) custom-call(s32[32]{0:T(128)S(1)} %get-tuple-element.95.plan, ...), custom_call_target="tpu_custom_call" | custom-call | flops 8589934592 | bytes 16777216 | tf_op jit(solution)/shard_map/pallas_call | solution.py:394
  53.1 1.5 %copy-done.43 = f32[2,2,128,1280]{3,2,1,0:T(8,128)} copy-done((f32[2,2,128,1280]{3,2,1,0:T(8,128)}, f32[2,2,128,1280]{3,2,1,0:T(8,128)S(1)}, u32[]{:S(2)}) %copy-start.43) | copy-done | bytes 2621464
  55.8 14.1 %collective-permute-start.25 = (bf16[256,256]{1,0:T(8,128)(2,1)}, bf16[256,256]{1,0:T(8,128)(2,1)}, u32[]{:S(2)}, u32[]{:S(2)}) collective-permute-start(bf16[256,256]{1,0:T(8,128)(2,1)} %get-tuple-element.173), channel_id=1, source_target_pairs={{0,4},{1,5},{4,8},{5,9},{8,12},{9,13},{12,14},{13,15},{14,10},{15,... | collective-permute-start | bytes 393224 | tf_op jit(solution)/shard_map/ppermute | solution.py:456
  70.0 1.5 %collective-permute-start.18 = (bf16[256,256]{1,0:T(8,128)(2,1)}, bf16[256,256]{1,0:T(8,128)(2,1)S(1)}, u32[]{:S(2)}, u32[]{:S(2)}) collective-permute-start(bf16[256,256]{1,0:T(8,128)(2,1)} %copy-done.40), channel_id=1, source_target_pairs={{0,4},{1,5},{4,8},{5,9},{8,12},{9,13},{12,14},{13,15},{14,10},{15,... | collective-permute-start | bytes 393224 | tf_op jit(solution)/shard_map/ppermute | solution.py:456
  72.2 1.9 %collective-permute-done.29 = bf16[256,256]{1,0:T(8,128)(2,1)} collective-permute-done((bf16[256,256]{1,0:T(8,128)(2,1)}, bf16[256,256]{1,0:T(8,128)(2,1)}, u32[]{:S(2)}, u32[]{:S(2)}) %collective-permute-start.29) | collective-permute-done | bytes 131104 | tf_op jit(solution)/shard_map/ppermute | solution.py:456
  83.7 1.7 %copy-done.44 = f32[2,2,128,1280]{3,2,1,0:T(8,128)S(1)} copy-done((f32[2,2,128,1280]{3,2,1,0:T(8,128)S(1)}, f32[2,2,128,1280]{3,2,1,0:T(8,128)}, u32[]{:S(2)}) %copy-start.44) | copy-done | bytes 2621464
  85.5 2.7 %shard_map.121 = (bf16[2,512,256]{2,1,0:T(8,128)(2,1)S(1)}, bf16[2,512,256]{2,1,0:T(8,128)(2,1)S(1)}, f32[2,2,128,1280]{3,2,1,0:T(8,128)S(1)}) custom-call(s32[32]{0:T(128)S(1)} %get-tuple-element.95.plan, bf16[2,128,1280]{2,1,0:T(8,128)(2,1)S(1)} %copy-done.4, bf16[2,128,1280]{2,1,0:T(8,128)(2,1)S(1)} %copy-done.34, bf16[2,1280,128]{2,1,0:T(8,128)(2,1)S(1)} %copy-done.37, ...), custom_call_target="tpu_custom_call" | custom-call | flops 8589934592 | bytes 16777216 | tf_op jit(solution)/shard_map/pallas_call | solution.py:394
  88.5 7.4 %collective-permute-start.31 = (bf16[512,256]{1,0:T(8,128)(2,1)S(1)}, bf16[512,256]{1,0:T(8,128)(2,1)S(1)}, u32[]{:S(2)}, u32[]{:S(2)}) collective-permute-start(bf16[512,256]{1,0:T(8,128)(2,1)S(1)} %get-tuple-element.190), channel_id=1, source_target_pairs={{4,0},{5,1},{8,4},{9,5},{12,8},{13,9},{14,12},{15,13},{10,14},{11,... | collective-permute-start | bytes 786440 | tf_op jit(solution)/shard_map/ppermute | solution.py:456
  96.1 1.7 %collective-permute-start.23 = (bf16[512,256]{1,0:T(8,128)(2,1)S(1)}, bf16[512,256]{1,0:T(8,128)(2,1)S(1)}, u32[]{:S(2)}, u32[]{:S(2)}) collective-permute-start(bf16[512,256]{1,0:T(8,128)(2,1)S(1)} %get-tuple-element.166), channel_id=1, source_target_pairs={{4,0},{5,1},{8,4},{9,5},{12,8},{13,9},{14,12},{15,13},{10,14},{11,... | collective-permute-start | bytes 786440 | tf_op jit(solution)/shard_map/ppermute | solution.py:456
  97.8 2.7 %shard_map.122 = (bf16[2,512,256]{2,1,0:T(8,128)(2,1)S(1)}, bf16[2,512,256]{2,1,0:T(8,128)(2,1)S(1)}, f32[2,2,128,1280]{3,2,1,0:T(8,128)S(1)}) custom-call(s32[32]{0:T(128)S(1)} %get-tuple-element.95.plan, bf16[2,128,1280]{2,1,0:T(8,128)(2,1)S(1)} %copy-done.4, bf16[2,128,1280]{2,1,0:T(8,128)(2,1)S(1)} %copy-done.35, bf16[2,1280,128]{2,1,0:T(8,128)(2,1)S(1)} %copy-done.37, ...), custom_call_target="tpu_custom_call" | custom-call | flops 8589934592 | bytes 16777216 | tf_op jit(solution)/shard_map/pallas_call | solution.py:394
  100.7 3.8 %collective-permute-start.28 = (bf16[512,256]{1,0:T(8,128)(2,1)S(1)}, bf16[512,256]{1,0:T(8,128)(2,1)S(1)}, u32[]{:S(2)}, u32[]{:S(2)}) collective-permute-start(bf16[512,256]{1,0:T(8,128)(2,1)S(1)} %get-tuple-element.187), channel_id=1, source_target_pairs={{0,4},{1,5},{4,8},{5,9},{8,12},{9,13},{12,14},{13,15},{14,10},{15,... | collective-permute-start | bytes 786440 | tf_op jit(solution)/shard_map/ppermute | solution.py:456
  104.5 5.0 %collective-permute-start.32 = (bf16[512,256]{1,0:T(8,128)(2,1)S(1)}, bf16[512,256]{1,0:T(8,128)(2,1)S(1)}, u32[]{:S(2)}, u32[]{:S(2)}) collective-permute-start(bf16[512,256]{1,0:T(8,128)(2,1)S(1)} %get-tuple-element.188), channel_id=1, source_target_pairs={{4,0},{5,1},{8,4},{9,5},{12,8},{13,9},{14,12},{15,13},{10,14},{11,... | collective-permute-start | bytes 786440 | tf_op jit(solution)/shard_map/ppermute | solution.py:456
  111.1 7.7 %shard_map.123 = (bf16[1,512,256]{2,1,0:T(8,128)(2,1)S(1)}, bf16[1,512,256]{2,1,0:T(8,128)(2,1)S(1)}, bf16[256,1280]{1,0:T(8,128)(2,1)S(1)}, bf16[256,1280]{1,0:T(8,128)(2,1)S(1)}) custom-call(s32[32]{0:T(128)S(1)} %get-tuple-element.95.plan, bf16[2,128,1280]{2,1,0:T(8,128)(2,1)S(1)} %copy-done.4, bf16[2,128,1280]{2,1,0:T(8,128)(2,1)S(1)} %copy-done.35, ...), custom_call_target="tpu_custom_call" | custom-call | flops 8589934592 | bytes 16777216 | tf_op jit(solution)/shard_map/pallas_call | solution.py:394
  118.8 7.4 %collective-permute-start.24 = (bf16[256,1280]{1,0:T(8,128)(2,1)S(1)}, bf16[256,1280]{1,0:T(8,128)(2,1)S(1)}, u32[]{:S(2)}, u32[]{:S(2)}) collective-permute-start(bf16[256,1280]{1,0:T(8,128)(2,1)S(1)} %get-tuple-element.171), channel_id=1, source_target_pairs={{0,1},{1,0},{2,3},{3,2},{4,5},{5,4},{6,7},{7,6},{8,9},{9,8},{10,11... | collective-permute-start | bytes 1966088 | tf_op jit(solution)/shard_map/ppermute | solution.py:507
  (197 shorter events, 36.8 us)
Async XLA Ops:
  7.2 12.7 %collective-permute-start.2 = (bf16[512,256]{1,0:T(8,128)(2,1)S(1)}, bf16[512,256]{1,0:T(8,128)(2,1)S(1)}, u32[]{:S(2)}, u32[]{:S(2)}) collective-permute-start(bf16[512,256]{1,0:T(8,128)(2,1)S(1)} %pad_maximum_fusion.3.block.refs_12_), channel_id=1, source_target_pairs={{0,4},{1,5},{4,8},{5,9},{8,12},{9,13},{12,14},{13,15},{14,10},{15,... | collective-permute-start | bytes 786440 | tf_op jit(solution)/shard_map/ppermute | solution.py:466
  7.4 12.5 %collective-permute-start.3 = (bf16[512,256]{1,0:T(8,128)(2,1)S(1)}, bf16[512,256]{1,0:T(8,128)(2,1)S(1)}, u32[]{:S(2)}, u32[]{:S(2)}) collective-permute-start(bf16[512,256]{1,0:T(8,128)(2,1)S(1)} %pad_maximum_fusion.3.block.refs_12_), channel_id=1, source_target_pairs={{4,0},{5,1},{8,4},{9,5},{12,8},{13,9},{14,12},{15,13},{10,14},{11,... | collective-permute-start | bytes 786440 | tf_op jit(solution)/shard_map/ppermute | solution.py:466
  13.7 10.7 %collective-permute-start.10 = (bf16[512,256]{1,0:T(8,128)(2,1)S(1)}, bf16[512,256]{1,0:T(8,128)(2,1)S(1)}, u32[]{:S(2)}, u32[]{:S(2)}) collective-permute-start(bf16[512,256]{1,0:T(8,128)(2,1)S(1)} %collective-permute-done.8.refs_1_.refs_14_), channel_id=1, source_target_pairs={{0,4},{1,5},{4,8},{5,9},{8,12},{9,13},{12,14},{13,15},{14,10},{15,... | collective-permute-start | bytes 786440 | tf_op jit(solution)/shard_map/ppermute | solution.py:466
  13.8 10.7 %collective-permute-start.11 = (bf16[512,256]{1,0:T(8,128)(2,1)S(1)}, bf16[512,256]{1,0:T(8,128)(2,1)S(1)}, u32[]{:S(2)}, u32[]{:S(2)}) collective-permute-start(bf16[512,256]{1,0:T(8,128)(2,1)S(1)} %collective-permute-done.9.refs_0_.refs_15_), channel_id=1, source_target_pairs={{4,0},{5,1},{8,4},{9,5},{12,8},{13,9},{14,12},{15,13},{10,14},{11,... | collective-permute-start | bytes 786440 | tf_op jit(solution)/shard_map/ppermute | solution.py:466
  20.0 10.1 %collective-permute-start.4 = (bf16[512,256]{1,0:T(8,128)(2,1)S(1)}, bf16[512,256]{1,0:T(8,128)(2,1)S(1)}, u32[]{:S(2)}, u32[]{:S(2)}) collective-permute-start(bf16[512,256]{1,0:T(8,128)(2,1)S(1)} %collective-permute-done.2.refs_1_.refs_12_), channel_id=1, source_target_pairs={{0,4},{1,5},{4,8},{5,9},{8,12},{9,13},{12,14},{13,15},{14,10},{15,... | collective-permute-start | bytes 786440 | tf_op jit(solution)/shard_map/ppermute | solution.py:466
  20.0 10.1 %collective-permute-start.5 = (bf16[512,256]{1,0:T(8,128)(2,1)S(1)}, bf16[512,256]{1,0:T(8,128)(2,1)S(1)}, u32[]{:S(2)}, u32[]{:S(2)}) collective-permute-start(bf16[512,256]{1,0:T(8,128)(2,1)S(1)} %collective-permute-done.3.refs_0_.refs_13_), channel_id=1, source_target_pairs={{4,0},{5,1},{8,4},{9,5},{12,8},{13,9},{14,12},{15,13},{10,14},{11,... | collective-permute-start | bytes 786440 | tf_op jit(solution)/shard_map/ppermute | solution.py:466
  24.5 11.2 %collective-permute-start.12 = (bf16[512,256]{1,0:T(8,128)(2,1)S(1)}, bf16[512,256]{1,0:T(8,128)(2,1)S(1)}, u32[]{:S(2)}, u32[]{:S(2)}) collective-permute-start(bf16[512,256]{1,0:T(8,128)(2,1)S(1)} %collective-permute-done.10.refs_1_.refs_14_), channel_id=1, source_target_pairs={{0,4},{1,5},{4,8},{5,9},{8,12},{9,13},{12,14},{13,15},{14,10},{15,... | collective-permute-start | bytes 786440 | tf_op jit(solution)/shard_map/ppermute | solution.py:466
  24.7 11.0 %collective-permute-start.13 = (bf16[512,256]{1,0:T(8,128)(2,1)S(1)}, bf16[512,256]{1,0:T(8,128)(2,1)S(1)}, u32[]{:S(2)}, u32[]{:S(2)}) collective-permute-start(bf16[512,256]{1,0:T(8,128)(2,1)S(1)} %collective-permute-done.11.refs_0_.refs_15_), channel_id=1, source_target_pairs={{4,0},{5,1},{8,4},{9,5},{12,8},{13,9},{14,12},{15,13},{10,14},{11,... | collective-permute-start | bytes 786440 | tf_op jit(solution)/shard_map/ppermute | solution.py:466
  30.1 11.2 %collective-permute-start.6 = (bf16[512,256]{1,0:T(8,128)(2,1)S(1)}, bf16[512,256]{1,0:T(8,128)(2,1)S(1)}, u32[]{:S(2)}, u32[]{:S(2)}) collective-permute-start(bf16[512,256]{1,0:T(8,128)(2,1)S(1)} %collective-permute-done.4.refs_1_.refs_12_), channel_id=1, source_target_pairs={{0,4},{1,5},{4,8},{5,9},{8,12},{9,13},{12,14},{13,15},{14,10},{15,... | collective-permute-start | bytes 786440 | tf_op jit(solution)/shard_map/ppermute | solution.py:466
  30.3 11.0 %collective-permute-start.7 = (bf16[512,256]{1,0:T(8,128)(2,1)S(1)}, bf16[512,256]{1,0:T(8,128)(2,1)S(1)}, u32[]{:S(2)}, u32[]{:S(2)}) collective-permute-start(bf16[512,256]{1,0:T(8,128)(2,1)S(1)} %collective-permute-done.5.refs_0_.refs_13_), channel_id=1, source_target_pairs={{4,0},{5,1},{8,4},{9,5},{12,8},{13,9},{14,12},{15,13},{10,14},{11,... | collective-permute-start | bytes 786440 | tf_op jit(solution)/shard_map/ppermute | solution.py:466
  55.8 16.4 %collective-permute-start.25 = (bf16[256,256]{1,0:T(8,128)(2,1)}, bf16[256,256]{1,0:T(8,128)(2,1)}, u32[]{:S(2)}, u32[]{:S(2)}) collective-permute-start(bf16[256,256]{1,0:T(8,128)(2,1)} %get-tuple-element.173), channel_id=1, source_target_pairs={{0,4},{1,5},{4,8},{5,9},{8,12},{9,13},{12,14},{13,15},{14,10},{15,... | collective-permute-start | bytes 393224 | tf_op jit(solution)/shard_map/ppermute | solution.py:456
  75.1 13.1 %collective-permute-start.26 = (bf16[512,256]{1,0:T(8,128)(2,1)S(1)}, bf16[512,256]{1,0:T(8,128)(2,1)S(1)}, u32[]{:S(2)}, u32[]{:S(2)}) collective-permute-start(bf16[512,256]{1,0:T(8,128)(2,1)S(1)} %get-tuple-element.183), channel_id=1, source_target_pairs={{0,4},{1,5},{4,8},{5,9},{8,12},{9,13},{12,14},{13,15},{14,10},{15,... | collective-permute-start | bytes 786440 | tf_op jit(solution)/shard_map/ppermute | solution.py:456
  75.2 13.1 %collective-permute-start.30 = (bf16[512,256]{1,0:T(8,128)(2,1)S(1)}, bf16[512,256]{1,0:T(8,128)(2,1)S(1)}, u32[]{:S(2)}, u32[]{:S(2)}) collective-permute-start(bf16[512,256]{1,0:T(8,128)(2,1)S(1)} %get-tuple-element.184), channel_id=1, source_target_pairs={{4,0},{5,1},{8,4},{9,5},{12,8},{13,9},{14,12},{15,13},{10,14},{11,... | collective-permute-start | bytes 786440 | tf_op jit(solution)/shard_map/ppermute | solution.py:456
  76.7 19.2 %collective-permute-start.20 = (bf16[512,256]{1,0:T(8,128)(2,1)S(1)}, bf16[512,256]{1,0:T(8,128)(2,1)S(1)}, u32[]{:S(2)}, u32[]{:S(2)}) collective-permute-start(bf16[512,256]{1,0:T(8,128)(2,1)S(1)} %get-tuple-element.157), channel_id=1, source_target_pairs={{0,4},{1,5},{4,8},{5,9},{8,12},{9,13},{12,14},{13,15},{14,10},{15,... | collective-permute-start | bytes 786440 | tf_op jit(solution)/shard_map/ppermute | solution.py:456
  76.8 19.0 %collective-permute-start.21 = (bf16[512,256]{1,0:T(8,128)(2,1)S(1)}, bf16[512,256]{1,0:T(8,128)(2,1)S(1)}, u32[]{:S(2)}, u32[]{:S(2)}) collective-permute-start(bf16[512,256]{1,0:T(8,128)(2,1)S(1)} %get-tuple-element.159), channel_id=1, source_target_pairs={{4,0},{5,1},{8,4},{9,5},{12,8},{13,9},{14,12},{15,13},{10,14},{11,... | collective-permute-start | bytes 786440 | tf_op jit(solution)/shard_map/ppermute | solution.py:456
  88.4 12.1 %collective-permute-start.27 = (bf16[512,256]{1,0:T(8,128)(2,1)S(1)}, bf16[512,256]{1,0:T(8,128)(2,1)S(1)}, u32[]{:S(2)}, u32[]{:S(2)}) collective-permute-start(bf16[512,256]{1,0:T(8,128)(2,1)S(1)} %get-tuple-element.189), channel_id=1, source_target_pairs={{0,4},{1,5},{4,8},{5,9},{8,12},{9,13},{12,14},{13,15},{14,10},{15,... | collective-permute-start | bytes 786440 | tf_op jit(solution)/shard_map/ppermute | solution.py:456
  88.5 12.0 %collective-permute-start.31 = (bf16[512,256]{1,0:T(8,128)(2,1)S(1)}, bf16[512,256]{1,0:T(8,128)(2,1)S(1)}, u32[]{:S(2)}, u32[]{:S(2)}) collective-permute-start(bf16[512,256]{1,0:T(8,128)(2,1)S(1)} %get-tuple-element.190), channel_id=1, source_target_pairs={{4,0},{5,1},{8,4},{9,5},{12,8},{13,9},{14,12},{15,13},{10,14},{11,... | collective-permute-start | bytes 786440 | tf_op jit(solution)/shard_map/ppermute | solution.py:456
  96.0 13.4 %collective-permute-start.22 = (bf16[512,256]{1,0:T(8,128)(2,1)S(1)}, bf16[512,256]{1,0:T(8,128)(2,1)S(1)}, u32[]{:S(2)}, u32[]{:S(2)}) collective-permute-start(bf16[512,256]{1,0:T(8,128)(2,1)S(1)} %get-tuple-element.164), channel_id=1, source_target_pairs={{0,4},{1,5},{4,8},{5,9},{8,12},{9,13},{12,14},{13,15},{14,10},{15,... | collective-permute-start | bytes 786440 | tf_op jit(solution)/shard_map/ppermute | solution.py:456
  96.1 13.4 %collective-permute-start.23 = (bf16[512,256]{1,0:T(8,128)(2,1)S(1)}, bf16[512,256]{1,0:T(8,128)(2,1)S(1)}, u32[]{:S(2)}, u32[]{:S(2)}) collective-permute-start(bf16[512,256]{1,0:T(8,128)(2,1)S(1)} %get-tuple-element.166), channel_id=1, source_target_pairs={{4,0},{5,1},{8,4},{9,5},{12,8},{13,9},{14,12},{15,13},{10,14},{11,... | collective-permute-start | bytes 786440 | tf_op jit(solution)/shard_map/ppermute | solution.py:456
  100.7 25.5 %collective-permute-start.28 = (bf16[512,256]{1,0:T(8,128)(2,1)S(1)}, bf16[512,256]{1,0:T(8,128)(2,1)S(1)}, u32[]{:S(2)}, u32[]{:S(2)}) collective-permute-start(bf16[512,256]{1,0:T(8,128)(2,1)S(1)} %get-tuple-element.187), channel_id=1, source_target_pairs={{0,4},{1,5},{4,8},{5,9},{8,12},{9,13},{12,14},{13,15},{14,10},{15,... | collective-permute-start | bytes 786440 | tf_op jit(solution)/shard_map/ppermute | solution.py:456
  104.5 21.7 %collective-permute-start.32 = (bf16[512,256]{1,0:T(8,128)(2,1)S(1)}, bf16[512,256]{1,0:T(8,128)(2,1)S(1)}, u32[]{:S(2)}, u32[]{:S(2)}) collective-permute-start(bf16[512,256]{1,0:T(8,128)(2,1)S(1)} %get-tuple-element.188), channel_id=1, source_target_pairs={{4,0},{5,1},{8,4},{9,5},{12,8},{13,9},{14,12},{15,13},{10,14},{11,... | collective-permute-start | bytes 786440 | tf_op jit(solution)/shard_map/ppermute | solution.py:456
  109.6 16.8 %collective-permute-start.34 = (bf16[512,256]{1,0:T(8,128)(2,1)S(1)}, bf16[512,256]{1,0:T(8,128)(2,1)S(1)}, u32[]{:S(2)}, u32[]{:S(2)}) collective-permute-start(bf16[512,256]{1,0:T(8,128)(2,1)S(1)} %get-tuple-element.179), channel_id=1, source_target_pairs={{0,4},{1,5},{4,8},{5,9},{8,12},{9,13},{12,14},{13,15},{14,10},{15,... | collective-permute-start | bytes 786440 | tf_op jit(solution)/shard_map/ppermute | solution.py:456
  109.6 16.8 %collective-permute-start.35 = (bf16[512,256]{1,0:T(8,128)(2,1)S(1)}, bf16[512,256]{1,0:T(8,128)(2,1)S(1)}, u32[]{:S(2)}, u32[]{:S(2)}) collective-permute-start(bf16[512,256]{1,0:T(8,128)(2,1)S(1)} %get-tuple-element.180), channel_id=1, source_target_pairs={{4,0},{5,1},{8,4},{9,5},{12,8},{13,9},{14,12},{15,13},{10,14},{11,... | collective-permute-start | bytes 786440 | tf_op jit(solution)/shard_map/ppermute | solution.py:456
  118.8 11.0 %collective-permute-start.24 = (bf16[256,1280]{1,0:T(8,128)(2,1)S(1)}, bf16[256,1280]{1,0:T(8,128)(2,1)S(1)}, u32[]{:S(2)}, u32[]{:S(2)}) collective-permute-start(bf16[256,1280]{1,0:T(8,128)(2,1)S(1)} %get-tuple-element.171), channel_id=1, source_target_pairs={{0,1},{1,0},{2,3},{3,2},{4,5},{5,4},{6,7},{7,6},{8,9},{9,8},{10,11... | collective-permute-start | bytes 1966088 | tf_op jit(solution)/shard_map/ppermute | solution.py:507
  (66 other events, 605.8 us)

commit v3 on v2

--- a/solution.py
+++ b/solution.py
@@ -420,6 +420,41 @@
     return x.astype(jnp.float32)
 
 
+def assemble_kernel(me_ref, *refs):
+    ours, theirs, refs = refs[0], refs[1], refs[2:]
+    kept, got, refs = refs[:HALF], refs[HALF:2 * HALF], refs[2 * HALF:]
+    query_grad, key_grad, value_grad, sems = refs
+    rows = ours.shape[0]
+    core = me_ref[0] % 2
+    pairs = []
+    for which, query, sums in ((core, ours, kept), (1 - core, theirs, got)):
+        column = pl.multiple_of(which * (HALF * WIDE), HALF * WIDE)
+        pairs.append((query, query_grad.at[:, pl.ds(column, HALF * WIDE)]))
+        for head in range(HALF):
+            column = pl.multiple_of((which * HALF + head) * DH, DH)
+            for first, out in ((0, key_grad), (DH, value_grad)):
+                pairs.append((sums[head].at[:rows, first:first + DH], out.at[:, pl.ds(column, DH)]))
+    for copy in run_copies(pairs, sems):
+        copy.wait()
+
+
+def assemble(me, ours, theirs, kept, got):
+    rows = ours.shape[0]
+    return pl.pallas_call(
+        assemble_kernel,
+        in_specs=[SMEM] + [HBM] * (2 + 2 * HALF),
+        out_specs=[HBM] * 3,
+        out_shape=[
+            jax.ShapeDtypeStruct((rows, 2 * HALF * WIDE), jnp.bfloat16),
+            jax.ShapeDtypeStruct((rows, 2 * HALF * DH), jnp.bfloat16),
+            jax.ShapeDtypeStruct((rows, 2 * HALF * DH), jnp.bfloat16),
+        ],
+        scratch_shapes=[pltpu.SemaphoreType.DMA((2 + 4 * HALF,))],
+        compiler_params=pltpu.CompilerParams(vmem_limit_bytes=2 << 20),
+        cost_estimate=pl.CostEstimate(flops=0, bytes_accessed=4 << 20, transcendentals=0),
+    )(me, ours, theirs, *kept, *got)
+
+
 def local(queries, keys, values, saved_out, grad_out, parents, assignment, lengths):
     rows = keys.shape[0]
     chips = lax.axis_size("leaf") // 2
@@ -512,17 +547,10 @@
     kept, got = [], []
     for head in range(HALF):
         summed = (wide(by_offset[0][head]) + ups[head] + downs[head]).astype(jnp.bfloat16)
-        kept.append(summed[:rows])
+        kept.append(summed)
         got.append(lax.ppermute(summed[rows:], "leaf", swap))
 
-    def whole(kept, got):
-        low = [jnp.where(core == 0, a, b) for a, b in zip(kept, got)]
-        high = [jnp.where(core == 0, b, a) for a, b in zip(kept, got)]
-        return jnp.concatenate(low + high, axis=1)
-
-    key_grad = whole([a[:, :DH] for a in kept], [a[:, :DH] for a in got])
-    value_grad = whole([a[:, DH:] for a in kept], [a[:, DH:] for a in got])
-    return (whole([ours], [theirs]), key_grad, value_grad)
+    return tuple(assemble(me, ours, theirs, kept, got))
 
 
 def solution(mesh):

time: 132 us -> 130 us (0.985)
  the two profiles are of different devices: /device:TPU:31 before, /device:TPU:0 now
where the time goes in v3:
time: 130 us
  starting transfers between devices  54 us (42%)
  Pallas kernels  44.5 us (34%)
  waiting for transfers between devices  27.2 us (21%)
  local copies, waits for them, and re-layouts  1.58 us (1%)
    ppermute x16, starting transfers between devices, shift(): return [lax.ppermute(array, 'leaf', ring) for array in arrays]  34.5 us
    pallas_call x4, Pallas kernels, gradients(): pl.pallas_call(functools.partial(grads_kernel, chips, tuple(offsets), fir...  25.2 us
    ppermute x16, waiting for transfers between devices, shift(): return [lax.ppermute(array, 'leaf', ring) for array in arrays]  14.6 us
    ppermute x6, starting transfers between devices, local(): lax.ppermute(down, 'leaf', left)  11.8 us
    pallas_call x2, Pallas kernels, prepare(): pl.pallas_call(functools.partial(prepare_kernel, head), in_specs=[SMEM] *...  9.22 us
    pallas_call x6, Pallas kernels, measure(): pl.pallas_call(functools.partial(measure_kernel, offsets), in_specs=[SMEM...  8.78 us
    ppermute x6, waiting for transfers between devices, local(): lax.ppermute(up, 'leaf', right)  7.92 us
    ppermute x2, starting transfers between devices, local(): lax.ppermute(down[rows:], 'leaf', left)  3.26 us
  transfers between devices with their start and end apart: 37, of which 17 were waited for; matrix products, arithmetic and copies ran while one was open for 1% of the time, Pallas kernels for 28%

profile of v3, /device:TPU:0, one launch (start us, length us, event | category | flops | bytes accessed | tf_op | source)
XLA Modules:
  0.0 129.7 jit_solution(10019899568576992293)
XLA Ops:
  4.6 2.7 %collective-permute-start.9 = (bf16[512,256]{1,0:T(8,128)(2,1)S(1)}, bf16[512,256]{1,0:T(8,128)(2,1)S(1)}, u32[]{:S(2)}, u32[]{:S(2)}) collective-permute-start(bf16[512,256]{1,0:T(8,128)(2,1)S(1)} %pad_maximum_fusion.3.block.refs_13_), channel_id=1, source_target_pairs={{4,0},{5,1},{8,4},{9,5},{12,8},{13,9},{14,12},{15,13},{10,14},{11,... | collective-permute-start | bytes 786440 | tf_op jit(solution)/shard_map/ppermute | solution.py:501
  7.4 2.0 %collective-permute-start.3 = (bf16[512,256]{1,0:T(8,128)(2,1)S(1)}, bf16[512,256]{1,0:T(8,128)(2,1)S(1)}, u32[]{:S(2)}, u32[]{:S(2)}) collective-permute-start(bf16[512,256]{1,0:T(8,128)(2,1)S(1)} %pad_maximum_fusion.2.block.refs_12_), channel_id=1, source_target_pairs={{4,0},{5,1},{8,4},{9,5},{12,8},{13,9},{14,12},{15,13},{10,14},{11,... | collective-permute-start | bytes 786440 | tf_op jit(solution)/shard_map/ppermute | solution.py:501
  9.5 4.6 %shard_map.116 = (s32[32]{0:T(128)S(1)}, bf16[2,128,1280]{2,1,0:T(8,128)(2,1)S(1)}, bf16[2,128,1280]{2,1,0:T(8,128)(2,1)S(1)}, bf16[2,1280,128]{2,1,0:T(8,128)(2...) custom-call(s32[1]{0:T(128)} %bitcast.me_ref, ...), custom_call_target="tpu_custom_call" | custom-call | bytes 12582912 | tf_op jit(solution)/shard_map/pallas_call | solution.py:157
  14.5 2.0 %collective-permute-done.8.refs_1_.refs_14_ = bf16[512,256]{1,0:T(8,128)(2,1)S(1)} collective-permute-done((bf16[512,256]{1,0:T(8,128)(2,1)S(1)}, bf16[512,256]{1,0:T(8,128)(2,1)S(1)}, u32[]{:S(2)}, u32[]{:S(2)}) %collective-permute-start.8) | collective-permute-done | bytes 262176 | tf_op jit(solution)/shard_map/ppermute | solution.py:501
  18.5 4.6 %shard_map.112 = (s32[32]{0:T(128)S(1)}, bf16[2,128,1280]{2,1,0:T(8,128)(2,1)S(1)}, bf16[2,128,1280]{2,1,0:T(8,128)(2,1)S(1)}, bf16[2,1280,128]{2,1,0:T(8,128)(2...) custom-call(s32[1]{0:T(128)} %bitcast.me_ref, ...), custom_call_target="tpu_custom_call" | custom-call | bytes 12582912 | tf_op jit(solution)/shard_map/pallas_call | solution.py:157
  25.2 2.3 %shard_map.117 = (f32[2,1,1280]{2,1,0:T(1,128)S(1)}, f32[2,1,1280]{2,1,0:T(1,128)S(1)}) custom-call(s32[32]{0:T(128)S(1)} %get-tuple-element.124.plan, bf16[2,128,1280]{2,1,0:T(8,128)(2,1)S(1)} %get-tuple-element.119.qt_ref.refs_7_.refs_6_, f32[2,1,1280]{2,1,0:T(1,128)S(1)} %get-tuple-element.127.top_in, f32[2,1,1280]{2,1,0:T(1,128)S(1)} %get-tuple-element.128.sum_in, ...), custom_call_target="tpu_custom_call" | custom-call | bytes 8388608 | tf_op jit(solution)/shard_map/pallas_call | solution.py:193
  29.7 2.3 %shard_map.113 = (f32[2,1,1280]{2,1,0:T(1,128)S(1)}, f32[2,1,1280]{2,1,0:T(1,128)S(1)}) custom-call(s32[32]{0:T(128)S(1)} %get-tuple-element.95.plan, bf16[2,128,1280]{2,1,0:T(8,128)(2,1)S(1)} %get-tuple-element.96.qt_ref.refs_0_, f32[2,1,1280]{2,1,0:T(1,128)S(1)} %get-tuple-element.103.top_in, f32[2,1,1280]{2,1,0:T(1,128)S(1)} %get-tuple-element.104.sum_in, ...), custom_call_target="tpu_custom_call" | custom-call | bytes 8388608 | tf_op jit(solution)/shard_map/pallas_call | solution.py:193
  36.9 2.1 %collective-permute-done.12.refs_1_.refs_20_ = bf16[512,256]{1,0:T(8,128)(2,1)S(1)} collective-permute-done((bf16[512,256]{1,0:T(8,128)(2,1)S(1)}, bf16[512,256]{1,0:T(8,128)(2,1)S(1)}, u32[]{:S(2)}, u32[]{:S(2)}) %collective-permute-start.12) | collective-permute-done | bytes 262176 | tf_op jit(solution)/shard_map/ppermute | solution.py:501
  42.0 2.5 %collective-permute-done.6.refs_1_.refs_16_ = bf16[512,256]{1,0:T(8,128)(2,1)S(1)} collective-permute-done((bf16[512,256]{1,0:T(8,128)(2,1)S(1)}, bf16[512,256]{1,0:T(8,128)(2,1)S(1)}, u32[]{:S(2)}, u32[]{:S(2)}) %collective-permute-start.6) | collective-permute-done | bytes 262176 | tf_op jit(solution)/shard_map/ppermute | solution.py:501
  51.2 6.5 %shard_map.120 = (bf16[3,512,256]{2,1,0:T(8,128)(2,1)S(1)}, bf16[3,512,256]{2,1,0:T(8,128)(2,1)S(1)}, bf16[256,256]{1,0:T(8,128)(2,1)S(1)}, bf16[256,256]{1,0:T(...) custom-call(s32[32]{0:T(128)S(1)} %get-tuple-element.95.plan, ...), custom_call_target="tpu_custom_call" | custom-call | flops 8589934592 | bytes 16777216 | tf_op jit(solution)/shard_map/pallas_call | solution.py:394
  57.7 2.5 %collective-permute-start.19 = (bf16[256,256]{1,0:T(8,128)(2,1)S(1)}, bf16[256,256]{1,0:T(8,128)(2,1)S(1)}, u32[]{:S(2)}, u32[]{:S(2)}) collective-permute-start(bf16[256,256]{1,0:T(8,128)(2,1)S(1)} %get-tuple-element.152), channel_id=1, source_target_pairs={{4,0},{5,1},{8,4},{9,5},{12,8},{13,9},{14,12},{15,13},{10,14},{11,... | collective-permute-start | bytes 393224 | tf_op jit(solution)/shard_map/ppermute | solution.py:491
  60.2 6.8 %collective-permute-start.25 = (bf16[256,256]{1,0:T(8,128)(2,1)S(1)}, bf16[256,256]{1,0:T(8,128)(2,1)S(1)}, u32[]{:S(2)}, u32[]{:S(2)}) collective-permute-start(bf16[256,256]{1,0:T(8,128)(2,1)S(1)} %get-tuple-element.173), channel_id=1, source_target_pairs={{0,4},{1,5},{4,8},{5,9},{8,12},{9,13},{12,14},{13,15},{14,10},{15,... | collective-permute-start | bytes 393224 | tf_op jit(solution)/shard_map/ppermute | solution.py:491
  67.6 2.3 %collective-permute-done.19 = bf16[256,256]{1,0:T(8,128)(2,1)S(1)} collective-permute-done((bf16[256,256]{1,0:T(8,128)(2,1)S(1)}, bf16[256,256]{1,0:T(8,128)(2,1)S(1)}, u32[]{:S(2)}, u32[]{:S(2)}) %collective-permute-start.19) | collective-permute-done | bytes 131104 | tf_op jit(solution)/shard_map/ppermute | solution.py:491
  72.1 6.7 %collective-permute-start.26 = (bf16[512,256]{1,0:T(8,128)(2,1)S(1)}, bf16[512,256]{1,0:T(8,128)(2,1)S(1)}, u32[]{:S(2)}, u32[]{:S(2)}) collective-permute-start(bf16[512,256]{1,0:T(8,128)(2,1)S(1)} %get-tuple-element.181), channel_id=1, source_target_pairs={{0,4},{1,5},{4,8},{5,9},{8,12},{9,13},{12,14},{13,15},{14,10},{15,... | collective-permute-start | bytes 786440 | tf_op jit(solution)/shard_map/ppermute | solution.py:491
  78.8 2.0 %collective-permute-start.20 = (bf16[512,256]{1,0:T(8,128)(2,1)S(1)}, bf16[512,256]{1,0:T(8,128)(2,1)S(1)}, u32[]{:S(2)}, u32[]{:S(2)}) collective-permute-start(bf16[512,256]{1,0:T(8,128)(2,1)S(1)} %get-tuple-element.157), channel_id=1, source_target_pairs={{0,4},{1,5},{4,8},{5,9},{8,12},{9,13},{12,14},{13,15},{14,10},{15,... | collective-permute-start | bytes 786440 | tf_op jit(solution)/shard_map/ppermute | solution.py:491
  80.8 2.7 %shard_map.121 = (bf16[2,512,256]{2,1,0:T(8,128)(2,1)S(1)}, bf16[2,512,256]{2,1,0:T(8,128)(2,1)S(1)}, f32[2,2,128,1280]{3,2,1,0:T(8,128)S(1)}) custom-call(s32[32]{0:T(128)S(1)} %get-tuple-element.95.plan, bf16[2,128,1280]{2,1,0:T(8,128)(2,1)S(1)} %get-tuple-element.96.qt_ref.refs_0_, bf16[2,128,1280]{2,1,0:T(8,128)(2,1)S(1)} %get-tuple-element.97.refs_1_, ...), custom_call_target="tpu_custom_call" | custom-call | flops 8589934592 | bytes 16777216 | tf_op jit(solution)/shard_map/pallas_call | solution.py:394
  83.6 2.2 %collective-permute-done.30 = bf16[512,256]{1,0:T(8,128)(2,1)S(1)} collective-permute-done((bf16[512,256]{1,0:T(8,128)(2,1)S(1)}, bf16[512,256]{1,0:T(8,128)(2,1)S(1)}, u32[]{:S(2)}, u32[]{:S(2)}) %collective-permute-start.30) | collective-permute-done | bytes 262176 | tf_op jit(solution)/shard_map/ppermute | solution.py:491
  85.9 8.6 %collective-permute-start.27 = (bf16[512,256]{1,0:T(8,128)(2,1)S(1)}, bf16[512,256]{1,0:T(8,128)(2,1)S(1)}, u32[]{:S(2)}, u32[]{:S(2)}) collective-permute-start(bf16[512,256]{1,0:T(8,128)(2,1)S(1)} %get-tuple-element.187), channel_id=1, source_target_pairs={{0,4},{1,5},{4,8},{5,9},{8,12},{9,13},{12,14},{13,15},{14,10},{15,... | collective-permute-start | bytes 786440 | tf_op jit(solution)/shard_map/ppermute | solution.py:491
  94.7 2.1 %collective-permute-start.22 = (bf16[512,256]{1,0:T(8,128)(2,1)S(1)}, bf16[512,256]{1,0:T(8,128)(2,1)S(1)}, u32[]{:S(2)}, u32[]{:S(2)}) collective-permute-start(bf16[512,256]{1,0:T(8,128)(2,1)S(1)} %get-tuple-element.164), channel_id=1, source_target_pairs={{0,4},{1,5},{4,8},{5,9},{8,12},{9,13},{12,14},{13,15},{14,10},{15,... | collective-permute-start | bytes 786440 | tf_op jit(solution)/shard_map/ppermute | solution.py:491
  96.8 8.3 %shard_map.122 = (bf16[2,512,256]{2,1,0:T(8,128)(2,1)S(1)}, bf16[2,512,256]{2,1,0:T(8,128)(2,1)S(1)}, f32[2,2,128,1280]{3,2,1,0:T(8,128)S(1)}) custom-call(s32[32]{0:T(128)S(1)} %get-tuple-element.95.plan, bf16[2,128,1280]{2,1,0:T(8,128)(2,1)S(1)} %get-tuple-element.96.qt_ref.refs_0_, bf16[2,128,1280]{2,1,0:T(8,128)(2,1)S(1)} %get-tuple-element.97.refs_1_, ...), custom_call_target="tpu_custom_call" | custom-call | flops 8589934592 | bytes 16777216 | tf_op jit(solution)/shard_map/pallas_call | solution.py:394
  107.4 7.7 %shard_map.123 = (bf16[1,512,256]{2,1,0:T(8,128)(2,1)S(1)}, bf16[1,512,256]{2,1,0:T(8,128)(2,1)S(1)}, bf16[256,1280]{1,0:T(8,128)(2,1)S(1)}, bf16[256,1280]{1,0:T(8,128)(2,1)S(1)}) custom-call(s32[32]{0:T(128)S(1)} %get-tuple-element.95.plan, bf16[2,128,1280]{2,1,0:T(8,128)(2,1)S(1)} %get-tuple-element.96.qt_ref.refs_0_, ...), custom_call_target="tpu_custom_call" | custom-call | flops 8589934592 | bytes 16777216 | tf_op jit(solution)/shard_map/pallas_call | solution.py:394
  115.3 3.1 %collective-permute-start.33 = (bf16[512,256]{1,0:T(8,128)(2,1)S(1)}, bf16[512,256]{1,0:T(8,128)(2,1)S(1)}, u32[]{:S(2)}, u32[]{:S(2)}) collective-permute-start(bf16[512,256]{1,0:T(8,128)(2,1)S(1)} %get-tuple-element.179), channel_id=1, source_target_pairs={{0,4},{1,5},{4,8},{5,9},{8,12},{9,13},{12,14},{13,15},{14,10},{15,... | collective-permute-start | bytes 786440 | tf_op jit(solution)/shard_map/ppermute | solution.py:491
  118.7 5.8 %collective-permute-done.33 = bf16[512,256]{1,0:T(8,128)(2,1)S(1)} collective-permute-done((bf16[512,256]{1,0:T(8,128)(2,1)S(1)}, bf16[512,256]{1,0:T(8,128)(2,1)S(1)}, u32[]{:S(2)}, u32[]{:S(2)}) %collective-permute-start.33) | collective-permute-done | bytes 262176 | tf_op jit(solution)/shard_map/ppermute | solution.py:491
  124.5 2.2 %collective-permute-done.34 = bf16[512,256]{1,0:T(8,128)(2,1)S(1)} collective-permute-done((bf16[512,256]{1,0:T(8,128)(2,1)S(1)}, bf16[512,256]{1,0:T(8,128)(2,1)S(1)}, u32[]{:S(2)}, u32[]{:S(2)}) %collective-permute-start.34) | collective-permute-done | bytes 262176 | tf_op jit(solution)/shard_map/ppermute | solution.py:491
  (100 shorter events, 33.8 us)
Async XLA Ops:
  7.4 15.7 %collective-permute-start.3 = (bf16[512,256]{1,0:T(8,128)(2,1)S(1)}, bf16[512,256]{1,0:T(8,128)(2,1)S(1)}, u32[]{:S(2)}, u32[]{:S(2)}) collective-permute-start(bf16[512,256]{1,0:T(8,128)(2,1)S(1)} %pad_maximum_fusion.2.block.refs_12_), channel_id=1, source_target_pairs={{4,0},{5,1},{8,4},{9,5},{12,8},{13,9},{14,12},{15,13},{10,14},{11,... | collective-permute-start | bytes 786440 | tf_op jit(solution)/shard_map/ppermute | solution.py:501
  9.4 13.7 %collective-permute-start.2 = (bf16[512,256]{1,0:T(8,128)(2,1)S(1)}, bf16[512,256]{1,0:T(8,128)(2,1)S(1)}, u32[]{:S(2)}, u32[]{:S(2)}) collective-permute-start(bf16[512,256]{1,0:T(8,128)(2,1)S(1)} %pad_maximum_fusion.2.block.refs_12_), channel_id=1, source_target_pairs={{0,4},{1,5},{4,8},{5,9},{8,12},{9,13},{12,14},{13,15},{14,10},{15,... | collective-permute-start | bytes 786440 | tf_op jit(solution)/shard_map/ppermute | solution.py:501
  16.4 11.2 %collective-permute-start.10 = (bf16[512,256]{1,0:T(8,128)(2,1)S(1)}, bf16[512,256]{1,0:T(8,128)(2,1)S(1)}, u32[]{:S(2)}, u32[]{:S(2)}) collective-permute-start(bf16[512,256]{1,0:T(8,128)(2,1)S(1)} %collective-permute-done.8.refs_1_.refs_14_), channel_id=1, source_target_pairs={{0,4},{1,5},{4,8},{5,9},{8,12},{9,13},{12,14},{13,15},{14,10},{15,... | collective-permute-start | bytes 786440 | tf_op jit(solution)/shard_map/ppermute | solution.py:501
  16.5 11.2 %collective-permute-start.11 = (bf16[512,256]{1,0:T(8,128)(2,1)S(1)}, bf16[512,256]{1,0:T(8,128)(2,1)S(1)}, u32[]{:S(2)}, u32[]{:S(2)}) collective-permute-start(bf16[512,256]{1,0:T(8,128)(2,1)S(1)} %collective-permute-done.9.refs_0_.refs_15_), channel_id=1, source_target_pairs={{4,0},{5,1},{8,4},{9,5},{12,8},{13,9},{14,12},{15,13},{10,14},{11,... | collective-permute-start | bytes 786440 | tf_op jit(solution)/shard_map/ppermute | solution.py:501
  23.1 10.2 %collective-permute-start.4 = (bf16[512,256]{1,0:T(8,128)(2,1)S(1)}, bf16[512,256]{1,0:T(8,128)(2,1)S(1)}, u32[]{:S(2)}, u32[]{:S(2)}) collective-permute-start(bf16[512,256]{1,0:T(8,128)(2,1)S(1)} %collective-permute-done.2.refs_1_.refs_12_), channel_id=1, source_target_pairs={{0,4},{1,5},{4,8},{5,9},{8,12},{9,13},{12,14},{13,15},{14,10},{15,... | collective-permute-start | bytes 786440 | tf_op jit(solution)/shard_map/ppermute | solution.py:501
  23.2 10.1 %collective-permute-start.5 = (bf16[512,256]{1,0:T(8,128)(2,1)S(1)}, bf16[512,256]{1,0:T(8,128)(2,1)S(1)}, u32[]{:S(2)}, u32[]{:S(2)}) collective-permute-start(bf16[512,256]{1,0:T(8,128)(2,1)S(1)} %collective-permute-done.3.refs_0_.refs_13_), channel_id=1, source_target_pairs={{4,0},{5,1},{8,4},{9,5},{12,8},{13,9},{14,12},{15,13},{10,14},{11,... | collective-permute-start | bytes 786440 | tf_op jit(solution)/shard_map/ppermute | solution.py:501
  27.7 11.2 %collective-permute-start.12 = (bf16[512,256]{1,0:T(8,128)(2,1)S(1)}, bf16[512,256]{1,0:T(8,128)(2,1)S(1)}, u32[]{:S(2)}, u32[]{:S(2)}) collective-permute-start(bf16[512,256]{1,0:T(8,128)(2,1)S(1)} %collective-permute-done.10.refs_1_.refs_14_), channel_id=1, source_target_pairs={{0,4},{1,5},{4,8},{5,9},{8,12},{9,13},{12,14},{13,15},{14,10},{15,... | collective-permute-start | bytes 786440 | tf_op jit(solution)/shard_map/ppermute | solution.py:501
  27.8 11.1 %collective-permute-start.13 = (bf16[512,256]{1,0:T(8,128)(2,1)S(1)}, bf16[512,256]{1,0:T(8,128)(2,1)S(1)}, u32[]{:S(2)}, u32[]{:S(2)}) collective-permute-start(bf16[512,256]{1,0:T(8,128)(2,1)S(1)} %collective-permute-done.11.refs_0_.refs_15_), channel_id=1, source_target_pairs={{4,0},{5,1},{8,4},{9,5},{12,8},{13,9},{14,12},{15,13},{10,14},{11,... | collective-permute-start | bytes 786440 | tf_op jit(solution)/shard_map/ppermute | solution.py:501
  33.3 11.2 %collective-permute-start.6 = (bf16[512,256]{1,0:T(8,128)(2,1)S(1)}, bf16[512,256]{1,0:T(8,128)(2,1)S(1)}, u32[]{:S(2)}, u32[]{:S(2)}) collective-permute-start(bf16[512,256]{1,0:T(8,128)(2,1)S(1)} %collective-permute-done.4.refs_1_.refs_12_), channel_id=1, source_target_pairs={{0,4},{1,5},{4,8},{5,9},{8,12},{9,13},{12,14},{13,15},{14,10},{15,... | collective-permute-start | bytes 786440 | tf_op jit(solution)/shard_map/ppermute | solution.py:501
  34.0 10.5 %collective-permute-start.7 = (bf16[512,256]{1,0:T(8,128)(2,1)S(1)}, bf16[512,256]{1,0:T(8,128)(2,1)S(1)}, u32[]{:S(2)}, u32[]{:S(2)}) collective-permute-start(bf16[512,256]{1,0:T(8,128)(2,1)S(1)} %collective-permute-done.5.refs_0_.refs_13_), channel_id=1, source_target_pairs={{4,0},{5,1},{8,4},{9,5},{12,8},{13,9},{14,12},{15,13},{10,14},{11,... | collective-permute-start | bytes 786440 | tf_op jit(solution)/shard_map/ppermute | solution.py:501
  39.0 10.3 %collective-permute-start.17 = (bf16[256,256]{1,0:T(8,128)(2,1)S(1)}, bf16[256,256]{1,0:T(8,128)(2,1)S(1)}, u32[]{:S(2)}, u32[]{:S(2)}) collective-permute-start(bf16[256,256]{1,0:T(8,128)(2,1)S(1)} %slice.69), channel_id=1, source_target_pairs={{4,0},{5,1},{8,4},{9,5},{12,8},{13,9},{14,12},{15,13},{10,14},{11,... | collective-permute-start | bytes 393224 | tf_op jit(solution)/shard_map/ppermute | solution.py:512
  57.7 9.9 %collective-permute-start.18 = (bf16[256,256]{1,0:T(8,128)(2,1)S(1)}, bf16[256,256]{1,0:T(8,128)(2,1)S(1)}, u32[]{:S(2)}, u32[]{:S(2)}) collective-permute-start(bf16[256,256]{1,0:T(8,128)(2,1)S(1)} %get-tuple-element.150), channel_id=1, source_target_pairs={{0,4},{1,5},{4,8},{5,9},{8,12},{9,13},{12,14},{13,15},{14,10},{15,... | collective-permute-start | bytes 393224 | tf_op jit(solution)/shard_map/ppermute | solution.py:491
  57.7 12.2 %collective-permute-start.19 = (bf16[256,256]{1,0:T(8,128)(2,1)S(1)}, bf16[256,256]{1,0:T(8,128)(2,1)S(1)}, u32[]{:S(2)}, u32[]{:S(2)}) collective-permute-start(bf16[256,256]{1,0:T(8,128)(2,1)S(1)} %get-tuple-element.152), channel_id=1, source_target_pairs={{4,0},{5,1},{8,4},{9,5},{12,8},{13,9},{14,12},{15,13},{10,14},{11,... | collective-permute-start | bytes 393224 | tf_op jit(solution)/shard_map/ppermute | solution.py:491
  60.2 10.3 %collective-permute-start.25 = (bf16[256,256]{1,0:T(8,128)(2,1)S(1)}, bf16[256,256]{1,0:T(8,128)(2,1)S(1)}, u32[]{:S(2)}, u32[]{:S(2)}) collective-permute-start(bf16[256,256]{1,0:T(8,128)(2,1)S(1)} %get-tuple-element.173), channel_id=1, source_target_pairs={{0,4},{1,5},{4,8},{5,9},{8,12},{9,13},{12,14},{13,15},{14,10},{15,... | collective-permute-start | bytes 393224 | tf_op jit(solution)/shard_map/ppermute | solution.py:491
  72.1 11.5 %collective-permute-start.26 = (bf16[512,256]{1,0:T(8,128)(2,1)S(1)}, bf16[512,256]{1,0:T(8,128)(2,1)S(1)}, u32[]{:S(2)}, u32[]{:S(2)}) collective-permute-start(bf16[512,256]{1,0:T(8,128)(2,1)S(1)} %get-tuple-element.181), channel_id=1, source_target_pairs={{0,4},{1,5},{4,8},{5,9},{8,12},{9,13},{12,14},{13,15},{14,10},{15,... | collective-permute-start | bytes 786440 | tf_op jit(solution)/shard_map/ppermute | solution.py:491
  78.8 15.7 %collective-permute-start.20 = (bf16[512,256]{1,0:T(8,128)(2,1)S(1)}, bf16[512,256]{1,0:T(8,128)(2,1)S(1)}, u32[]{:S(2)}, u32[]{:S(2)}) collective-permute-start(bf16[512,256]{1,0:T(8,128)(2,1)S(1)} %get-tuple-element.157), channel_id=1, source_target_pairs={{0,4},{1,5},{4,8},{5,9},{8,12},{9,13},{12,14},{13,15},{14,10},{15,... | collective-permute-start | bytes 786440 | tf_op jit(solution)/shard_map/ppermute | solution.py:491
  80.8 13.7 %collective-permute-start.21 = (bf16[512,256]{1,0:T(8,128)(2,1)S(1)}, bf16[512,256]{1,0:T(8,128)(2,1)S(1)}, u32[]{:S(2)}, u32[]{:S(2)}) collective-permute-start(bf16[512,256]{1,0:T(8,128)(2,1)S(1)} %get-tuple-element.159), channel_id=1, source_target_pairs={{4,0},{5,1},{8,4},{9,5},{12,8},{13,9},{14,12},{15,13},{10,14},{11,... | collective-permute-start | bytes 786440 | tf_op jit(solution)/shard_map/ppermute | solution.py:491
  85.9 19.1 %collective-permute-start.27 = (bf16[512,256]{1,0:T(8,128)(2,1)S(1)}, bf16[512,256]{1,0:T(8,128)(2,1)S(1)}, u32[]{:S(2)}, u32[]{:S(2)}) collective-permute-start(bf16[512,256]{1,0:T(8,128)(2,1)S(1)} %get-tuple-element.187), channel_id=1, source_target_pairs={{0,4},{1,5},{4,8},{5,9},{8,12},{9,13},{12,14},{13,15},{14,10},{15,... | collective-permute-start | bytes 786440 | tf_op jit(solution)/shard_map/ppermute | solution.py:491
  94.5 10.5 %collective-permute-start.31 = (bf16[512,256]{1,0:T(8,128)(2,1)S(1)}, bf16[512,256]{1,0:T(8,128)(2,1)S(1)}, u32[]{:S(2)}, u32[]{:S(2)}) collective-permute-start(bf16[512,256]{1,0:T(8,128)(2,1)S(1)} %get-tuple-element.188), channel_id=1, source_target_pairs={{4,0},{5,1},{8,4},{9,5},{12,8},{13,9},{14,12},{15,13},{10,14},{11,... | collective-permute-start | bytes 786440 | tf_op jit(solution)/shard_map/ppermute | solution.py:491
  94.7 12.6 %collective-permute-start.22 = (bf16[512,256]{1,0:T(8,128)(2,1)S(1)}, bf16[512,256]{1,0:T(8,128)(2,1)S(1)}, u32[]{:S(2)}, u32[]{:S(2)}) collective-permute-start(bf16[512,256]{1,0:T(8,128)(2,1)S(1)} %get-tuple-element.164), channel_id=1, source_target_pairs={{0,4},{1,5},{4,8},{5,9},{8,12},{9,13},{12,14},{13,15},{14,10},{15,... | collective-permute-start | bytes 786440 | tf_op jit(solution)/shard_map/ppermute | solution.py:491
  96.8 10.5 %collective-permute-start.23 = (bf16[512,256]{1,0:T(8,128)(2,1)S(1)}, bf16[512,256]{1,0:T(8,128)(2,1)S(1)}, u32[]{:S(2)}, u32[]{:S(2)}) collective-permute-start(bf16[512,256]{1,0:T(8,128)(2,1)S(1)} %get-tuple-element.166), channel_id=1, source_target_pairs={{4,0},{5,1},{8,4},{9,5},{12,8},{13,9},{14,12},{15,13},{10,14},{11,... | collective-permute-start | bytes 786440 | tf_op jit(solution)/shard_map/ppermute | solution.py:491
  105.2 13.1 %collective-permute-start.28 = (bf16[512,256]{1,0:T(8,128)(2,1)S(1)}, bf16[512,256]{1,0:T(8,128)(2,1)S(1)}, u32[]{:S(2)}, u32[]{:S(2)}) collective-permute-start(bf16[512,256]{1,0:T(8,128)(2,1)S(1)} %get-tuple-element.185), channel_id=1, source_target_pairs={{0,4},{1,5},{4,8},{5,9},{8,12},{9,13},{12,14},{13,15},{14,10},{15,... | collective-permute-start | bytes 786440 | tf_op jit(solution)/shard_map/ppermute | solution.py:491
  105.4 12.9 %collective-permute-start.32 = (bf16[512,256]{1,0:T(8,128)(2,1)S(1)}, bf16[512,256]{1,0:T(8,128)(2,1)S(1)}, u32[]{:S(2)}, u32[]{:S(2)}) collective-permute-start(bf16[512,256]{1,0:T(8,128)(2,1)S(1)} %get-tuple-element.186), channel_id=1, source_target_pairs={{4,0},{5,1},{8,4},{9,5},{12,8},{13,9},{14,12},{15,13},{10,14},{11,... | collective-permute-start | bytes 786440 | tf_op jit(solution)/shard_map/ppermute | solution.py:491
  115.2 13.1 %collective-permute-start.24 = (bf16[256,1280]{1,0:T(8,128)(2,1)S(1)}, bf16[256,1280]{1,0:T(8,128)(2,1)S(1)}, u32[]{:S(2)}, u32[]{:S(2)}) collective-permute-start(bf16[256,1280]{1,0:T(8,128)(2,1)S(1)} %get-tuple-element.171), channel_id=1, source_target_pairs={{0,1},{1,0},{2,3},{3,2},{4,5},{5,4},{6,7},{7,6},{8,9},{9,8},{10,11... | collective-permute-start | bytes 1966088 | tf_op jit(solution)/shard_map/ppermute | solution.py:542
  (20 other events, 114.2 us)

commit v4 on v3

--- a/solution.py
+++ b/solution.py
@@ -20,13 +20,14 @@
 SCALE = 1.0 / math.sqrt(DH)
 EXP_SCALE = SCALE / math.log(2.0)
 NN = (((1,), (0,)), ((), ()))
+NT = (((1,), (1,)), ((), ()))
 SMEM = pl.BlockSpec(memory_space=pltpu.SMEM)
 HBM = pl.BlockSpec(memory_space=pl.ANY)
 VMEM = pl.BlockSpec(memory_space=pltpu.VMEM)
 
 
-def dot(a, b):
-    return lax.dot_general(a, b, NN, preferred_element_type=jnp.float32)
+def dot(a, b, dims=NN):
+    return lax.dot_general(a, b, dims, preferred_element_type=jnp.float32)
 
 
 def ring_order(chips):
@@ -142,12 +143,17 @@
             gt_ref[side, :, lanes] = masked.T
             qt_ref[side, :, lanes] = query.T
             terms = masked.astype(jnp.float32) * o_ref[side, :, cols].astype(jnp.float32)
-            delta_ref[side, :, lanes] = jnp.sum(terms.T, axis=0, keepdims=True)
+            delta = jnp.sum(terms, axis=1, keepdims=True)
+            delta_ref[side, lanes, :] = jnp.broadcast_to(delta, (rows, DH))
     measure_blocks(plan, [0], kv_ref, qt_ref, top_ref, sum_ref)
 
 
 def row_stats(rows):
     return jax.ShapeDtypeStruct((2, 1, PER * rows), jnp.float32)
+
+
+def wide_stats(rows):
+    return jax.ShapeDtypeStruct((2, PER * rows, DH), jnp.float32)
 
 
 def prepare(head, tables, mine, other, block):
@@ -164,7 +170,7 @@
             jax.ShapeDtypeStruct((2, DH, PER * rows), bf16),
             jax.ShapeDtypeStruct((2, PER * rows, DH), bf16),
             jax.ShapeDtypeStruct((2, PER * rows, DH), bf16),
-            row_stats(rows),
+            wide_stats(rows),
             row_stats(rows),
             row_stats(rows),
         ],
@@ -222,12 +228,12 @@
         ups, downs, refs = refs[:HALF], refs[HALF:2 * HALF], refs[2 * HALF:]
         lse_out, refs = refs[:HALF], refs[HALF:]
     outs, refs = refs[:2 if last else 1], refs[2 if last else 1:]
-    (kv_ref, acc_ref, stage_ref, zero_ref, p_ref, ds_ref, sum_ref, dqt_ref, offset_ref,
+    (kv_ref, acc_ref, stage_ref, zero_ref, p_ref, ds_ref, top_ref, sum_ref, dq_ref, offset_ref,
      sems, kv_sems, out_sems, zero_sems) = refs
     lse_ref = lse_out if first else [head[5] for head in shared]
     if not last:
-        dqt_ref = outs[0]
-    rows = acc_ref.shape[1]
+        dq_ref = outs[0]
+    rows = acc_ref.shape[2]
     slots = stage_ref.shape[0]
 
     pairs = []
@@ -285,16 +291,17 @@
         return carry
 
     lax.fori_loop(0, 2 * len(offsets), send_zeros, 0)
-    dqt_ref[...] = jnp.zeros_like(dqt_ref) if first else carried[...]
+    dq_ref[...] = jnp.zeros_like(dq_ref) if first else carried[...]
     for copy in copies:
         copy.wait()
     if first:
         for head in range(HALF):
-            top_ref, total_ref = lse_out[head], sum_ref.at[head]
             top_ref[...] = shared[head][5][...]
-            total_ref[...] = shared[head][6][...]
-            measure_blocks(plan, [far], kv_ref.at[:, head], shared[head][0], top_ref, total_ref)
-            top_ref[...] = top_ref[...] * EXP_SCALE + jnp.log2(total_ref[...])
+            sum_ref[...] = shared[head][6][...]
+            measure_blocks(plan, [far], kv_ref.at[:, head], shared[head][0], top_ref, sum_ref)
+            for side in range(2):
+                lse = top_ref[side] * EXP_SCALE + jnp.log2(sum_ref[side])
+                lse_out[head][side] = jnp.broadcast_to(lse, (DH, lse.shape[1])).T
 
     def visit(i, done):
         at_block, half = i // 2, i % 2
@@ -310,22 +317,25 @@
         def look(side, carry):
             @pl.when(sees(side, i) > 0)
             def _():
-                allowed = seen_keys(rows, sees(side, i))
+                key_at = lax.broadcasted_iota(jnp.int32, (rows, rows), 1)
+                row_at = lax.broadcasted_iota(jnp.int32, (rows, rows), 0)
+                allowed = key_at <= jnp.where(sees(side, i) == OWN, row_at, sees(side, i) - 1)
                 for head in range(HALF):
                     qt_ref, gt_ref, gm_ref, qm_ref, delta_ref = shared[head][:5]
                     k = kv_ref[at_block, head, here, :DH]
                     v = kv_ref[at_block, head, here, DH:]
                     for h in range(PER):
-                        lanes = slice(h * rows, (h + 1) * rows)
-                        part = (side, slice(None), lanes)
-                        s = dot(k, qt_ref[part]) * EXP_SCALE - lse_ref[head][part]
+                        span = slice(h * rows, (h + 1) * rows)
+                        lse = jnp.concatenate([lse_ref[head][side, span, :]] * (rows // DH), axis=1)
+                        delta = jnp.concatenate([delta_ref[side, span, :]] * (rows // DH), axis=1)
+                        s = dot(qm_ref[side, span, :], k, NT) * EXP_SCALE - lse
                         p = jnp.where(allowed, jnp.exp2(s), 0.0)
-                        ds = p * (dot(v, gt_ref[part]) - delta_ref[part])
-                        p_ref[head, :, lanes] = p.astype(p_ref.dtype)
-                        ds_ref[head, :, lanes] = ds.astype(ds_ref.dtype)
-                    acc_ref[head, :, DH:] += dot(p_ref[head], gm_ref[side])
-                    acc_ref[head, :, :DH] += dot(ds_ref[head], qm_ref[side])
-                    dqt_ref[head, side] += dot(k.T, ds_ref[head])
+                        ds = p * (dot(gm_ref[side, span, :], v, NT) - delta)
+                        p_ref[head, span, :] = p.astype(p_ref.dtype)
+                        ds_ref[head, span, :] = ds.astype(ds_ref.dtype)
+                    acc_ref[head, DH:, :] += dot(gt_ref[side], p_ref[head])
+                    acc_ref[head, :DH, :] += dot(qt_ref[side], ds_ref[head])
+                    dq_ref[head, side] += dot(ds_ref[head], k)
 
             return carry
 
@@ -340,19 +350,20 @@
             acc_ref[...] = jnp.zeros_like(acc_ref)
             lax.fori_loop(0, 2, look, 0)
             for head in range(HALF):
-                stage_ref[slot, head, :, :DH] = (acc_ref[head, :, :DH] * SCALE).astype(stage_ref.dtype)
-                stage_ref[slot, head, :, DH:] = acc_ref[head, :, DH:].astype(stage_ref.dtype)
+                stage_ref[slot, head, :, :DH] = (acc_ref[head, :DH, :] * SCALE).T.astype(stage_ref.dtype)
+                stage_ref[slot, head, :, DH:] = acc_ref[head, DH:, :].T.astype(stage_ref.dtype)
             send(i, [stage_ref.at[slot, head] for head in range(HALF)], lambda head: out_sems.at[slot, head])
 
         return done + seen(i).astype(jnp.int32)
 
     done = lax.fori_loop(0, 2 * len(offsets), visit, jnp.int32(0))
     if last:
-        for side, dq_ref in enumerate(outs):
+        for side, out_ref in enumerate(outs):
             for head in range(HALF):
                 for h in range(PER):
-                    dq = (dqt_ref[head, side, :, h * rows:(h + 1) * rows] * SCALE).astype(dq_ref.dtype)
-                    dq_ref[:, (head * PER + h) * DH:(head * PER + h + 1) * DH] = dq.T
+                    cols = slice((head * PER + h) * DH, (head * PER + h + 1) * DH)
+                    dq = dq_ref[head, side, h * rows:(h + 1) * rows, :] * SCALE
+                    out_ref[:, cols] = dq.astype(out_ref.dtype)
 
     def zeros_sent(i, carry):
         @pl.when(jnp.logical_not(seen(i)))
@@ -380,10 +391,10 @@
     dense = jax.ShapeDtypeStruct((len(offsets), 2 * rows, 2 * DH), bf16)
     piece = jax.ShapeDtypeStruct((rows, 2 * DH), bf16)
     query = jax.ShapeDtypeStruct((rows, HALF * WIDE), bf16)
-    sums = jax.ShapeDtypeStruct((HALF, 2, DH, PER * rows), f32)
+    sums = jax.ShapeDtypeStruct((HALF, 2, PER * rows, DH), f32)
     out_shape, out_specs = [dense] * HALF, [HBM] * HALF
     if first:
-        out_shape += [piece] * (2 * HALF) + [row_stats(rows)] * HALF
+        out_shape += [piece] * (2 * HALF) + [wide_stats(rows)] * HALF
         out_specs += [HBM] * (2 * HALF) + [VMEM] * HALF
     out_shape += [query] * 2 if last else [sums]
     out_specs += [VMEM] * (2 if last else 1)
@@ -398,13 +409,14 @@
         out_shape=out_shape,
         scratch_shapes=[
             pltpu.VMEM((len(offsets), HALF, 2 * rows, 2 * DH), bf16),
-            pltpu.VMEM((HALF, rows, 2 * DH), f32),
+            pltpu.VMEM((HALF, 2 * DH, rows), f32),
             pltpu.VMEM((4, HALF, rows, 2 * DH), bf16),
             pltpu.VMEM((rows, 2 * DH), bf16),
-            pltpu.VMEM((HALF, rows, PER * rows), bf16),
-            pltpu.VMEM((HALF, rows, PER * rows), bf16),
-            pltpu.VMEM((HALF, 2, 1, PER * rows), f32),
-            pltpu.VMEM((HALF, 2, DH, PER * rows) if last else (8, DH), f32),
+            pltpu.VMEM((HALF, PER * rows, rows), bf16),
+            pltpu.VMEM((HALF, PER * rows, rows), bf16),
+            pltpu.VMEM((2, 1, PER * rows), f32),
+            pltpu.VMEM((2, 1, PER * rows), f32),
+            pltpu.VMEM((HALF, 2, PER * rows, DH) if last else (8, DH), f32),
             pltpu.SMEM((len(offsets),), jnp.int32),
             pltpu.SemaphoreType.DMA((2 * HALF,)),
             pltpu.SemaphoreType.DMA((len(offsets), HALF)),
@@ -412,7 +424,7 @@
             pltpu.SemaphoreType.DMA((2 * len(offsets), HALF)),
         ],
         compiler_params=pltpu.CompilerParams(vmem_limit_bytes=(13 << 20) + (len(offsets) << 19)),
-        cost_estimate=pl.CostEstimate(flops=8 << 30, bytes_accessed=16 << 20, transcendentals=0),
+        cost_estimate=pl.CostEstimate(flops=(1 if last else 8) << 30, bytes_accessed=1 << 20, transcendentals=0),
     )(plan, *arrays)
 
 

time: 130 us -> 125 us (0.962)
  starting transfers between devices: 54 us -> 44.1 us
  Pallas kernels: 44.5 us -> 51.8 us
  waiting for transfers between devices: 27.2 us -> 24.7 us
    ppermute x16, starting transfers between devices: 34.5 us -> 25.4 us  [shift(): return [lax.ppermute(array, 'leaf', ring) for array in arrays]]
    pallas_call x4, Pallas kernels: 25.2 us -> 30.6 us  [gradients(): pl.pallas_call(functools.partial(grads_kernel, chips, tuple(offsets), fir...]
    pallas_call x6, Pallas kernels: 8.78 us -> 12 us  [measure(): pl.pallas_call(functools.partial(measure_kernel, offsets), in_specs=[SMEM...]
    ppermute x6, waiting for transfers between devices: 7.92 us -> 6.14 us  [local(): lax.ppermute(up, 'leaf', right)]
    ppermute x16, waiting for transfers between devices: 14.6 us -> 13.2 us  [shift(): return [lax.ppermute(array, 'leaf', ring) for array in arrays]]
  transfers between devices with their start and end apart: 37 -> 37, of which waited for: 17 -> 13; matrix products, arithmetic and copies ran while one was open for 1% -> 1% of each run, Pallas kernels for 28% -> 35%
where the time goes in v4:
time: 125 us
  Pallas kernels  51.8 us (41%)
  starting transfers between devices  44.1 us (35%)
  waiting for transfers between devices  24.7 us (20%)
  local copies, waits for them, and re-layouts  1.58 us (1%)
  between operations  1.29 us (1%)
    pallas_call x4, Pallas kernels, gradients(): pl.pallas_call(functools.partial(grads_kernel, chips, tuple(offsets), fir...  30.6 us
    ppermute x16, starting transfers between devices, shift(): return [lax.ppermute(array, 'leaf', ring) for array in arrays]  25.4 us
    ppermute x16, waiting for transfers between devices, shift(): return [lax.ppermute(array, 'leaf', ring) for array in arrays]  13.2 us
    pallas_call x6, Pallas kernels, measure(): pl.pallas_call(functools.partial(measure_kernel, offsets), in_specs=[SMEM...  12 us
    ppermute x6, starting transfers between devices, local(): lax.ppermute(down, 'leaf', left)  11.6 us
    pallas_call x2, Pallas kernels, prepare(): pl.pallas_call(functools.partial(prepare_kernel, head), in_specs=[SMEM] *...  7.98 us
    ppermute x6, waiting for transfers between devices, local(): lax.ppermute(up, 'leaf', right)  6.14 us
    ppermute x2, starting transfers between devices, local(): lax.ppermute(down[rows:], 'leaf', left)  3.17 us
  transfers between devices with their start and end apart: 37, of which 13 were waited for; matrix products, arithmetic and copies ran while one was open for 1% of the time, Pallas kernels for 35%

profile of v4, /device:TPU:0, one launch (start us, length us, event | category | flops | bytes accessed | tf_op | source)
XLA Modules:
  0.0 124.5 jit_solution(1240125986021630392)
XLA Ops:
  4.6 2.7 %collective-permute-start.9 = (bf16[512,256]{1,0:T(8,128)(2,1)S(1)}, bf16[512,256]{1,0:T(8,128)(2,1)S(1)}, u32[]{:S(2)}, u32[]{:S(2)}) collective-permute-start(bf16[512,256]{1,0:T(8,128)(2,1)S(1)} %pad_maximum_fusion.3.block.refs_13_), channel_id=1, source_target_pairs={{4,0},{5,1},{8,4},{9,5},{12,8},{13,9},{14,12},{15,13},{10,14},{11,... | collective-permute-start | bytes 786440 | tf_op jit(solution)/shard_map/ppermute | solution.py:513
  7.4 2.0 %collective-permute-start.3 = (bf16[512,256]{1,0:T(8,128)(2,1)S(1)}, bf16[512,256]{1,0:T(8,128)(2,1)S(1)}, u32[]{:S(2)}, u32[]{:S(2)}) collective-permute-start(bf16[512,256]{1,0:T(8,128)(2,1)S(1)} %pad_maximum_fusion.2.block.refs_12_), channel_id=1, source_target_pairs={{4,0},{5,1},{8,4},{9,5},{12,8},{13,9},{14,12},{15,13},{10,14},{11,... | collective-permute-start | bytes 786440 | tf_op jit(solution)/shard_map/ppermute | solution.py:513
  9.5 4.0 %shard_map.116 = (s32[32]{0:T(128)S(1)}, bf16[2,128,1280]{2,1,0:T(8,128)(2,1)S(1)}, bf16[2,128,1280]{2,1,0:T(8,128)(2,1)S(1)}, bf16[2,1280,128]{2,1,0:T(8,128)(2...) custom-call(s32[1]{0:T(128)} %bitcast.me_ref, ...), custom_call_target="tpu_custom_call" | custom-call | bytes 12582912 | tf_op jit(solution)/shard_map/pallas_call | solution.py:163
  14.5 2.0 %collective-permute-done.8.refs_1_.refs_14_ = bf16[512,256]{1,0:T(8,128)(2,1)S(1)} collective-permute-done((bf16[512,256]{1,0:T(8,128)(2,1)S(1)}, bf16[512,256]{1,0:T(8,128)(2,1)S(1)}, u32[]{:S(2)}, u32[]{:S(2)}) %collective-permute-start.8) | collective-permute-done | bytes 262176 | tf_op jit(solution)/shard_map/ppermute | solution.py:513
  16.5 1.9 %collective-permute-start.11 = (bf16[512,256]{1,0:T(8,128)(2,1)S(1)}, bf16[512,256]{1,0:T(8,128)(2,1)S(1)}, u32[]{:S(2)}, u32[]{:S(2)}) collective-permute-start(bf16[512,256]{1,0:T(8,128)(2,1)S(1)} %collective-permute-done.9.refs_0_.refs_15_), channel_id=1, source_target_pairs={{4,0},{5,1},{8,4},{9,5},{12,8},{13,9},{14,12},{15,13},{10,14},{11,... | collective-permute-start | bytes 786440 | tf_op jit(solution)/shard_map/ppermute | solution.py:513
  18.5 4.0 %shard_map.112 = (s32[32]{0:T(128)S(1)}, bf16[2,128,1280]{2,1,0:T(8,128)(2,1)S(1)}, bf16[2,128,1280]{2,1,0:T(8,128)(2,1)S(1)}, bf16[2,1280,128]{2,1,0:T(8,128)(2...) custom-call(s32[1]{0:T(128)} %bitcast.me_ref, ...), custom_call_target="tpu_custom_call" | custom-call | bytes 12582912 | tf_op jit(solution)/shard_map/pallas_call | solution.py:163
  24.7 2.9 %shard_map.117 = (f32[2,1,1280]{2,1,0:T(1,128)S(1)}, f32[2,1,1280]{2,1,0:T(1,128)S(1)}) custom-call(s32[32]{0:T(128)S(1)} %get-tuple-element.124.plan, bf16[2,128,1280]{2,1,0:T(8,128)(2,1)S(1)} %get-tuple-element.119.qt_ref.refs_7_.refs_6_, f32[2,1,1280]{2,1,0:T(1,128)S(1)} %get-tuple-element.127.top_in, f32[2,1,1280]{2,1,0:T(1,128)S(1)} %get-tuple-element.128.sum_in, ...), custom_call_target="tpu_custom_call" | custom-call | bytes 8388608 | tf_op jit(solution)/shard_map/pallas_call | solution.py:199
  27.8 1.9 %collective-permute-start.13 = (bf16[512,256]{1,0:T(8,128)(2,1)S(1)}, bf16[512,256]{1,0:T(8,128)(2,1)S(1)}, u32[]{:S(2)}, u32[]{:S(2)}) collective-permute-start(bf16[512,256]{1,0:T(8,128)(2,1)S(1)} %collective-permute-done.11.refs_0_.refs_15_), channel_id=1, source_target_pairs={{4,0},{5,1},{8,4},{9,5},{12,8},{13,9},{14,12},{15,13},{10,14},{11,... | collective-permute-start | bytes 786440 | tf_op jit(solution)/shard_map/ppermute | solution.py:513
  29.7 2.9 %shard_map.113 = (f32[2,1,1280]{2,1,0:T(1,128)S(1)}, f32[2,1,1280]{2,1,0:T(1,128)S(1)}) custom-call(s32[32]{0:T(128)S(1)} %get-tuple-element.95.plan, bf16[2,128,1280]{2,1,0:T(8,128)(2,1)S(1)} %get-tuple-element.96.qt_ref.refs_0_, f32[2,1,1280]{2,1,0:T(1,128)S(1)} %get-tuple-element.103.top_in, f32[2,1,1280]{2,1,0:T(1,128)S(1)} %get-tuple-element.104.sum_in, ...), custom_call_target="tpu_custom_call" | custom-call | bytes 8388608 | tf_op jit(solution)/shard_map/pallas_call | solution.py:199
  41.1 3.4 %collective-permute-done.6.refs_1_.refs_16_ = bf16[512,256]{1,0:T(8,128)(2,1)S(1)} collective-permute-done((bf16[512,256]{1,0:T(8,128)(2,1)S(1)}, bf16[512,256]{1,0:T(8,128)(2,1)S(1)}, u32[]{:S(2)}, u32[]{:S(2)}) %collective-permute-start.6) | collective-permute-done | bytes 262176 | tf_op jit(solution)/shard_map/ppermute | solution.py:513
  51.2 7.4 %shard_map.120 = (bf16[3,512,256]{2,1,0:T(8,128)(2,1)S(1)}, bf16[3,512,256]{2,1,0:T(8,128)(2,1)S(1)}, bf16[256,256]{1,0:T(8,128)(2,1)S(1)}, bf16[256,256]{1,0:T(...) custom-call(s32[32]{0:T(128)S(1)} %get-tuple-element.95.plan, ...), custom_call_target="tpu_custom_call" | custom-call | flops 8589934592 | bytes 1048576 | tf_op jit(solution)/shard_map/pallas_call | solution.py:405
  60.6 4.2 %collective-permute-start.25 = (bf16[256,256]{1,0:T(8,128)(2,1)S(1)}, bf16[256,256]{1,0:T(8,128)(2,1)S(1)}, u32[]{:S(2)}, u32[]{:S(2)}) collective-permute-start(bf16[256,256]{1,0:T(8,128)(2,1)S(1)} %get-tuple-element.173), channel_id=1, source_target_pairs={{0,4},{1,5},{4,8},{5,9},{8,12},{9,13},{12,14},{13,15},{14,10},{15,... | collective-permute-start | bytes 393224 | tf_op jit(solution)/shard_map/ppermute | solution.py:503
  64.8 3.0 %collective-permute-done.19 = bf16[256,256]{1,0:T(8,128)(2,1)S(1)} collective-permute-done((bf16[256,256]{1,0:T(8,128)(2,1)S(1)}, bf16[256,256]{1,0:T(8,128)(2,1)S(1)}, u32[]{:S(2)}, u32[]{:S(2)}) %collective-permute-start.19) | collective-permute-done | bytes 131104 | tf_op jit(solution)/shard_map/ppermute | solution.py:503
  67.8 2.2 %collective-permute-done.29 = bf16[256,256]{1,0:T(8,128)(2,1)S(1)} collective-permute-done((bf16[256,256]{1,0:T(8,128)(2,1)S(1)}, bf16[256,256]{1,0:T(8,128)(2,1)S(1)}, u32[]{:S(2)}, u32[]{:S(2)}) %collective-permute-start.29) | collective-permute-done | bytes 131104 | tf_op jit(solution)/shard_map/ppermute | solution.py:503
  70.1 6.8 %collective-permute-start.26 = (bf16[512,256]{1,0:T(8,128)(2,1)S(1)}, bf16[512,256]{1,0:T(8,128)(2,1)S(1)}, u32[]{:S(2)}, u32[]{:S(2)}) collective-permute-start(bf16[512,256]{1,0:T(8,128)(2,1)S(1)} %get-tuple-element.181), channel_id=1, source_target_pairs={{0,4},{1,5},{4,8},{5,9},{8,12},{9,13},{12,14},{13,15},{14,10},{15,... | collective-permute-start | bytes 786440 | tf_op jit(solution)/shard_map/ppermute | solution.py:503
  76.9 2.0 %collective-permute-start.20 = (bf16[512,256]{1,0:T(8,128)(2,1)S(1)}, bf16[512,256]{1,0:T(8,128)(2,1)S(1)}, u32[]{:S(2)}, u32[]{:S(2)}) collective-permute-start(bf16[512,256]{1,0:T(8,128)(2,1)S(1)} %get-tuple-element.157), channel_id=1, source_target_pairs={{0,4},{1,5},{4,8},{5,9},{8,12},{9,13},{12,14},{13,15},{14,10},{15,... | collective-permute-start | bytes 786440 | tf_op jit(solution)/shard_map/ppermute | solution.py:503
  78.9 6.8 %shard_map.121 = (bf16[2,512,256]{2,1,0:T(8,128)(2,1)S(1)}, bf16[2,512,256]{2,1,0:T(8,128)(2,1)S(1)}, f32[2,2,1280,128]{3,2,1,0:T(8,128)S(1)}) custom-call(s32[32]{0:T(128)S(1)} %get-tuple-element.95.plan, bf16[2,128,1280]{2,1,0:T(8,128)(2,1)S(1)} %get-tuple-element.96.qt_ref.refs_0_, bf16[2,128,1280]{2,1,0:T(8,128)(2,1)S(1)} %get-tuple-element.97.refs_1_, ...), custom_call_target="tpu_custom_call" | custom-call | flops 8589934592 | bytes 1048576 | tf_op jit(solution)/shard_map/pallas_call | solution.py:405
  85.8 3.3 %collective-permute-start.27 = (bf16[512,256]{1,0:T(8,128)(2,1)S(1)}, bf16[512,256]{1,0:T(8,128)(2,1)S(1)}, u32[]{:S(2)}, u32[]{:S(2)}) collective-permute-start(bf16[512,256]{1,0:T(8,128)(2,1)S(1)} %get-tuple-element.187), channel_id=1, source_target_pairs={{0,4},{1,5},{4,8},{5,9},{8,12},{9,13},{12,14},{13,15},{14,10},{15,... | collective-permute-start | bytes 786440 | tf_op jit(solution)/shard_map/ppermute | solution.py:503
  89.2 2.8 %collective-permute-start.22 = (bf16[512,256]{1,0:T(8,128)(2,1)S(1)}, bf16[512,256]{1,0:T(8,128)(2,1)S(1)}, u32[]{:S(2)}, u32[]{:S(2)}) collective-permute-start(bf16[512,256]{1,0:T(8,128)(2,1)S(1)} %get-tuple-element.164), channel_id=1, source_target_pairs={{0,4},{1,5},{4,8},{5,9},{8,12},{9,13},{12,14},{13,15},{14,10},{15,... | collective-permute-start | bytes 786440 | tf_op jit(solution)/shard_map/ppermute | solution.py:503
  92.1 10.4 %shard_map.122 = (bf16[2,512,256]{2,1,0:T(8,128)(2,1)S(1)}, bf16[2,512,256]{2,1,0:T(8,128)(2,1)S(1)}, f32[2,2,1280,128]{3,2,1,0:T(8,128)S(1)}) custom-call(s32[32]{0:T(128)S(1)} %get-tuple-element.95.plan, bf16[2,128,1280]{2,1,0:T(8,128)(2,1)S(1)} %get-tuple-element.96.qt_ref.refs_0_, bf16[2,128,1280]{2,1,0:T(8,128)(2,1)S(1)} %get-tuple-element.97.refs_1_, ...), custom_call_target="tpu_custom_call" | custom-call | flops 8589934592 | bytes 1048576 | tf_op jit(solution)/shard_map/pallas_call | solution.py:405
  102.7 2.0 %collective-permute-start.32 = (bf16[512,256]{1,0:T(8,128)(2,1)S(1)}, bf16[512,256]{1,0:T(8,128)(2,1)S(1)}, u32[]{:S(2)}, u32[]{:S(2)}) collective-permute-start(bf16[512,256]{1,0:T(8,128)(2,1)S(1)} %get-tuple-element.186), channel_id=1, source_target_pairs={{4,0},{5,1},{8,4},{9,5},{12,8},{13,9},{14,12},{15,13},{10,14},{11,... | collective-permute-start | bytes 786440 | tf_op jit(solution)/shard_map/ppermute | solution.py:503
  104.9 6.1 %shard_map.123 = (bf16[1,512,256]{2,1,0:T(8,128)(2,1)S(1)}, bf16[1,512,256]{2,1,0:T(8,128)(2,1)S(1)}, bf16[256,1280]{1,0:T(8,128)(2,1)S(1)}, bf16[256,1280]{1,0:T(8,128)(2,1)S(1)}) custom-call(s32[32]{0:T(128)S(1)} %get-tuple-element.95.plan, bf16[2,128,1280]{2,1,0:T(8,128)(2,1)S(1)} %get-tuple-element.96.qt_ref.refs_0_, ...), custom_call_target="tpu_custom_call" | custom-call | flops 1073741824 | bytes 1048576 | tf_op jit(solution)/shard_map/pallas_call | solution.py:405
  111.0 2.1 %collective-permute-start.33 = (bf16[512,256]{1,0:T(8,128)(2,1)S(1)}, bf16[512,256]{1,0:T(8,128)(2,1)S(1)}, u32[]{:S(2)}, u32[]{:S(2)}) collective-permute-start(bf16[512,256]{1,0:T(8,128)(2,1)S(1)} %get-tuple-element.179), channel_id=1, source_target_pairs={{0,4},{1,5},{4,8},{5,9},{8,12},{9,13},{12,14},{13,15},{14,10},{15,... | collective-permute-start | bytes 786440 | tf_op jit(solution)/shard_map/ppermute | solution.py:503
  113.5 6.3 %collective-permute-done.33 = bf16[512,256]{1,0:T(8,128)(2,1)S(1)} collective-permute-done((bf16[512,256]{1,0:T(8,128)(2,1)S(1)}, bf16[512,256]{1,0:T(8,128)(2,1)S(1)}, u32[]{:S(2)}, u32[]{:S(2)}) %collective-permute-start.33) | collective-permute-done | bytes 262176 | tf_op jit(solution)/shard_map/ppermute | solution.py:503
  (100 shorter events, 30.4 us)
Async XLA Ops:
  4.6 9.9 %collective-permute-start.9 = (bf16[512,256]{1,0:T(8,128)(2,1)S(1)}, bf16[512,256]{1,0:T(8,128)(2,1)S(1)}, u32[]{:S(2)}, u32[]{:S(2)}) collective-permute-start(bf16[512,256]{1,0:T(8,128)(2,1)S(1)} %pad_maximum_fusion.3.block.refs_13_), channel_id=1, source_target_pairs={{4,0},{5,1},{8,4},{9,5},{12,8},{13,9},{14,12},{15,13},{10,14},{11,... | collective-permute-start | bytes 786440 | tf_op jit(solution)/shard_map/ppermute | solution.py:513
  7.3 9.2 %collective-permute-start.8 = (bf16[512,256]{1,0:T(8,128)(2,1)S(1)}, bf16[512,256]{1,0:T(8,128)(2,1)S(1)}, u32[]{:S(2)}, u32[]{:S(2)}) collective-permute-start(bf16[512,256]{1,0:T(8,128)(2,1)S(1)} %pad_maximum_fusion.3.block.refs_13_), channel_id=1, source_target_pairs={{0,4},{1,5},{4,8},{5,9},{8,12},{9,13},{12,14},{13,15},{14,10},{15,... | collective-permute-start | bytes 786440 | tf_op jit(solution)/shard_map/ppermute | solution.py:513
  7.4 15.0 %collective-permute-start.3 = (bf16[512,256]{1,0:T(8,128)(2,1)S(1)}, bf16[512,256]{1,0:T(8,128)(2,1)S(1)}, u32[]{:S(2)}, u32[]{:S(2)}) collective-permute-start(bf16[512,256]{1,0:T(8,128)(2,1)S(1)} %pad_maximum_fusion.2.block.refs_12_), channel_id=1, source_target_pairs={{4,0},{5,1},{8,4},{9,5},{12,8},{13,9},{14,12},{15,13},{10,14},{11,... | collective-permute-start | bytes 786440 | tf_op jit(solution)/shard_map/ppermute | solution.py:513
  9.4 13.1 %collective-permute-start.2 = (bf16[512,256]{1,0:T(8,128)(2,1)S(1)}, bf16[512,256]{1,0:T(8,128)(2,1)S(1)}, u32[]{:S(2)}, u32[]{:S(2)}) collective-permute-start(bf16[512,256]{1,0:T(8,128)(2,1)S(1)} %pad_maximum_fusion.2.block.refs_12_), channel_id=1, source_target_pairs={{0,4},{1,5},{4,8},{5,9},{8,12},{9,13},{12,14},{13,15},{14,10},{15,... | collective-permute-start | bytes 786440 | tf_op jit(solution)/shard_map/ppermute | solution.py:513
  16.4 11.2 %collective-permute-start.10 = (bf16[512,256]{1,0:T(8,128)(2,1)S(1)}, bf16[512,256]{1,0:T(8,128)(2,1)S(1)}, u32[]{:S(2)}, u32[]{:S(2)}) collective-permute-start(bf16[512,256]{1,0:T(8,128)(2,1)S(1)} %collective-permute-done.8.refs_1_.refs_14_), channel_id=1, source_target_pairs={{0,4},{1,5},{4,8},{5,9},{8,12},{9,13},{12,14},{13,15},{14,10},{15,... | collective-permute-start | bytes 786440 | tf_op jit(solution)/shard_map/ppermute | solution.py:513
  16.5 11.2 %collective-permute-start.11 = (bf16[512,256]{1,0:T(8,128)(2,1)S(1)}, bf16[512,256]{1,0:T(8,128)(2,1)S(1)}, u32[]{:S(2)}, u32[]{:S(2)}) collective-permute-start(bf16[512,256]{1,0:T(8,128)(2,1)S(1)} %collective-permute-done.9.refs_0_.refs_15_), channel_id=1, source_target_pairs={{4,0},{5,1},{8,4},{9,5},{12,8},{13,9},{14,12},{15,13},{10,14},{11,... | collective-permute-start | bytes 786440 | tf_op jit(solution)/shard_map/ppermute | solution.py:513
  22.5 10.8 %collective-permute-start.4 = (bf16[512,256]{1,0:T(8,128)(2,1)S(1)}, bf16[512,256]{1,0:T(8,128)(2,1)S(1)}, u32[]{:S(2)}, u32[]{:S(2)}) collective-permute-start(bf16[512,256]{1,0:T(8,128)(2,1)S(1)} %collective-permute-done.2.refs_1_.refs_12_), channel_id=1, source_target_pairs={{0,4},{1,5},{4,8},{5,9},{8,12},{9,13},{12,14},{13,15},{14,10},{15,... | collective-permute-start | bytes 786440 | tf_op jit(solution)/shard_map/ppermute | solution.py:513
  23.2 10.1 %collective-permute-start.5 = (bf16[512,256]{1,0:T(8,128)(2,1)S(1)}, bf16[512,256]{1,0:T(8,128)(2,1)S(1)}, u32[]{:S(2)}, u32[]{:S(2)}) collective-permute-start(bf16[512,256]{1,0:T(8,128)(2,1)S(1)} %collective-permute-done.3.refs_0_.refs_13_), channel_id=1, source_target_pairs={{4,0},{5,1},{8,4},{9,5},{12,8},{13,9},{14,12},{15,13},{10,14},{11,... | collective-permute-start | bytes 786440 | tf_op jit(solution)/shard_map/ppermute | solution.py:513
  27.7 11.3 %collective-permute-start.12 = (bf16[512,256]{1,0:T(8,128)(2,1)S(1)}, bf16[512,256]{1,0:T(8,128)(2,1)S(1)}, u32[]{:S(2)}, u32[]{:S(2)}) collective-permute-start(bf16[512,256]{1,0:T(8,128)(2,1)S(1)} %collective-permute-done.10.refs_1_.refs_14_), channel_id=1, source_target_pairs={{0,4},{1,5},{4,8},{5,9},{8,12},{9,13},{12,14},{13,15},{14,10},{15,... | collective-permute-start | bytes 786440 | tf_op jit(solution)/shard_map/ppermute | solution.py:513
  27.8 11.2 %collective-permute-start.13 = (bf16[512,256]{1,0:T(8,128)(2,1)S(1)}, bf16[512,256]{1,0:T(8,128)(2,1)S(1)}, u32[]{:S(2)}, u32[]{:S(2)}) collective-permute-start(bf16[512,256]{1,0:T(8,128)(2,1)S(1)} %collective-permute-done.11.refs_0_.refs_15_), channel_id=1, source_target_pairs={{4,0},{5,1},{8,4},{9,5},{12,8},{13,9},{14,12},{15,13},{10,14},{11,... | collective-permute-start | bytes 786440 | tf_op jit(solution)/shard_map/ppermute | solution.py:513
  33.3 11.2 %collective-permute-start.6 = (bf16[512,256]{1,0:T(8,128)(2,1)S(1)}, bf16[512,256]{1,0:T(8,128)(2,1)S(1)}, u32[]{:S(2)}, u32[]{:S(2)}) collective-permute-start(bf16[512,256]{1,0:T(8,128)(2,1)S(1)} %collective-permute-done.4.refs_1_.refs_12_), channel_id=1, source_target_pairs={{0,4},{1,5},{4,8},{5,9},{8,12},{9,13},{12,14},{13,15},{14,10},{15,... | collective-permute-start | bytes 786440 | tf_op jit(solution)/shard_map/ppermute | solution.py:513
  33.9 10.7 %collective-permute-start.7 = (bf16[512,256]{1,0:T(8,128)(2,1)S(1)}, bf16[512,256]{1,0:T(8,128)(2,1)S(1)}, u32[]{:S(2)}, u32[]{:S(2)}) collective-permute-start(bf16[512,256]{1,0:T(8,128)(2,1)S(1)} %collective-permute-done.5.refs_0_.refs_13_), channel_id=1, source_target_pairs={{4,0},{5,1},{8,4},{9,5},{12,8},{13,9},{14,12},{15,13},{10,14},{11,... | collective-permute-start | bytes 786440 | tf_op jit(solution)/shard_map/ppermute | solution.py:513
  39.0 10.2 %collective-permute-start.17 = (bf16[256,256]{1,0:T(8,128)(2,1)S(1)}, bf16[256,256]{1,0:T(8,128)(2,1)S(1)}, u32[]{:S(2)}, u32[]{:S(2)}) collective-permute-start(bf16[256,256]{1,0:T(8,128)(2,1)S(1)} %slice.69), channel_id=1, source_target_pairs={{4,0},{5,1},{8,4},{9,5},{12,8},{13,9},{14,12},{15,13},{10,14},{11,... | collective-permute-start | bytes 393224 | tf_op jit(solution)/shard_map/ppermute | solution.py:524
  70.1 15.6 %collective-permute-start.26 = (bf16[512,256]{1,0:T(8,128)(2,1)S(1)}, bf16[512,256]{1,0:T(8,128)(2,1)S(1)}, u32[]{:S(2)}, u32[]{:S(2)}) collective-permute-start(bf16[512,256]{1,0:T(8,128)(2,1)S(1)} %get-tuple-element.181), channel_id=1, source_target_pairs={{0,4},{1,5},{4,8},{5,9},{8,12},{9,13},{12,14},{13,15},{14,10},{15,... | collective-permute-start | bytes 786440 | tf_op jit(solution)/shard_map/ppermute | solution.py:503
  76.9 8.8 %collective-permute-start.30 = (bf16[512,256]{1,0:T(8,128)(2,1)S(1)}, bf16[512,256]{1,0:T(8,128)(2,1)S(1)}, u32[]{:S(2)}, u32[]{:S(2)}) collective-permute-start(bf16[512,256]{1,0:T(8,128)(2,1)S(1)} %get-tuple-element.182), channel_id=1, source_target_pairs={{4,0},{5,1},{8,4},{9,5},{12,8},{13,9},{14,12},{15,13},{10,14},{11,... | collective-permute-start | bytes 786440 | tf_op jit(solution)/shard_map/ppermute | solution.py:503
  76.9 12.2 %collective-permute-start.20 = (bf16[512,256]{1,0:T(8,128)(2,1)S(1)}, bf16[512,256]{1,0:T(8,128)(2,1)S(1)}, u32[]{:S(2)}, u32[]{:S(2)}) collective-permute-start(bf16[512,256]{1,0:T(8,128)(2,1)S(1)} %get-tuple-element.157), channel_id=1, source_target_pairs={{0,4},{1,5},{4,8},{5,9},{8,12},{9,13},{12,14},{13,15},{14,10},{15,... | collective-permute-start | bytes 786440 | tf_op jit(solution)/shard_map/ppermute | solution.py:503
  78.9 10.2 %collective-permute-start.21 = (bf16[512,256]{1,0:T(8,128)(2,1)S(1)}, bf16[512,256]{1,0:T(8,128)(2,1)S(1)}, u32[]{:S(2)}, u32[]{:S(2)}) collective-permute-start(bf16[512,256]{1,0:T(8,128)(2,1)S(1)} %get-tuple-element.159), channel_id=1, source_target_pairs={{4,0},{5,1},{8,4},{9,5},{12,8},{13,9},{14,12},{15,13},{10,14},{11,... | collective-permute-start | bytes 786440 | tf_op jit(solution)/shard_map/ppermute | solution.py:503
  85.8 16.6 %collective-permute-start.27 = (bf16[512,256]{1,0:T(8,128)(2,1)S(1)}, bf16[512,256]{1,0:T(8,128)(2,1)S(1)}, u32[]{:S(2)}, u32[]{:S(2)}) collective-permute-start(bf16[512,256]{1,0:T(8,128)(2,1)S(1)} %get-tuple-element.187), channel_id=1, source_target_pairs={{0,4},{1,5},{4,8},{5,9},{8,12},{9,13},{12,14},{13,15},{14,10},{15,... | collective-permute-start | bytes 786440 | tf_op jit(solution)/shard_map/ppermute | solution.py:503
  89.1 13.4 %collective-permute-start.31 = (bf16[512,256]{1,0:T(8,128)(2,1)S(1)}, bf16[512,256]{1,0:T(8,128)(2,1)S(1)}, u32[]{:S(2)}, u32[]{:S(2)}) collective-permute-start(bf16[512,256]{1,0:T(8,128)(2,1)S(1)} %get-tuple-element.188), channel_id=1, source_target_pairs={{4,0},{5,1},{8,4},{9,5},{12,8},{13,9},{14,12},{15,13},{10,14},{11,... | collective-permute-start | bytes 786440 | tf_op jit(solution)/shard_map/ppermute | solution.py:503
  89.2 15.5 %collective-permute-start.22 = (bf16[512,256]{1,0:T(8,128)(2,1)S(1)}, bf16[512,256]{1,0:T(8,128)(2,1)S(1)}, u32[]{:S(2)}, u32[]{:S(2)}) collective-permute-start(bf16[512,256]{1,0:T(8,128)(2,1)S(1)} %get-tuple-element.164), channel_id=1, source_target_pairs={{0,4},{1,5},{4,8},{5,9},{8,12},{9,13},{12,14},{13,15},{14,10},{15,... | collective-permute-start | bytes 786440 | tf_op jit(solution)/shard_map/ppermute | solution.py:503
  92.1 12.6 %collective-permute-start.23 = (bf16[512,256]{1,0:T(8,128)(2,1)S(1)}, bf16[512,256]{1,0:T(8,128)(2,1)S(1)}, u32[]{:S(2)}, u32[]{:S(2)}) collective-permute-start(bf16[512,256]{1,0:T(8,128)(2,1)S(1)} %get-tuple-element.166), channel_id=1, source_target_pairs={{4,0},{5,1},{8,4},{9,5},{12,8},{13,9},{14,12},{15,13},{10,14},{11,... | collective-permute-start | bytes 786440 | tf_op jit(solution)/shard_map/ppermute | solution.py:503
  102.7 10.5 %collective-permute-start.28 = (bf16[512,256]{1,0:T(8,128)(2,1)S(1)}, bf16[512,256]{1,0:T(8,128)(2,1)S(1)}, u32[]{:S(2)}, u32[]{:S(2)}) collective-permute-start(bf16[512,256]{1,0:T(8,128)(2,1)S(1)} %get-tuple-element.185), channel_id=1, source_target_pairs={{0,4},{1,5},{4,8},{5,9},{8,12},{9,13},{12,14},{13,15},{14,10},{15,... | collective-permute-start | bytes 786440 | tf_op jit(solution)/shard_map/ppermute | solution.py:503
  102.7 10.4 %collective-permute-start.32 = (bf16[512,256]{1,0:T(8,128)(2,1)S(1)}, bf16[512,256]{1,0:T(8,128)(2,1)S(1)}, u32[]{:S(2)}, u32[]{:S(2)}) collective-permute-start(bf16[512,256]{1,0:T(8,128)(2,1)S(1)} %get-tuple-element.186), channel_id=1, source_target_pairs={{4,0},{5,1},{8,4},{9,5},{12,8},{13,9},{14,12},{15,13},{10,14},{11,... | collective-permute-start | bytes 786440 | tf_op jit(solution)/shard_map/ppermute | solution.py:503
  110.9 12.1 %collective-permute-start.24 = (bf16[256,1280]{1,0:T(8,128)(2,1)S(1)}, bf16[256,1280]{1,0:T(8,128)(2,1)S(1)}, u32[]{:S(2)}, u32[]{:S(2)}) collective-permute-start(bf16[256,1280]{1,0:T(8,128)(2,1)S(1)} %get-tuple-element.171), channel_id=1, source_target_pairs={{0,1},{1,0},{2,3},{3,2},{4,5},{5,4},{6,7},{7,6},{8,9},{9,8},{10,11... | collective-permute-start | bytes 1966088 | tf_op jit(solution)/shard_map/ppermute | solution.py:554
  (20 other events, 110.1 us)

commit v5 on v3

--- a/solution.py
+++ b/solution.py
@@ -300,12 +300,13 @@
         at_block, half = i // 2, i % 2
         here = pl.ds(pl.multiple_of(half * rows, rows), rows)
 
-        @pl.when((half == 0) & (offset_ref[at_block] != far))
-        def _():
-            for head in range(HALF):
-                pltpu.make_async_copy(
-                    blocks[head][-1], kv_ref.at[at_block, head], kv_sems.at[at_block, head]
-                ).wait()
+        if len(offsets) > first:
+            @pl.when((half == 0) & (offset_ref[at_block] != far))
+            def _():
+                for head in range(HALF):
+                    pltpu.make_async_copy(
+                        blocks[head][-1], kv_ref.at[at_block, head], kv_sems.at[at_block, head]
+                    ).wait()
 
         def look(side, carry):
             @pl.when(sees(side, i) > 0)
@@ -371,7 +372,7 @@
 def gradients(prepared, stats, offsets, blocks, carried, last):
     plan = prepared[0][0]
     chips = plan.shape[0] // 4
-    rows = blocks[0][-1].shape[0] // 2
+    rows = prepared[0][3].shape[1] // PER
     first = carried is None
     bf16, f32 = jnp.bfloat16, jnp.float32
     shared = [(*prepared[head][1:6], *stats[head]) for head in range(HALF)]
@@ -514,22 +515,22 @@
         stats[head] = measure(met, prepared[head], stats[head], [blocks[head][at] for at in met])
 
     offsets = [far]
-    for step in range(1, far - 2):
+    for step in range(1, far - 3):
         offsets += [far + step, far - step]
     arrays = [halves[head] + [blocks[head][at] for at in offsets[1:]] for head in range(HALF)]
     *terms, carried = gradients(prepared, stats, offsets, arrays, None, False)
     lse = [[a] for a in terms[3 * HALF:]]
     by_offset = {at: [terms[head][slot] for head in range(HALF)] for slot, at in enumerate(offsets)}
-    ups = [jnp.pad(wide(a), ((0, rows), (0, 0))) for a in shift(terms[HALF:2 * HALF], right)]
-    downs = [jnp.pad(wide(a), ((rows, 0), (0, 0))) for a in shift(terms[2 * HALF:3 * HALF], left)]
+    ups, downs = terms[HALF:2 * HALF], terms[2 * HALF:3 * HALF]
 
     def add(sums, at):
         return [(a + wide(b)).astype(jnp.bfloat16) for a, b in zip(sums, by_offset[at])]
 
-    later = {3: [chips - 2, 2], 2: [chips - 1, 1], 1: [0]}
+    later = {4: [chips - 3, 3], 3: [chips - 2, 2], 2: [chips - 1, 1], 1: [0]}
     ours = theirs = None
-    for step in range(far - 1, 0, -1):
-        ups, downs = add(ups, step), add(downs, chips - step)
+    for step in range(far, 0, -1):
+        if step < far:
+            ups, downs = add(ups, step), add(downs, chips - step)
         if step in later:
             last = 0 in later[step]
             (lse, carried), held = lax.optimization_barrier(((lse, carried), (ups[1:], downs[1:])))
@@ -544,6 +545,9 @@
                 carried = lead
         ups = [wide(a) for a in shift(ups, right)]
         downs = [wide(a) for a in shift(downs, left)]
+        if step == far:
+            ups = [jnp.pad(a, ((0, rows), (0, 0))) for a in ups]
+            downs = [jnp.pad(a, ((rows, 0), (0, 0))) for a in downs]
     kept, got = [], []
     for head in range(HALF):
         summed = (wide(by_offset[0][head]) + ups[head] + downs[head]).astype(jnp.bfloat16)

time: 130 us -> 120 us (0.923)
  starting transfers between devices: 54 us -> 43.5 us
    ppermute x16, starting transfers between devices: 34.5 us -> 24.7 us  [shift(): return [lax.ppermute(array, 'leaf', ring) for array in arrays]]
    ppermute x6, waiting for transfers between devices: 7.92 us -> 11.2 us  [local(): lax.ppermute(up, 'leaf', right)]
    pallas_call x4 -> x5, Pallas kernels: 25.2 us -> 28.1 us  [gradients(): pl.pallas_call(functools.partial(grads_kernel, chips, tuple(offsets), fir...]
    ppermute x16, waiting for transfers between devices: 14.6 us -> 12.3 us  [shift(): return [lax.ppermute(array, 'leaf', ring) for array in arrays]]
  transfers between devices with their start and end apart: 37 -> 37, of which waited for: 17 -> 13; matrix products, arithmetic and copies ran while one was open for 1% -> 1% of each run, Pallas kernels for 28% -> 30%
where the time goes in v5:
time: 120 us
  Pallas kernels  45.2 us (38%)
  starting transfers between devices  43.5 us (36%)
  waiting for transfers between devices  27.6 us (23%)
  local copies, waits for them, and re-layouts  1.58 us (1%)
  between operations  1.29 us (1%)
    pallas_call x5, Pallas kernels, gradients(): pl.pallas_call(functools.partial(grads_kernel, chips, tuple(offsets), fir...  28.1 us
    ppermute x16, starting transfers between devices, shift(): return [lax.ppermute(array, 'leaf', ring) for array in arrays]  24.7 us
    ppermute x16, waiting for transfers between devices, shift(): return [lax.ppermute(array, 'leaf', ring) for array in arrays]  12.3 us
    ppermute x6, starting transfers between devices, local(): lax.ppermute(down, 'leaf', left)  11.3 us
    ppermute x6, waiting for transfers between devices, local(): lax.ppermute(up, 'leaf', right)  11.2 us
    pallas_call x2, Pallas kernels, prepare(): pl.pallas_call(functools.partial(prepare_kernel, head), in_specs=[SMEM] *...  8.16 us
    pallas_call x6, Pallas kernels, measure(): pl.pallas_call(functools.partial(measure_kernel, offsets), in_specs=[SMEM...  7.71 us
    ppermute x2, starting transfers between devices, local(): lax.ppermute(down[rows:], 'leaf', left)  3.34 us
  transfers between devices with their start and end apart: 37, of which 13 were waited for; matrix products, arithmetic and copies ran while one was open for 1% of the time, Pallas kernels for 30%

profile of v5, /device:TPU:0, one launch (start us, length us, event | category | flops | bytes accessed | tf_op | source)
XLA Modules:
  0.0 120.4 jit_solution(3657560327391839691)
XLA Ops:
  4.6 2.7 %collective-permute-start.9 = (bf16[512,256]{1,0:T(8,128)(2,1)S(1)}, bf16[512,256]{1,0:T(8,128)(2,1)S(1)}, u32[]{:S(2)}, u32[]{:S(2)}) collective-permute-start(bf16[512,256]{1,0:T(8,128)(2,1)S(1)} %pad_maximum_fusion.3.block.refs_13_), channel_id=1, source_target_pairs={{4,0},{5,1},{8,4},{9,5},{12,8},{13,9},{14,12},{15,13},{10,14},{11,... | collective-permute-start | bytes 786440 | tf_op jit(solution)/shard_map/ppermute | solution.py:502
  7.4 2.0 %collective-permute-start.3 = (bf16[512,256]{1,0:T(8,128)(2,1)S(1)}, bf16[512,256]{1,0:T(8,128)(2,1)S(1)}, u32[]{:S(2)}, u32[]{:S(2)}) collective-permute-start(bf16[512,256]{1,0:T(8,128)(2,1)S(1)} %pad_maximum_fusion.2.block.refs_12_), channel_id=1, source_target_pairs={{4,0},{5,1},{8,4},{9,5},{12,8},{13,9},{14,12},{15,13},{10,14},{11,... | collective-permute-start | bytes 786440 | tf_op jit(solution)/shard_map/ppermute | solution.py:502
  9.5 4.1 %shard_map.116 = (s32[32]{0:T(128)S(1)}, bf16[2,128,1280]{2,1,0:T(8,128)(2,1)S(1)}, bf16[2,128,1280]{2,1,0:T(8,128)(2,1)S(1)}, bf16[2,1280,128]{2,1,0:T(8,128)(2...) custom-call(s32[1]{0:T(128)} %bitcast.me_ref, ...), custom_call_target="tpu_custom_call" | custom-call | bytes 12582912 | tf_op jit(solution)/shard_map/pallas_call | solution.py:157
  14.5 2.0 %collective-permute-done.8.refs_1_.refs_14_ = bf16[512,256]{1,0:T(8,128)(2,1)S(1)} collective-permute-done((bf16[512,256]{1,0:T(8,128)(2,1)S(1)}, bf16[512,256]{1,0:T(8,128)(2,1)S(1)}, u32[]{:S(2)}, u32[]{:S(2)}) %collective-permute-start.8) | collective-permute-done | bytes 262176 | tf_op jit(solution)/shard_map/ppermute | solution.py:502
  16.5 1.9 %collective-permute-start.11 = (bf16[512,256]{1,0:T(8,128)(2,1)S(1)}, bf16[512,256]{1,0:T(8,128)(2,1)S(1)}, u32[]{:S(2)}, u32[]{:S(2)}) collective-permute-start(bf16[512,256]{1,0:T(8,128)(2,1)S(1)} %collective-permute-done.9.refs_0_.refs_15_), channel_id=1, source_target_pairs={{4,0},{5,1},{8,4},{9,5},{12,8},{13,9},{14,12},{15,13},{10,14},{11,... | collective-permute-start | bytes 786440 | tf_op jit(solution)/shard_map/ppermute | solution.py:502
  18.5 4.1 %shard_map.112 = (s32[32]{0:T(128)S(1)}, bf16[2,128,1280]{2,1,0:T(8,128)(2,1)S(1)}, bf16[2,128,1280]{2,1,0:T(8,128)(2,1)S(1)}, bf16[2,1280,128]{2,1,0:T(8,128)(2...) custom-call(s32[1]{0:T(128)} %bitcast.me_ref, ...), custom_call_target="tpu_custom_call" | custom-call | bytes 12582912 | tf_op jit(solution)/shard_map/pallas_call | solution.py:157
  22.7 1.9 %collective-permute-start.5 = (bf16[512,256]{1,0:T(8,128)(2,1)S(1)}, bf16[512,256]{1,0:T(8,128)(2,1)S(1)}, u32[]{:S(2)}, u32[]{:S(2)}) collective-permute-start(bf16[512,256]{1,0:T(8,128)(2,1)S(1)} %collective-permute-done.3.refs_0_.refs_13_), channel_id=1, source_target_pairs={{4,0},{5,1},{8,4},{9,5},{12,8},{13,9},{14,12},{15,13},{10,14},{11,... | collective-permute-start | bytes 786440 | tf_op jit(solution)/shard_map/ppermute | solution.py:502
  25.4 2.3 %collective-permute-done.10.refs_1_.refs_14_ = bf16[512,256]{1,0:T(8,128)(2,1)S(1)} collective-permute-done((bf16[512,256]{1,0:T(8,128)(2,1)S(1)}, bf16[512,256]{1,0:T(8,128)(2,1)S(1)}, u32[]{:S(2)}, u32[]{:S(2)}) %collective-permute-start.10) | collective-permute-done | bytes 262176 | tf_op jit(solution)/shard_map/ppermute | solution.py:502
  27.8 1.9 %collective-permute-start.13 = (bf16[512,256]{1,0:T(8,128)(2,1)S(1)}, bf16[512,256]{1,0:T(8,128)(2,1)S(1)}, u32[]{:S(2)}, u32[]{:S(2)}) collective-permute-start(bf16[512,256]{1,0:T(8,128)(2,1)S(1)} %collective-permute-done.11.refs_0_.refs_15_), channel_id=1, source_target_pairs={{4,0},{5,1},{8,4},{9,5},{12,8},{13,9},{14,12},{15,13},{10,14},{11,... | collective-permute-start | bytes 786440 | tf_op jit(solution)/shard_map/ppermute | solution.py:502
  30.5 2.8 %collective-permute-done.4.refs_1_.refs_12_ = bf16[512,256]{1,0:T(8,128)(2,1)S(1)} collective-permute-done((bf16[512,256]{1,0:T(8,128)(2,1)S(1)}, bf16[512,256]{1,0:T(8,128)(2,1)S(1)}, u32[]{:S(2)}, u32[]{:S(2)}) %collective-permute-start.4) | collective-permute-done | bytes 262176 | tf_op jit(solution)/shard_map/ppermute | solution.py:502
  41.4 3.1 %collective-permute-done.6.refs_1_.refs_12_ = bf16[512,256]{1,0:T(8,128)(2,1)S(1)} collective-permute-done((bf16[512,256]{1,0:T(8,128)(2,1)S(1)}, bf16[512,256]{1,0:T(8,128)(2,1)S(1)}, u32[]{:S(2)}, u32[]{:S(2)}) %collective-permute-start.6) | collective-permute-done | bytes 262176 | tf_op jit(solution)/shard_map/ppermute | solution.py:502
  51.2 8.4 %shard_map.120 = (bf16[1,512,256]{2,1,0:T(8,128)(2,1)}, bf16[1,512,256]{2,1,0:T(8,128)(2,1)}, bf16[256,256]{1,0:T(8,128)(2,1)S(1)}, bf16[256,256]{1,0:T(8,128)(2...) custom-call(s32[32]{0:T(128)S(1)} %get-tuple-element.101.plan, ...), custom_call_target="tpu_custom_call" | custom-call | flops 8589934592 | bytes 16777216 | tf_op jit(solution)/shard_map/pallas_call | solution.py:395
  63.7 6.4 %shard_map.121 = (bf16[2,512,256]{2,1,0:T(8,128)(2,1)S(1)}, bf16[2,512,256]{2,1,0:T(8,128)(2,1)S(1)}, f32[2,2,128,1280]{3,2,1,0:T(8,128)S(1)}) custom-call(s32[32]{0:T(128)S(1)} %get-tuple-element.101.plan, bf16[2,128,1280]{2,1,0:T(8,128)(2,1)S(1)} %get-tuple-element.102.qt_ref.refs_0_, bf16[2,128,1280]{2,1,0:T(8,128)(2,1)S(1)} %get-tuple-element.103.refs_1_, ...), custom_call_target="tpu_custom_call" | custom-call | flops 8589934592 | bytes 16777216 | tf_op jit(solution)/shard_map/pallas_call | solution.py:395
  70.8 6.4 %collective-permute-start.30 = (bf16[512,256]{1,0:T(8,128)(2,1)S(1)}, bf16[512,256]{1,0:T(8,128)(2,1)S(1)}, u32[]{:S(2)}, u32[]{:S(2)}) collective-permute-start(bf16[512,256]{1,0:T(8,128)(2,1)S(1)} %get-tuple-element.198), channel_id=1, source_target_pairs={{4,0},{5,1},{8,4},{9,5},{12,8},{13,9},{14,12},{15,13},{10,14},{11,... | collective-permute-start | bytes 786440 | tf_op jit(solution)/shard_map/ppermute | solution.py:492
  77.2 2.0 %collective-permute-start.21 = (bf16[512,256]{1,0:T(8,128)(2,1)S(1)}, bf16[512,256]{1,0:T(8,128)(2,1)S(1)}, u32[]{:S(2)}, u32[]{:S(2)}) collective-permute-start(bf16[512,256]{1,0:T(8,128)(2,1)S(1)} %get-tuple-element.171), channel_id=1, source_target_pairs={{4,0},{5,1},{8,4},{9,5},{12,8},{13,9},{14,12},{15,13},{10,14},{11,... | collective-permute-start | bytes 786440 | tf_op jit(solution)/shard_map/ppermute | solution.py:492
  79.3 4.6 %shard_map.122 = (bf16[2,512,256]{2,1,0:T(8,128)(2,1)S(1)}, bf16[2,512,256]{2,1,0:T(8,128)(2,1)S(1)}, f32[2,2,128,1280]{3,2,1,0:T(8,128)S(1)}) custom-call(s32[32]{0:T(128)S(1)} %get-tuple-element.101.plan, bf16[2,128,1280]{2,1,0:T(8,128)(2,1)S(1)} %get-tuple-element.102.qt_ref.refs_0_, bf16[2,128,1280]{2,1,0:T(8,128)(2,1)S(1)} %get-tuple-element.103.refs_1_, ...), custom_call_target="tpu_custom_call" | custom-call | flops 8589934592 | bytes 16777216 | tf_op jit(solution)/shard_map/pallas_call | solution.py:395
  84.0 3.7 %collective-permute-start.27 = (bf16[512,256]{1,0:T(8,128)(2,1)S(1)}, bf16[512,256]{1,0:T(8,128)(2,1)S(1)}, u32[]{:S(2)}, u32[]{:S(2)}) collective-permute-start(bf16[512,256]{1,0:T(8,128)(2,1)S(1)} %get-tuple-element.195), channel_id=1, source_target_pairs={{0,4},{1,5},{4,8},{5,9},{8,12},{9,13},{12,14},{13,15},{14,10},{15,... | collective-permute-start | bytes 786440 | tf_op jit(solution)/shard_map/ppermute | solution.py:492
  88.1 2.0 %collective-permute-start.22 = (bf16[512,256]{1,0:T(8,128)(2,1)S(1)}, bf16[512,256]{1,0:T(8,128)(2,1)S(1)}, u32[]{:S(2)}, u32[]{:S(2)}) collective-permute-start(bf16[512,256]{1,0:T(8,128)(2,1)S(1)} %get-tuple-element.176), channel_id=1, source_target_pairs={{0,4},{1,5},{4,8},{5,9},{8,12},{9,13},{12,14},{13,15},{14,10},{15,... | collective-permute-start | bytes 786440 | tf_op jit(solution)/shard_map/ppermute | solution.py:492
  90.3 2.7 %shard_map.123 = (bf16[2,512,256]{2,1,0:T(8,128)(2,1)S(1)}, bf16[2,512,256]{2,1,0:T(8,128)(2,1)S(1)}, f32[2,2,128,1280]{3,2,1,0:T(8,128)S(1)}) custom-call(s32[32]{0:T(128)S(1)} %get-tuple-element.101.plan, bf16[2,128,1280]{2,1,0:T(8,128)(2,1)S(1)} %get-tuple-element.102.qt_ref.refs_0_, bf16[2,128,1280]{2,1,0:T(8,128)(2,1)S(1)} %get-tuple-element.103.refs_1_, ...), custom_call_target="tpu_custom_call" | custom-call | flops 8589934592 | bytes 16777216 | tf_op jit(solution)/shard_map/pallas_call | solution.py:395
  93.1 2.0 %collective-permute-done.27 = bf16[512,256]{1,0:T(8,128)(2,1)S(1)} collective-permute-done((bf16[512,256]{1,0:T(8,128)(2,1)S(1)}, bf16[512,256]{1,0:T(8,128)(2,1)S(1)}, u32[]{:S(2)}, u32[]{:S(2)}) %collective-permute-start.27) | collective-permute-done | bytes 262176 | tf_op jit(solution)/shard_map/ppermute | solution.py:492
  95.2 3.4 %collective-permute-start.28 = (bf16[512,256]{1,0:T(8,128)(2,1)S(1)}, bf16[512,256]{1,0:T(8,128)(2,1)S(1)}, u32[]{:S(2)}, u32[]{:S(2)}) collective-permute-start(bf16[512,256]{1,0:T(8,128)(2,1)S(1)} %get-tuple-element.193), channel_id=1, source_target_pairs={{0,4},{1,5},{4,8},{5,9},{8,12},{9,13},{12,14},{13,15},{14,10},{15,... | collective-permute-start | bytes 786440 | tf_op jit(solution)/shard_map/ppermute | solution.py:492
  100.0 6.0 %shard_map.124 = (bf16[1,512,256]{2,1,0:T(8,128)(2,1)S(1)}, bf16[1,512,256]{2,1,0:T(8,128)(2,1)S(1)}, bf16[256,1280]{1,0:T(8,128)(2,1)S(1)}, bf16[256,1280]{1,0:T(8,128)(2,1)S(1)}) custom-call(s32[32]{0:T(128)S(1)} %get-tuple-element.101.plan, bf16[2,128,1280]{2,1,0:T(8,128)(2,1)S(1)} %get-tuple-element.102.qt_ref.refs_0_, ...), custom_call_target="tpu_custom_call" | custom-call | flops 8589934592 | bytes 16777216 | tf_op jit(solution)/shard_map/pallas_call | solution.py:395
  108.3 6.5 %collective-permute-done.33 = bf16[512,256]{1,0:T(8,128)(2,1)S(1)} collective-permute-done((bf16[512,256]{1,0:T(8,128)(2,1)S(1)}, bf16[512,256]{1,0:T(8,128)(2,1)S(1)}, u32[]{:S(2)}, u32[]{:S(2)}) %collective-permute-start.33) | collective-permute-done | bytes 262176 | tf_op jit(solution)/shard_map/ppermute | solution.py:492
  114.9 2.5 %collective-permute-done.34 = bf16[512,256]{1,0:T(8,128)(2,1)S(1)} collective-permute-done((bf16[512,256]{1,0:T(8,128)(2,1)S(1)}, bf16[512,256]{1,0:T(8,128)(2,1)S(1)}, u32[]{:S(2)}, u32[]{:S(2)}) %collective-permute-start.34) | collective-permute-done | bytes 262176 | tf_op jit(solution)/shard_map/ppermute | solution.py:492
  (101 shorter events, 33.6 us)
Async XLA Ops:
  4.6 9.9 %collective-permute-start.9 = (bf16[512,256]{1,0:T(8,128)(2,1)S(1)}, bf16[512,256]{1,0:T(8,128)(2,1)S(1)}, u32[]{:S(2)}, u32[]{:S(2)}) collective-permute-start(bf16[512,256]{1,0:T(8,128)(2,1)S(1)} %pad_maximum_fusion.3.block.refs_13_), channel_id=1, source_target_pairs={{4,0},{5,1},{8,4},{9,5},{12,8},{13,9},{14,12},{15,13},{10,14},{11,... | collective-permute-start | bytes 786440 | tf_op jit(solution)/shard_map/ppermute | solution.py:502
  7.4 15.1 %collective-permute-start.3 = (bf16[512,256]{1,0:T(8,128)(2,1)S(1)}, bf16[512,256]{1,0:T(8,128)(2,1)S(1)}, u32[]{:S(2)}, u32[]{:S(2)}) collective-permute-start(bf16[512,256]{1,0:T(8,128)(2,1)S(1)} %pad_maximum_fusion.2.block.refs_12_), channel_id=1, source_target_pairs={{4,0},{5,1},{8,4},{9,5},{12,8},{13,9},{14,12},{15,13},{10,14},{11,... | collective-permute-start | bytes 786440 | tf_op jit(solution)/shard_map/ppermute | solution.py:502
  9.4 13.2 %collective-permute-start.2 = (bf16[512,256]{1,0:T(8,128)(2,1)S(1)}, bf16[512,256]{1,0:T(8,128)(2,1)S(1)}, u32[]{:S(2)}, u32[]{:S(2)}) collective-permute-start(bf16[512,256]{1,0:T(8,128)(2,1)S(1)} %pad_maximum_fusion.2.block.refs_12_), channel_id=1, source_target_pairs={{0,4},{1,5},{4,8},{5,9},{8,12},{9,13},{12,14},{13,15},{14,10},{15,... | collective-permute-start | bytes 786440 | tf_op jit(solution)/shard_map/ppermute | solution.py:502
  16.4 11.2 %collective-permute-start.10 = (bf16[512,256]{1,0:T(8,128)(2,1)S(1)}, bf16[512,256]{1,0:T(8,128)(2,1)S(1)}, u32[]{:S(2)}, u32[]{:S(2)}) collective-permute-start(bf16[512,256]{1,0:T(8,128)(2,1)S(1)} %collective-permute-done.8.refs_1_.refs_14_), channel_id=1, source_target_pairs={{0,4},{1,5},{4,8},{5,9},{8,12},{9,13},{12,14},{13,15},{14,10},{15,... | collective-permute-start | bytes 786440 | tf_op jit(solution)/shard_map/ppermute | solution.py:502
  16.5 11.2 %collective-permute-start.11 = (bf16[512,256]{1,0:T(8,128)(2,1)S(1)}, bf16[512,256]{1,0:T(8,128)(2,1)S(1)}, u32[]{:S(2)}, u32[]{:S(2)}) collective-permute-start(bf16[512,256]{1,0:T(8,128)(2,1)S(1)} %collective-permute-done.9.refs_0_.refs_15_), channel_id=1, source_target_pairs={{4,0},{5,1},{8,4},{9,5},{12,8},{13,9},{14,12},{15,13},{10,14},{11,... | collective-permute-start | bytes 786440 | tf_op jit(solution)/shard_map/ppermute | solution.py:502
  22.6 10.7 %collective-permute-start.4 = (bf16[512,256]{1,0:T(8,128)(2,1)S(1)}, bf16[512,256]{1,0:T(8,128)(2,1)S(1)}, u32[]{:S(2)}, u32[]{:S(2)}) collective-permute-start(bf16[512,256]{1,0:T(8,128)(2,1)S(1)} %collective-permute-done.2.refs_1_.refs_12_), channel_id=1, source_target_pairs={{0,4},{1,5},{4,8},{5,9},{8,12},{9,13},{12,14},{13,15},{14,10},{15,... | collective-permute-start | bytes 786440 | tf_op jit(solution)/shard_map/ppermute | solution.py:502
  22.7 10.6 %collective-permute-start.5 = (bf16[512,256]{1,0:T(8,128)(2,1)S(1)}, bf16[512,256]{1,0:T(8,128)(2,1)S(1)}, u32[]{:S(2)}, u32[]{:S(2)}) collective-permute-start(bf16[512,256]{1,0:T(8,128)(2,1)S(1)} %collective-permute-done.3.refs_0_.refs_13_), channel_id=1, source_target_pairs={{4,0},{5,1},{8,4},{9,5},{12,8},{13,9},{14,12},{15,13},{10,14},{11,... | collective-permute-start | bytes 786440 | tf_op jit(solution)/shard_map/ppermute | solution.py:502
  27.7 11.2 %collective-permute-start.12 = (bf16[512,256]{1,0:T(8,128)(2,1)S(1)}, bf16[512,256]{1,0:T(8,128)(2,1)S(1)}, u32[]{:S(2)}, u32[]{:S(2)}) collective-permute-start(bf16[512,256]{1,0:T(8,128)(2,1)S(1)} %collective-permute-done.10.refs_1_.refs_14_), channel_id=1, source_target_pairs={{0,4},{1,5},{4,8},{5,9},{8,12},{9,13},{12,14},{13,15},{14,10},{15,... | collective-permute-start | bytes 786440 | tf_op jit(solution)/shard_map/ppermute | solution.py:502
  27.8 11.1 %collective-permute-start.13 = (bf16[512,256]{1,0:T(8,128)(2,1)S(1)}, bf16[512,256]{1,0:T(8,128)(2,1)S(1)}, u32[]{:S(2)}, u32[]{:S(2)}) collective-permute-start(bf16[512,256]{1,0:T(8,128)(2,1)S(1)} %collective-permute-done.11.refs_0_.refs_15_), channel_id=1, source_target_pairs={{4,0},{5,1},{8,4},{9,5},{12,8},{13,9},{14,12},{15,13},{10,14},{11,... | collective-permute-start | bytes 786440 | tf_op jit(solution)/shard_map/ppermute | solution.py:502
  33.3 11.2 %collective-permute-start.6 = (bf16[512,256]{1,0:T(8,128)(2,1)S(1)}, bf16[512,256]{1,0:T(8,128)(2,1)S(1)}, u32[]{:S(2)}, u32[]{:S(2)}) collective-permute-start(bf16[512,256]{1,0:T(8,128)(2,1)S(1)} %collective-permute-done.4.refs_1_.refs_12_), channel_id=1, source_target_pairs={{0,4},{1,5},{4,8},{5,9},{8,12},{9,13},{12,14},{13,15},{14,10},{15,... | collective-permute-start | bytes 786440 | tf_op jit(solution)/shard_map/ppermute | solution.py:502
  34.5 10.1 %collective-permute-start.7 = (bf16[512,256]{1,0:T(8,128)(2,1)S(1)}, bf16[512,256]{1,0:T(8,128)(2,1)S(1)}, u32[]{:S(2)}, u32[]{:S(2)}) collective-permute-start(bf16[512,256]{1,0:T(8,128)(2,1)S(1)} %collective-permute-done.5.refs_0_.refs_13_), channel_id=1, source_target_pairs={{4,0},{5,1},{8,4},{9,5},{12,8},{13,9},{14,12},{15,13},{10,14},{11,... | collective-permute-start | bytes 786440 | tf_op jit(solution)/shard_map/ppermute | solution.py:502
  39.0 11.3 %collective-permute-start.17 = (bf16[256,256]{1,0:T(8,128)(2,1)S(1)}, bf16[256,256]{1,0:T(8,128)(2,1)S(1)}, u32[]{:S(2)}, u32[]{:S(2)}) collective-permute-start(bf16[256,256]{1,0:T(8,128)(2,1)S(1)} %slice.69), channel_id=1, source_target_pairs={{4,0},{5,1},{8,4},{9,5},{12,8},{13,9},{14,12},{15,13},{10,14},{11,... | collective-permute-start | bytes 393224 | tf_op jit(solution)/shard_map/ppermute | solution.py:513
  59.6 10.5 %collective-permute-start.18 = (bf16[256,256]{1,0:T(8,128)(2,1)S(1)}, bf16[256,256]{1,0:T(8,128)(2,1)S(1)}, u32[]{:S(2)}, u32[]{:S(2)}) collective-permute-start(bf16[256,256]{1,0:T(8,128)(2,1)S(1)} %get-tuple-element.162), channel_id=1, source_target_pairs={{0,4},{1,5},{4,8},{5,9},{8,12},{9,13},{12,14},{13,15},{14,10},{15,... | collective-permute-start | bytes 393224 | tf_op jit(solution)/shard_map/ppermute | solution.py:492
  60.1 10.0 %collective-permute-start.19 = (bf16[256,256]{1,0:T(8,128)(2,1)S(1)}, bf16[256,256]{1,0:T(8,128)(2,1)S(1)}, u32[]{:S(2)}, u32[]{:S(2)}) collective-permute-start(bf16[256,256]{1,0:T(8,128)(2,1)S(1)} %get-tuple-element.164), channel_id=1, source_target_pairs={{4,0},{5,1},{8,4},{9,5},{12,8},{13,9},{14,12},{15,13},{10,14},{11,... | collective-permute-start | bytes 393224 | tf_op jit(solution)/shard_map/ppermute | solution.py:492
  70.3 13.6 %collective-permute-start.26 = (bf16[512,256]{1,0:T(8,128)(2,1)S(1)}, bf16[512,256]{1,0:T(8,128)(2,1)S(1)}, u32[]{:S(2)}, u32[]{:S(2)}) collective-permute-start(bf16[512,256]{1,0:T(8,128)(2,1)S(1)} %get-tuple-element.197), channel_id=1, source_target_pairs={{0,4},{1,5},{4,8},{5,9},{8,12},{9,13},{12,14},{13,15},{14,10},{15,... | collective-permute-start | bytes 786440 | tf_op jit(solution)/shard_map/ppermute | solution.py:492
  70.8 13.1 %collective-permute-start.30 = (bf16[512,256]{1,0:T(8,128)(2,1)S(1)}, bf16[512,256]{1,0:T(8,128)(2,1)S(1)}, u32[]{:S(2)}, u32[]{:S(2)}) collective-permute-start(bf16[512,256]{1,0:T(8,128)(2,1)S(1)} %get-tuple-element.198), channel_id=1, source_target_pairs={{4,0},{5,1},{8,4},{9,5},{12,8},{13,9},{14,12},{15,13},{10,14},{11,... | collective-permute-start | bytes 786440 | tf_op jit(solution)/shard_map/ppermute | solution.py:492
  77.2 10.7 %collective-permute-start.20 = (bf16[512,256]{1,0:T(8,128)(2,1)S(1)}, bf16[512,256]{1,0:T(8,128)(2,1)S(1)}, u32[]{:S(2)}, u32[]{:S(2)}) collective-permute-start(bf16[512,256]{1,0:T(8,128)(2,1)S(1)} %get-tuple-element.169), channel_id=1, source_target_pairs={{0,4},{1,5},{4,8},{5,9},{8,12},{9,13},{12,14},{13,15},{14,10},{15,... | collective-permute-start | bytes 786440 | tf_op jit(solution)/shard_map/ppermute | solution.py:492
  77.2 10.7 %collective-permute-start.21 = (bf16[512,256]{1,0:T(8,128)(2,1)S(1)}, bf16[512,256]{1,0:T(8,128)(2,1)S(1)}, u32[]{:S(2)}, u32[]{:S(2)}) collective-permute-start(bf16[512,256]{1,0:T(8,128)(2,1)S(1)} %get-tuple-element.171), channel_id=1, source_target_pairs={{4,0},{5,1},{8,4},{9,5},{12,8},{13,9},{14,12},{15,13},{10,14},{11,... | collective-permute-start | bytes 786440 | tf_op jit(solution)/shard_map/ppermute | solution.py:492
  84.0 11.0 %collective-permute-start.27 = (bf16[512,256]{1,0:T(8,128)(2,1)S(1)}, bf16[512,256]{1,0:T(8,128)(2,1)S(1)}, u32[]{:S(2)}, u32[]{:S(2)}) collective-permute-start(bf16[512,256]{1,0:T(8,128)(2,1)S(1)} %get-tuple-element.195), channel_id=1, source_target_pairs={{0,4},{1,5},{4,8},{5,9},{8,12},{9,13},{12,14},{13,15},{14,10},{15,... | collective-permute-start | bytes 786440 | tf_op jit(solution)/shard_map/ppermute | solution.py:492
  88.1 11.8 %collective-permute-start.22 = (bf16[512,256]{1,0:T(8,128)(2,1)S(1)}, bf16[512,256]{1,0:T(8,128)(2,1)S(1)}, u32[]{:S(2)}, u32[]{:S(2)}) collective-permute-start(bf16[512,256]{1,0:T(8,128)(2,1)S(1)} %get-tuple-element.176), channel_id=1, source_target_pairs={{0,4},{1,5},{4,8},{5,9},{8,12},{9,13},{12,14},{13,15},{14,10},{15,... | collective-permute-start | bytes 786440 | tf_op jit(solution)/shard_map/ppermute | solution.py:492
  90.0 9.8 %collective-permute-start.23 = (bf16[512,256]{1,0:T(8,128)(2,1)S(1)}, bf16[512,256]{1,0:T(8,128)(2,1)S(1)}, u32[]{:S(2)}, u32[]{:S(2)}) collective-permute-start(bf16[512,256]{1,0:T(8,128)(2,1)S(1)} %get-tuple-element.178), channel_id=1, source_target_pairs={{4,0},{5,1},{8,4},{9,5},{12,8},{13,9},{14,12},{15,13},{10,14},{11,... | collective-permute-start | bytes 786440 | tf_op jit(solution)/shard_map/ppermute | solution.py:492
  95.2 12.9 %collective-permute-start.28 = (bf16[512,256]{1,0:T(8,128)(2,1)S(1)}, bf16[512,256]{1,0:T(8,128)(2,1)S(1)}, u32[]{:S(2)}, u32[]{:S(2)}) collective-permute-start(bf16[512,256]{1,0:T(8,128)(2,1)S(1)} %get-tuple-element.193), channel_id=1, source_target_pairs={{0,4},{1,5},{4,8},{5,9},{8,12},{9,13},{12,14},{13,15},{14,10},{15,... | collective-permute-start | bytes 786440 | tf_op jit(solution)/shard_map/ppermute | solution.py:492
  106.0 13.0 %collective-permute-start.24 = (bf16[256,1280]{1,0:T(8,128)(2,1)S(1)}, bf16[256,1280]{1,0:T(8,128)(2,1)S(1)}, u32[]{:S(2)}, u32[]{:S(2)}) collective-permute-start(bf16[256,1280]{1,0:T(8,128)(2,1)S(1)} %get-tuple-element.183), channel_id=1, source_target_pairs={{0,1},{1,0},{2,3},{3,2},{4,5},{5,4},{6,7},{7,6},{8,9},{9,8},{10,11... | collective-permute-start | bytes 1966088 | tf_op jit(solution)/shard_map/ppermute | solution.py:543
  106.9 10.4 %collective-permute-start.34 = (bf16[512,256]{1,0:T(8,128)(2,1)S(1)}, bf16[512,256]{1,0:T(8,128)(2,1)S(1)}, u32[]{:S(2)}, u32[]{:S(2)}) collective-permute-start(bf16[512,256]{1,0:T(8,128)(2,1)S(1)} %get-tuple-element.192), channel_id=1, source_target_pairs={{4,0},{5,1},{8,4},{9,5},{12,8},{13,9},{14,12},{15,13},{10,14},{11,... | collective-permute-start | bytes 786440 | tf_op jit(solution)/shard_map/ppermute | solution.py:492
  (20 other events, 119.5 us)

commit v6 on v5

--- a/solution.py
+++ b/solution.py
@@ -524,7 +524,7 @@
     ups, downs = terms[HALF:2 * HALF], terms[2 * HALF:3 * HALF]
 
     def add(sums, at):
-        return [(a + wide(b)).astype(jnp.bfloat16) for a, b in zip(sums, by_offset[at])]
+        return [(wide(a) + wide(b)).astype(jnp.bfloat16) for a, b in zip(sums, by_offset[at])]
 
     later = {4: [chips - 3, 3], 3: [chips - 2, 2], 2: [chips - 1, 1], 1: [0]}
     ours = theirs = None
@@ -540,17 +540,18 @@
             for slot, at in enumerate(later[step]):
                 by_offset[at] = [terms[head][slot] for head in range(HALF)]
             if last:
-                ours, theirs = terms[HALF], lax.ppermute(lead, "leaf", swap)
+                ours, theirs = terms[HALF], lead
             else:
                 carried = lead
-        ups = [wide(a) for a in shift(ups, right)]
-        downs = [wide(a) for a in shift(downs, left)]
+        ups, downs = shift(ups, right), shift(downs, left)
         if step == far:
             ups = [jnp.pad(a, ((0, rows), (0, 0))) for a in ups]
             downs = [jnp.pad(a, ((rows, 0), (0, 0))) for a in downs]
+    theirs, ups, downs = lax.optimization_barrier((theirs, ups, downs))
+    theirs = lax.ppermute(theirs, "leaf", swap)
     kept, got = [], []
     for head in range(HALF):
-        summed = (wide(by_offset[0][head]) + ups[head] + downs[head]).astype(jnp.bfloat16)
+        summed = (wide(by_offset[0][head]) + wide(ups[head]) + wide(downs[head])).astype(jnp.bfloat16)
         kept.append(summed)
         got.append(lax.ppermute(summed[rows:], "leaf", swap))
 

time: 120 us -> 114 us (0.950); the launches traced: 120 us -> 113 us
  waiting for transfers between devices: 27.6 us -> 23.2 us
  starting transfers between devices: 43.5 us -> 40.6 us
    ppermute x16, waiting for transfers between devices: 12.3 us -> 7.21 us  [shift(): return [lax.ppermute(array, 'leaf', ring) for array in arrays]]
    ppermute x16, starting transfers between devices: 24.7 us -> 21.7 us  [shift(): return [lax.ppermute(array, 'leaf', ring) for array in arrays]]
  transfers between devices with their start and end apart: 37 -> 37, of which waited for: 13 -> 14; matrix products, arithmetic and copies ran while one was open for 1% -> 1% of each run, Pallas kernels for 30% -> 31%
where the time goes in v6:
time: 114 us; the launch traced here: 113 us
  Pallas kernels  45.2 us (40%)
  starting transfers between devices  40.6 us (36%)
  waiting for transfers between devices  23.2 us (20%)
  local copies, waits for them, and re-layouts  1.58 us (1%)
  between operations  1.33 us (1%)
  other arithmetic  1.15 us (1%)
    pallas_call x5, Pallas kernels, gradients(): pl.pallas_call(functools.partial(grads_kernel, chips, tuple(offsets), fir...  28.1 us
    ppermute x16, starting transfers between devices, shift(): return [lax.ppermute(array, 'leaf', ring) for array in arrays]  21.7 us
    ppermute x6, starting transfers between devices, local(): lax.ppermute(down, 'leaf', left)  11.3 us
    ppermute x6, waiting for transfers between devices, local(): lax.ppermute(up, 'leaf', right)  10.5 us
    pallas_call x2, Pallas kernels, prepare(): pl.pallas_call(functools.partial(prepare_kernel, head), in_specs=[SMEM] *...  8.16 us
    pallas_call x6, Pallas kernels, measure(): pl.pallas_call(functools.partial(measure_kernel, offsets), in_specs=[SMEM...  7.71 us
    ppermute x16, waiting for transfers between devices, shift(): return [lax.ppermute(array, 'leaf', ring) for array in arrays]  7.21 us
    ppermute x2, starting transfers between devices, local(): lax.ppermute(down[rows:], 'leaf', left)  3.27 us
  transfers between devices with their start and end apart: 37, of which 14 were waited for; matrix products, arithmetic and copies ran while one was open for 1% of the time, Pallas kernels for 31%

profile of v6, /device:TPU:0, one launch (start us, length us, event | category | flops | bytes accessed | tf_op | source)
XLA Modules:
  0.0 113.0 jit_solution(9073915108780594513)
XLA Ops:
  4.6 2.7 %collective-permute-start.9 = (bf16[512,256]{1,0:T(8,128)(2,1)S(1)}, bf16[512,256]{1,0:T(8,128)(2,1)S(1)}, u32[]{:S(2)}, u32[]{:S(2)}) collective-permute-start(bf16[512,256]{1,0:T(8,128)(2,1)S(1)} %pad_maximum_fusion.3.block.refs_13_), channel_id=1, source_target_pairs={{4,0},{5,1},{8,4},{9,5},{12,8},{13,9},{14,12},{15,13},{10,14},{11,... | collective-permute-start | bytes 786440 | tf_op jit(solution)/shard_map/ppermute | solution.py:502
  7.4 2.0 %collective-permute-start.3 = (bf16[512,256]{1,0:T(8,128)(2,1)S(1)}, bf16[512,256]{1,0:T(8,128)(2,1)S(1)}, u32[]{:S(2)}, u32[]{:S(2)}) collective-permute-start(bf16[512,256]{1,0:T(8,128)(2,1)S(1)} %pad_maximum_fusion.2.block.refs_12_), channel_id=1, source_target_pairs={{4,0},{5,1},{8,4},{9,5},{12,8},{13,9},{14,12},{15,13},{10,14},{11,... | collective-permute-start | bytes 786440 | tf_op jit(solution)/shard_map/ppermute | solution.py:502
  9.5 4.1 %shard_map.116 = (s32[32]{0:T(128)S(1)}, bf16[2,128,1280]{2,1,0:T(8,128)(2,1)S(1)}, bf16[2,128,1280]{2,1,0:T(8,128)(2,1)S(1)}, bf16[2,1280,128]{2,1,0:T(8,128)(2...) custom-call(s32[1]{0:T(128)} %bitcast.me_ref, ...), custom_call_target="tpu_custom_call" | custom-call | bytes 12582912 | tf_op jit(solution)/shard_map/pallas_call | solution.py:157
  14.5 2.0 %collective-permute-done.8.refs_1_.refs_14_ = bf16[512,256]{1,0:T(8,128)(2,1)S(1)} collective-permute-done((bf16[512,256]{1,0:T(8,128)(2,1)S(1)}, bf16[512,256]{1,0:T(8,128)(2,1)S(1)}, u32[]{:S(2)}, u32[]{:S(2)}) %collective-permute-start.8) | collective-permute-done | bytes 262176 | tf_op jit(solution)/shard_map/ppermute | solution.py:502
  16.5 1.9 %collective-permute-start.11 = (bf16[512,256]{1,0:T(8,128)(2,1)S(1)}, bf16[512,256]{1,0:T(8,128)(2,1)S(1)}, u32[]{:S(2)}, u32[]{:S(2)}) collective-permute-start(bf16[512,256]{1,0:T(8,128)(2,1)S(1)} %collective-permute-done.9.refs_0_.refs_15_), channel_id=1, source_target_pairs={{4,0},{5,1},{8,4},{9,5},{12,8},{13,9},{14,12},{15,13},{10,14},{11,... | collective-permute-start | bytes 786440 | tf_op jit(solution)/shard_map/ppermute | solution.py:502
  18.5 4.1 %shard_map.112 = (s32[32]{0:T(128)S(1)}, bf16[2,128,1280]{2,1,0:T(8,128)(2,1)S(1)}, bf16[2,128,1280]{2,1,0:T(8,128)(2,1)S(1)}, bf16[2,1280,128]{2,1,0:T(8,128)(2...) custom-call(s32[1]{0:T(128)} %bitcast.me_ref, ...), custom_call_target="tpu_custom_call" | custom-call | bytes 12582912 | tf_op jit(solution)/shard_map/pallas_call | solution.py:157
  22.7 1.9 %collective-permute-start.5 = (bf16[512,256]{1,0:T(8,128)(2,1)S(1)}, bf16[512,256]{1,0:T(8,128)(2,1)S(1)}, u32[]{:S(2)}, u32[]{:S(2)}) collective-permute-start(bf16[512,256]{1,0:T(8,128)(2,1)S(1)} %collective-permute-done.3.refs_0_.refs_13_), channel_id=1, source_target_pairs={{4,0},{5,1},{8,4},{9,5},{12,8},{13,9},{14,12},{15,13},{10,14},{11,... | collective-permute-start | bytes 786440 | tf_op jit(solution)/shard_map/ppermute | solution.py:502
  25.4 2.3 %collective-permute-done.10.refs_1_.refs_14_ = bf16[512,256]{1,0:T(8,128)(2,1)S(1)} collective-permute-done((bf16[512,256]{1,0:T(8,128)(2,1)S(1)}, bf16[512,256]{1,0:T(8,128)(2,1)S(1)}, u32[]{:S(2)}, u32[]{:S(2)}) %collective-permute-start.10) | collective-permute-done | bytes 262176 | tf_op jit(solution)/shard_map/ppermute | solution.py:502
  30.5 2.8 %collective-permute-done.4.refs_1_.refs_12_ = bf16[512,256]{1,0:T(8,128)(2,1)S(1)} collective-permute-done((bf16[512,256]{1,0:T(8,128)(2,1)S(1)}, bf16[512,256]{1,0:T(8,128)(2,1)S(1)}, u32[]{:S(2)}, u32[]{:S(2)}) %collective-permute-start.4) | collective-permute-done | bytes 262176 | tf_op jit(solution)/shard_map/ppermute | solution.py:502
  41.1 3.4 %collective-permute-done.6.refs_1_.refs_12_ = bf16[512,256]{1,0:T(8,128)(2,1)S(1)} collective-permute-done((bf16[512,256]{1,0:T(8,128)(2,1)S(1)}, bf16[512,256]{1,0:T(8,128)(2,1)S(1)}, u32[]{:S(2)}, u32[]{:S(2)}) %collective-permute-start.6) | collective-permute-done | bytes 262176 | tf_op jit(solution)/shard_map/ppermute | solution.py:502
  51.2 8.4 %shard_map.120 = (bf16[1,512,256]{2,1,0:T(8,128)(2,1)}, bf16[1,512,256]{2,1,0:T(8,128)(2,1)}, bf16[256,256]{1,0:T(8,128)(2,1)S(1)}, bf16[256,256]{1,0:T(8,128)(2...) custom-call(s32[32]{0:T(128)S(1)} %get-tuple-element.106.plan, ...), custom_call_target="tpu_custom_call" | custom-call | flops 8589934592 | bytes 16777216 | tf_op jit(solution)/shard_map/pallas_call | solution.py:395
  59.7 2.0 %collective-permute-start.19 = (bf16[256,256]{1,0:T(8,128)(2,1)S(1)}, bf16[256,256]{1,0:T(8,128)(2,1)S(1)}, u32[]{:S(2)}, u32[]{:S(2)}) collective-permute-start(bf16[256,256]{1,0:T(8,128)(2,1)S(1)} %get-tuple-element.169), channel_id=1, source_target_pairs={{4,0},{5,1},{8,4},{9,5},{12,8},{13,9},{14,12},{15,13},{10,14},{11,... | collective-permute-start | bytes 393224 | tf_op jit(solution)/shard_map/ppermute | solution.py:492
  61.7 2.0 %collective-permute-start.29 = (bf16[256,256]{1,0:T(8,128)(2,1)S(1)}, bf16[256,256]{1,0:T(8,128)(2,1)S(1)}, u32[]{:S(2)}, u32[]{:S(2)}) collective-permute-start(bf16[256,256]{1,0:T(8,128)(2,1)S(1)} %get-tuple-element.194), channel_id=1, source_target_pairs={{4,0},{5,1},{8,4},{9,5},{12,8},{13,9},{14,12},{15,13},{10,14},{11,... | collective-permute-start | bytes 393224 | tf_op jit(solution)/shard_map/ppermute | solution.py:492
  63.7 4.6 %shard_map.121 = (bf16[2,512,256]{2,1,0:T(8,128)(2,1)S(1)}, bf16[2,512,256]{2,1,0:T(8,128)(2,1)S(1)}, f32[2,2,128,1280]{3,2,1,0:T(8,128)S(1)}) custom-call(s32[32]{0:T(128)S(1)} %get-tuple-element.106.plan, bf16[2,128,1280]{2,1,0:T(8,128)(2,1)S(1)} %get-tuple-element.107.qt_ref.refs_0_, bf16[2,128,1280]{2,1,0:T(8,128)(2,1)S(1)} %get-tuple-element.108.refs_1_, ...), custom_call_target="tpu_custom_call" | custom-call | flops 8589934592 | bytes 16777216 | tf_op jit(solution)/shard_map/pallas_call | solution.py:395
  68.5 6.7 %collective-permute-start.30 = (bf16[512,256]{1,0:T(8,128)(2,1)S(1)}, bf16[512,256]{1,0:T(8,128)(2,1)S(1)}, u32[]{:S(2)}, u32[]{:S(2)}) collective-permute-start(bf16[512,256]{1,0:T(8,128)(2,1)S(1)} %get-tuple-element.207), channel_id=1, source_target_pairs={{4,0},{5,1},{8,4},{9,5},{12,8},{13,9},{14,12},{15,13},{10,14},{11,... | collective-permute-start | bytes 786440 | tf_op jit(solution)/shard_map/ppermute | solution.py:492
  75.3 2.1 %collective-permute-start.21 = (bf16[512,256]{1,0:T(8,128)(2,1)S(1)}, bf16[512,256]{1,0:T(8,128)(2,1)S(1)}, u32[]{:S(2)}, u32[]{:S(2)}) collective-permute-start(bf16[512,256]{1,0:T(8,128)(2,1)S(1)} %get-tuple-element.176), channel_id=1, source_target_pairs={{4,0},{5,1},{8,4},{9,5},{12,8},{13,9},{14,12},{15,13},{10,14},{11,... | collective-permute-start | bytes 786440 | tf_op jit(solution)/shard_map/ppermute | solution.py:492
  77.3 6.4 %shard_map.122 = (bf16[2,512,256]{2,1,0:T(8,128)(2,1)S(1)}, bf16[2,512,256]{2,1,0:T(8,128)(2,1)S(1)}, f32[2,2,128,1280]{3,2,1,0:T(8,128)S(1)}) custom-call(s32[32]{0:T(128)S(1)} %get-tuple-element.106.plan, bf16[2,128,1280]{2,1,0:T(8,128)(2,1)S(1)} %get-tuple-element.107.qt_ref.refs_0_, bf16[2,128,1280]{2,1,0:T(8,128)(2,1)S(1)} %get-tuple-element.108.refs_1_, ...), custom_call_target="tpu_custom_call" | custom-call | flops 8589934592 | bytes 16777216 | tf_op jit(solution)/shard_map/pallas_call | solution.py:395
  83.9 2.0 %collective-permute-start.31 = (bf16[512,256]{1,0:T(8,128)(2,1)S(1)}, bf16[512,256]{1,0:T(8,128)(2,1)S(1)}, u32[]{:S(2)}, u32[]{:S(2)}) collective-permute-start(bf16[512,256]{1,0:T(8,128)(2,1)S(1)} %get-tuple-element.205), channel_id=1, source_target_pairs={{4,0},{5,1},{8,4},{9,5},{12,8},{13,9},{14,12},{15,13},{10,14},{11,... | collective-permute-start | bytes 786440 | tf_op jit(solution)/shard_map/ppermute | solution.py:492
  89.0 2.7 %shard_map.123 = (bf16[2,512,256]{2,1,0:T(8,128)(2,1)S(1)}, bf16[2,512,256]{2,1,0:T(8,128)(2,1)S(1)}, f32[2,2,128,1280]{3,2,1,0:T(8,128)S(1)}) custom-call(s32[32]{0:T(128)S(1)} %get-tuple-element.106.plan, bf16[2,128,1280]{2,1,0:T(8,128)(2,1)S(1)} %get-tuple-element.107.qt_ref.refs_0_, bf16[2,128,1280]{2,1,0:T(8,128)(2,1)S(1)} %get-tuple-element.108.refs_1_, ...), custom_call_target="tpu_custom_call" | custom-call | flops 8589934592 | bytes 16777216 | tf_op jit(solution)/shard_map/pallas_call | solution.py:395
  92.7 2.5 %collective-permute-done.26 = bf16[512,256]{1,0:T(8,128)(2,1)S(1)} collective-permute-done((bf16[512,256]{1,0:T(8,128)(2,1)S(1)}, bf16[512,256]{1,0:T(8,128)(2,1)S(1)}, u32[]{:S(2)}, u32[]{:S(2)}) %collective-permute-start.26) | collective-permute-done | bytes 262176 | tf_op jit(solution)/shard_map/ppermute | solution.py:492
  95.4 2.5 %collective-permute-start.27 = (bf16[512,256]{1,0:T(8,128)(2,1)S(1)}, bf16[512,256]{1,0:T(8,128)(2,1)S(1)}, u32[]{:S(2)}, u32[]{:S(2)}) collective-permute-start(bf16[512,256]{1,0:T(8,128)(2,1)S(1)} %get-tuple-element.204), channel_id=1, source_target_pairs={{0,4},{1,5},{4,8},{5,9},{8,12},{9,13},{12,14},{13,15},{14,10},{15,... | collective-permute-start | bytes 786440 | tf_op jit(solution)/shard_map/ppermute | solution.py:492
  97.9 2.9 %collective-permute-done.22 = bf16[512,256]{1,0:T(8,128)(2,1)S(1)} collective-permute-done((bf16[512,256]{1,0:T(8,128)(2,1)S(1)}, bf16[512,256]{1,0:T(8,128)(2,1)S(1)}, u32[]{:S(2)}, u32[]{:S(2)}) %collective-permute-start.22) | collective-permute-done | bytes 262176 | tf_op jit(solution)/shard_map/ppermute | solution.py:492
  101.0 2.0 %collective-permute-start.33 = (bf16[512,256]{1,0:T(8,128)(2,1)S(1)}, bf16[512,256]{1,0:T(8,128)(2,1)S(1)}, u32[]{:S(2)}, u32[]{:S(2)}) collective-permute-start(bf16[512,256]{1,0:T(8,128)(2,1)S(1)} %get-tuple-element.195), channel_id=1, source_target_pairs={{4,0},{5,1},{8,4},{9,5},{12,8},{13,9},{14,12},{15,13},{10,14},{11,... | collective-permute-start | bytes 786440 | tf_op jit(solution)/shard_map/ppermute | solution.py:492
  103.0 5.9 %shard_map.124 = (bf16[1,512,256]{2,1,0:T(8,128)(2,1)S(1)}, bf16[1,512,256]{2,1,0:T(8,128)(2,1)S(1)}, bf16[256,1280]{1,0:T(8,128)(2,1)S(1)}, bf16[256,1280]{1,0:T(8,128)(2,1)S(1)}) custom-call(s32[32]{0:T(128)S(1)} %get-tuple-element.106.plan, bf16[2,128,1280]{2,1,0:T(8,128)(2,1)S(1)} %get-tuple-element.107.qt_ref.refs_0_, ...), custom_call_target="tpu_custom_call" | custom-call | flops 8589934592 | bytes 16777216 | tf_op jit(solution)/shard_map/pallas_call | solution.py:395
  (101 shorter events, 31.7 us)
Async XLA Ops:
  4.6 9.9 %collective-permute-start.9 = (bf16[512,256]{1,0:T(8,128)(2,1)S(1)}, bf16[512,256]{1,0:T(8,128)(2,1)S(1)}, u32[]{:S(2)}, u32[]{:S(2)}) collective-permute-start(bf16[512,256]{1,0:T(8,128)(2,1)S(1)} %pad_maximum_fusion.3.block.refs_13_), channel_id=1, source_target_pairs={{4,0},{5,1},{8,4},{9,5},{12,8},{13,9},{14,12},{15,13},{10,14},{11,... | collective-permute-start | bytes 786440 | tf_op jit(solution)/shard_map/ppermute | solution.py:502
  7.3 9.2 %collective-permute-start.8 = (bf16[512,256]{1,0:T(8,128)(2,1)S(1)}, bf16[512,256]{1,0:T(8,128)(2,1)S(1)}, u32[]{:S(2)}, u32[]{:S(2)}) collective-permute-start(bf16[512,256]{1,0:T(8,128)(2,1)S(1)} %pad_maximum_fusion.3.block.refs_13_), channel_id=1, source_target_pairs={{0,4},{1,5},{4,8},{5,9},{8,12},{9,13},{12,14},{13,15},{14,10},{15,... | collective-permute-start | bytes 786440 | tf_op jit(solution)/shard_map/ppermute | solution.py:502
  7.4 15.1 %collective-permute-start.3 = (bf16[512,256]{1,0:T(8,128)(2,1)S(1)}, bf16[512,256]{1,0:T(8,128)(2,1)S(1)}, u32[]{:S(2)}, u32[]{:S(2)}) collective-permute-start(bf16[512,256]{1,0:T(8,128)(2,1)S(1)} %pad_maximum_fusion.2.block.refs_12_), channel_id=1, source_target_pairs={{4,0},{5,1},{8,4},{9,5},{12,8},{13,9},{14,12},{15,13},{10,14},{11,... | collective-permute-start | bytes 786440 | tf_op jit(solution)/shard_map/ppermute | solution.py:502
  9.4 13.2 %collective-permute-start.2 = (bf16[512,256]{1,0:T(8,128)(2,1)S(1)}, bf16[512,256]{1,0:T(8,128)(2,1)S(1)}, u32[]{:S(2)}, u32[]{:S(2)}) collective-permute-start(bf16[512,256]{1,0:T(8,128)(2,1)S(1)} %pad_maximum_fusion.2.block.refs_12_), channel_id=1, source_target_pairs={{0,4},{1,5},{4,8},{5,9},{8,12},{9,13},{12,14},{13,15},{14,10},{15,... | collective-permute-start | bytes 786440 | tf_op jit(solution)/shard_map/ppermute | solution.py:502
  16.4 11.2 %collective-permute-start.10 = (bf16[512,256]{1,0:T(8,128)(2,1)S(1)}, bf16[512,256]{1,0:T(8,128)(2,1)S(1)}, u32[]{:S(2)}, u32[]{:S(2)}) collective-permute-start(bf16[512,256]{1,0:T(8,128)(2,1)S(1)} %collective-permute-done.8.refs_1_.refs_14_), channel_id=1, source_target_pairs={{0,4},{1,5},{4,8},{5,9},{8,12},{9,13},{12,14},{13,15},{14,10},{15,... | collective-permute-start | bytes 786440 | tf_op jit(solution)/shard_map/ppermute | solution.py:502
  16.5 11.2 %collective-permute-start.11 = (bf16[512,256]{1,0:T(8,128)(2,1)S(1)}, bf16[512,256]{1,0:T(8,128)(2,1)S(1)}, u32[]{:S(2)}, u32[]{:S(2)}) collective-permute-start(bf16[512,256]{1,0:T(8,128)(2,1)S(1)} %collective-permute-done.9.refs_0_.refs_15_), channel_id=1, source_target_pairs={{4,0},{5,1},{8,4},{9,5},{12,8},{13,9},{14,12},{15,13},{10,14},{11,... | collective-permute-start | bytes 786440 | tf_op jit(solution)/shard_map/ppermute | solution.py:502
  22.6 10.7 %collective-permute-start.4 = (bf16[512,256]{1,0:T(8,128)(2,1)S(1)}, bf16[512,256]{1,0:T(8,128)(2,1)S(1)}, u32[]{:S(2)}, u32[]{:S(2)}) collective-permute-start(bf16[512,256]{1,0:T(8,128)(2,1)S(1)} %collective-permute-done.2.refs_1_.refs_12_), channel_id=1, source_target_pairs={{0,4},{1,5},{4,8},{5,9},{8,12},{9,13},{12,14},{13,15},{14,10},{15,... | collective-permute-start | bytes 786440 | tf_op jit(solution)/shard_map/ppermute | solution.py:502
  22.7 10.6 %collective-permute-start.5 = (bf16[512,256]{1,0:T(8,128)(2,1)S(1)}, bf16[512,256]{1,0:T(8,128)(2,1)S(1)}, u32[]{:S(2)}, u32[]{:S(2)}) collective-permute-start(bf16[512,256]{1,0:T(8,128)(2,1)S(1)} %collective-permute-done.3.refs_0_.refs_13_), channel_id=1, source_target_pairs={{4,0},{5,1},{8,4},{9,5},{12,8},{13,9},{14,12},{15,13},{10,14},{11,... | collective-permute-start | bytes 786440 | tf_op jit(solution)/shard_map/ppermute | solution.py:502
  27.7 11.3 %collective-permute-start.12 = (bf16[512,256]{1,0:T(8,128)(2,1)S(1)}, bf16[512,256]{1,0:T(8,128)(2,1)S(1)}, u32[]{:S(2)}, u32[]{:S(2)}) collective-permute-start(bf16[512,256]{1,0:T(8,128)(2,1)S(1)} %collective-permute-done.10.refs_1_.refs_14_), channel_id=1, source_target_pairs={{0,4},{1,5},{4,8},{5,9},{8,12},{9,13},{12,14},{13,15},{14,10},{15,... | collective-permute-start | bytes 786440 | tf_op jit(solution)/shard_map/ppermute | solution.py:502
  27.8 11.2 %collective-permute-start.13 = (bf16[512,256]{1,0:T(8,128)(2,1)S(1)}, bf16[512,256]{1,0:T(8,128)(2,1)S(1)}, u32[]{:S(2)}, u32[]{:S(2)}) collective-permute-start(bf16[512,256]{1,0:T(8,128)(2,1)S(1)} %collective-permute-done.11.refs_0_.refs_15_), channel_id=1, source_target_pairs={{4,0},{5,1},{8,4},{9,5},{12,8},{13,9},{14,12},{15,13},{10,14},{11,... | collective-permute-start | bytes 786440 | tf_op jit(solution)/shard_map/ppermute | solution.py:502
  33.3 11.2 %collective-permute-start.6 = (bf16[512,256]{1,0:T(8,128)(2,1)S(1)}, bf16[512,256]{1,0:T(8,128)(2,1)S(1)}, u32[]{:S(2)}, u32[]{:S(2)}) collective-permute-start(bf16[512,256]{1,0:T(8,128)(2,1)S(1)} %collective-permute-done.4.refs_1_.refs_12_), channel_id=1, source_target_pairs={{0,4},{1,5},{4,8},{5,9},{8,12},{9,13},{12,14},{13,15},{14,10},{15,... | collective-permute-start | bytes 786440 | tf_op jit(solution)/shard_map/ppermute | solution.py:502
  34.5 10.1 %collective-permute-start.7 = (bf16[512,256]{1,0:T(8,128)(2,1)S(1)}, bf16[512,256]{1,0:T(8,128)(2,1)S(1)}, u32[]{:S(2)}, u32[]{:S(2)}) collective-permute-start(bf16[512,256]{1,0:T(8,128)(2,1)S(1)} %collective-permute-done.5.refs_0_.refs_13_), channel_id=1, source_target_pairs={{4,0},{5,1},{8,4},{9,5},{12,8},{13,9},{14,12},{15,13},{10,14},{11,... | collective-permute-start | bytes 786440 | tf_op jit(solution)/shard_map/ppermute | solution.py:502
  39.0 10.2 %collective-permute-start.17 = (bf16[256,256]{1,0:T(8,128)(2,1)S(1)}, bf16[256,256]{1,0:T(8,128)(2,1)S(1)}, u32[]{:S(2)}, u32[]{:S(2)}) collective-permute-start(bf16[256,256]{1,0:T(8,128)(2,1)S(1)} %slice.69), channel_id=1, source_target_pairs={{4,0},{5,1},{8,4},{9,5},{12,8},{13,9},{14,12},{15,13},{10,14},{11,... | collective-permute-start | bytes 393224 | tf_op jit(solution)/shard_map/ppermute | solution.py:513
  59.6 8.7 %collective-permute-start.18 = (bf16[256,256]{1,0:T(8,128)(2,1)S(1)}, bf16[256,256]{1,0:T(8,128)(2,1)S(1)}, u32[]{:S(2)}, u32[]{:S(2)}) collective-permute-start(bf16[256,256]{1,0:T(8,128)(2,1)S(1)} %get-tuple-element.167), channel_id=1, source_target_pairs={{0,4},{1,5},{4,8},{5,9},{8,12},{9,13},{12,14},{13,15},{14,10},{15,... | collective-permute-start | bytes 393224 | tf_op jit(solution)/shard_map/ppermute | solution.py:492
  59.7 8.7 %collective-permute-start.19 = (bf16[256,256]{1,0:T(8,128)(2,1)S(1)}, bf16[256,256]{1,0:T(8,128)(2,1)S(1)}, u32[]{:S(2)}, u32[]{:S(2)}) collective-permute-start(bf16[256,256]{1,0:T(8,128)(2,1)S(1)} %get-tuple-element.169), channel_id=1, source_target_pairs={{4,0},{5,1},{8,4},{9,5},{12,8},{13,9},{14,12},{15,13},{10,14},{11,... | collective-permute-start | bytes 393224 | tf_op jit(solution)/shard_map/ppermute | solution.py:492
  68.5 15.2 %collective-permute-start.30 = (bf16[512,256]{1,0:T(8,128)(2,1)S(1)}, bf16[512,256]{1,0:T(8,128)(2,1)S(1)}, u32[]{:S(2)}, u32[]{:S(2)}) collective-permute-start(bf16[512,256]{1,0:T(8,128)(2,1)S(1)} %get-tuple-element.207), channel_id=1, source_target_pairs={{4,0},{5,1},{8,4},{9,5},{12,8},{13,9},{14,12},{15,13},{10,14},{11,... | collective-permute-start | bytes 786440 | tf_op jit(solution)/shard_map/ppermute | solution.py:492
  75.3 11.5 %collective-permute-start.20 = (bf16[512,256]{1,0:T(8,128)(2,1)S(1)}, bf16[512,256]{1,0:T(8,128)(2,1)S(1)}, u32[]{:S(2)}, u32[]{:S(2)}) collective-permute-start(bf16[512,256]{1,0:T(8,128)(2,1)S(1)} %get-tuple-element.174), channel_id=1, source_target_pairs={{0,4},{1,5},{4,8},{5,9},{8,12},{9,13},{12,14},{13,15},{14,10},{15,... | collective-permute-start | bytes 786440 | tf_op jit(solution)/shard_map/ppermute | solution.py:492
  75.3 11.5 %collective-permute-start.21 = (bf16[512,256]{1,0:T(8,128)(2,1)S(1)}, bf16[512,256]{1,0:T(8,128)(2,1)S(1)}, u32[]{:S(2)}, u32[]{:S(2)}) collective-permute-start(bf16[512,256]{1,0:T(8,128)(2,1)S(1)} %get-tuple-element.176), channel_id=1, source_target_pairs={{4,0},{5,1},{8,4},{9,5},{12,8},{13,9},{14,12},{15,13},{10,14},{11,... | collective-permute-start | bytes 786440 | tf_op jit(solution)/shard_map/ppermute | solution.py:492
  83.9 8.8 %collective-permute-start.31 = (bf16[512,256]{1,0:T(8,128)(2,1)S(1)}, bf16[512,256]{1,0:T(8,128)(2,1)S(1)}, u32[]{:S(2)}, u32[]{:S(2)}) collective-permute-start(bf16[512,256]{1,0:T(8,128)(2,1)S(1)} %get-tuple-element.205), channel_id=1, source_target_pairs={{4,0},{5,1},{8,4},{9,5},{12,8},{13,9},{14,12},{15,13},{10,14},{11,... | collective-permute-start | bytes 786440 | tf_op jit(solution)/shard_map/ppermute | solution.py:492
  85.9 9.2 %collective-permute-start.26 = (bf16[512,256]{1,0:T(8,128)(2,1)S(1)}, bf16[512,256]{1,0:T(8,128)(2,1)S(1)}, u32[]{:S(2)}, u32[]{:S(2)}) collective-permute-start(bf16[512,256]{1,0:T(8,128)(2,1)S(1)} %get-tuple-element.206), channel_id=1, source_target_pairs={{0,4},{1,5},{4,8},{5,9},{8,12},{9,13},{12,14},{13,15},{14,10},{15,... | collective-permute-start | bytes 786440 | tf_op jit(solution)/shard_map/ppermute | solution.py:492
  86.9 13.9 %collective-permute-start.22 = (bf16[512,256]{1,0:T(8,128)(2,1)S(1)}, bf16[512,256]{1,0:T(8,128)(2,1)S(1)}, u32[]{:S(2)}, u32[]{:S(2)}) collective-permute-start(bf16[512,256]{1,0:T(8,128)(2,1)S(1)} %get-tuple-element.181), channel_id=1, source_target_pairs={{0,4},{1,5},{4,8},{5,9},{8,12},{9,13},{12,14},{13,15},{14,10},{15,... | collective-permute-start | bytes 786440 | tf_op jit(solution)/shard_map/ppermute | solution.py:492
  87.2 13.6 %collective-permute-start.23 = (bf16[512,256]{1,0:T(8,128)(2,1)S(1)}, bf16[512,256]{1,0:T(8,128)(2,1)S(1)}, u32[]{:S(2)}, u32[]{:S(2)}) collective-permute-start(bf16[512,256]{1,0:T(8,128)(2,1)S(1)} %get-tuple-element.183), channel_id=1, source_target_pairs={{4,0},{5,1},{8,4},{9,5},{12,8},{13,9},{14,12},{15,13},{10,14},{11,... | collective-permute-start | bytes 786440 | tf_op jit(solution)/shard_map/ppermute | solution.py:492
  95.3 13.6 %collective-permute-start.32 = (bf16[512,256]{1,0:T(8,128)(2,1)S(1)}, bf16[512,256]{1,0:T(8,128)(2,1)S(1)}, u32[]{:S(2)}, u32[]{:S(2)}) collective-permute-start(bf16[512,256]{1,0:T(8,128)(2,1)S(1)} %get-tuple-element.203), channel_id=1, source_target_pairs={{4,0},{5,1},{8,4},{9,5},{12,8},{13,9},{14,12},{15,13},{10,14},{11,... | collective-permute-start | bytes 786440 | tf_op jit(solution)/shard_map/ppermute | solution.py:492
  95.4 13.6 %collective-permute-start.27 = (bf16[512,256]{1,0:T(8,128)(2,1)S(1)}, bf16[512,256]{1,0:T(8,128)(2,1)S(1)}, u32[]{:S(2)}, u32[]{:S(2)}) collective-permute-start(bf16[512,256]{1,0:T(8,128)(2,1)S(1)} %get-tuple-element.204), channel_id=1, source_target_pairs={{0,4},{1,5},{4,8},{5,9},{8,12},{9,13},{12,14},{13,15},{14,10},{15,... | collective-permute-start | bytes 786440 | tf_op jit(solution)/shard_map/ppermute | solution.py:492
  (20 other events, 99.7 us)

commit v7 on v6

--- a/solution.py
+++ b/solution.py
@@ -219,7 +219,7 @@
         carried, refs = refs[0], refs[1:]
     terms, refs = refs[:HALF], refs[HALF:]
     if first:
-        ups, downs, refs = refs[:HALF], refs[HALF:2 * HALF], refs[2 * HALF:]
+        up_ref, down_ref, refs = refs[0], refs[1], refs[2:]
         lse_out, refs = refs[:HALF], refs[HALF:]
     outs, refs = refs[:2 if last else 1], refs[2 if last else 1:]
     (kv_ref, acc_ref, stage_ref, zero_ref, p_ref, ds_ref, sum_ref, dqt_ref, offset_ref,
@@ -267,11 +267,11 @@
 
             @pl.when(i == 0)
             def _():
-                put(ups[head])
+                put(up_ref.at[head])
 
             @pl.when(i == 1)
             def _():
-                put(downs[head])
+                put(down_ref.at[head])
 
     def sent(sem_of):
         for head in range(HALF):
@@ -379,13 +379,13 @@
     arrays = [a for head in shared for a in head] + [a for head in blocks for a in head]
     arrays += [] if first else [carried]
     dense = jax.ShapeDtypeStruct((len(offsets), 2 * rows, 2 * DH), bf16)
-    piece = jax.ShapeDtypeStruct((rows, 2 * DH), bf16)
+    piece = jax.ShapeDtypeStruct((HALF, rows, 2 * DH), bf16)
     query = jax.ShapeDtypeStruct((rows, HALF * WIDE), bf16)
     sums = jax.ShapeDtypeStruct((HALF, 2, DH, PER * rows), f32)
     out_shape, out_specs = [dense] * HALF, [HBM] * HALF
     if first:
-        out_shape += [piece] * (2 * HALF) + [row_stats(rows)] * HALF
-        out_specs += [HBM] * (2 * HALF) + [VMEM] * HALF
+        out_shape += [piece] * 2 + [row_stats(rows)] * HALF
+        out_specs += [HBM] * 2 + [VMEM] * HALF
     out_shape += [query] * 2 if last else [sums]
     out_specs += [VMEM] * (2 if last else 1)
     flat = sum(len(head) for head in shared)
@@ -519,9 +519,9 @@
         offsets += [far + step, far - step]
     arrays = [halves[head] + [blocks[head][at] for at in offsets[1:]] for head in range(HALF)]
     *terms, carried = gradients(prepared, stats, offsets, arrays, None, False)
-    lse = [[a] for a in terms[3 * HALF:]]
+    lse = [[a] for a in terms[HALF + 2:]]
     by_offset = {at: [terms[head][slot] for head in range(HALF)] for slot, at in enumerate(offsets)}
-    ups, downs = terms[HALF:2 * HALF], terms[2 * HALF:3 * HALF]
+    ups, downs = terms[HALF:HALF + 1], terms[HALF + 1:HALF + 2]
 
     def add(sums, at):
         return [(wide(a) + wide(b)).astype(jnp.bfloat16) for a, b in zip(sums, by_offset[at])]
@@ -533,8 +533,8 @@
             ups, downs = add(ups, step), add(downs, chips - step)
         if step in later:
             last = 0 in later[step]
-            (lse, carried), held = lax.optimization_barrier(((lse, carried), (ups[1:], downs[1:])))
-            ups, downs = ups[:1] + held[0], downs[:1] + held[1]
+            (lse, carried), held = lax.optimization_barrier(((lse, carried), (ups[-1:], downs[-1:])))
+            ups, downs = ups[:-1] + held[0], downs[:-1] + held[1]
             arrays = [[blocks[head][at] for at in later[step]] for head in range(HALF)]
             *terms, lead = gradients(prepared, lse, later[step], arrays, carried, last)
             for slot, at in enumerate(later[step]):
@@ -545,8 +545,8 @@
                 carried = lead
         ups, downs = shift(ups, right), shift(downs, left)
         if step == far:
-            ups = [jnp.pad(a, ((0, rows), (0, 0))) for a in ups]
-            downs = [jnp.pad(a, ((rows, 0), (0, 0))) for a in downs]
+            ups = [jnp.pad(a, ((0, rows), (0, 0))) for a in ups[0]]
+            downs = [jnp.pad(a, ((rows, 0), (0, 0))) for a in downs[0]]
     theirs, ups, downs = lax.optimization_barrier((theirs, ups, downs))
     theirs = lax.ppermute(theirs, "leaf", swap)
     kept, got = [], []

time: 114 us -> 112 us (0.982)
  starting transfers between devices: 40.6 us -> 33.8 us
  Pallas kernels: 45.2 us -> 51.2 us
  waiting for transfers between devices: 23.2 us -> 21.3 us
    ppermute x16 -> x14, starting transfers between devices: 21.7 us -> 14.9 us  [shift(): return [lax.ppermute(array, 'leaf', ring) for array in arrays]]
    pallas_call x5, Pallas kernels: 28.1 us -> 31.9 us  [gradients(): pl.pallas_call(functools.partial(grads_kernel, chips, tuple(offsets), fir...]
    pallas_call x6, Pallas kernels: 7.71 us -> 9.84 us  [measure(): pl.pallas_call(functools.partial(measure_kernel, offsets), in_specs=[SMEM...]
    ppermute x2, waiting for transfers between devices: 1.58 us -> 0.01 us  [local(): lax.ppermute(up[:rows], 'leaf', right)]
    ppermute x16 -> x14, waiting for transfers between devices: 7.21 us -> 7.19 us  [shift(): return [lax.ppermute(array, 'leaf', ring) for array in arrays]]
  transfers between devices with their start and end apart: 37 -> 35, of which waited for: 14 -> 13; matrix products, arithmetic and copies ran while one was open for 1% -> 1% of each run, Pallas kernels for 31% -> 38%
where the time goes in v7:
time: 112 us; the launch traced here: 110 us
  Pallas kernels  51.2 us (46%)
  starting transfers between devices  33.8 us (30%)
  waiting for transfers between devices  21.3 us (19%)
  local copies, waits for them, and re-layouts  1.62 us (1%)
  between operations  1.34 us (1%)
  other arithmetic  1.13 us (1%)
    pallas_call x5, Pallas kernels, gradients(): pl.pallas_call(functools.partial(grads_kernel, chips, tuple(offsets), fir...  31.9 us
    ppermute x14, starting transfers between devices, shift(): return [lax.ppermute(array, 'leaf', ring) for array in arrays]  14.9 us
    ppermute x6, starting transfers between devices, local(): lax.ppermute(down, 'leaf', left)  11.8 us
    ppermute x6, waiting for transfers between devices, local(): lax.ppermute(up, 'leaf', right)  10.5 us
    pallas_call x6, Pallas kernels, measure(): pl.pallas_call(functools.partial(measure_kernel, offsets), in_specs=[SMEM...  9.84 us
    pallas_call x2, Pallas kernels, prepare(): pl.pallas_call(functools.partial(prepare_kernel, head), in_specs=[SMEM] *...  8.16 us
    ppermute x14, waiting for transfers between devices, shift(): return [lax.ppermute(array, 'leaf', ring) for array in arrays]  7.19 us
    ppermute x2, starting transfers between devices, local(): lax.ppermute(down[rows:], 'leaf', left)  3.35 us
  transfers between devices with their start and end apart: 35, of which 13 were waited for; matrix products, arithmetic and copies ran while one was open for 1% of the time, Pallas kernels for 38%

profile of v7, /device:TPU:0, one launch (start us, length us, event | category | flops | bytes accessed | tf_op | source)
XLA Modules:
  0.0 110.3 jit_solution(6863708084737191493)
XLA Ops:
  4.6 2.7 %collective-permute-start.9 = (bf16[512,256]{1,0:T(8,128)(2,1)S(1)}, bf16[512,256]{1,0:T(8,128)(2,1)S(1)}, u32[]{:S(2)}, u32[]{:S(2)}) collective-permute-start(bf16[512,256]{1,0:T(8,128)(2,1)S(1)} %pad_maximum_fusion.3.block.refs_13_), channel_id=1, source_target_pairs={{4,0},{5,1},{8,4},{9,5},{12,8},{13,9},{14,12},{15,13},{10,14},{11,... | collective-permute-start | bytes 786440 | tf_op jit(solution)/shard_map/ppermute | solution.py:502
  7.4 2.0 %collective-permute-start.3 = (bf16[512,256]{1,0:T(8,128)(2,1)S(1)}, bf16[512,256]{1,0:T(8,128)(2,1)S(1)}, u32[]{:S(2)}, u32[]{:S(2)}) collective-permute-start(bf16[512,256]{1,0:T(8,128)(2,1)S(1)} %pad_maximum_fusion.2.block.refs_12_), channel_id=1, source_target_pairs={{4,0},{5,1},{8,4},{9,5},{12,8},{13,9},{14,12},{15,13},{10,14},{11,... | collective-permute-start | bytes 786440 | tf_op jit(solution)/shard_map/ppermute | solution.py:502
  9.5 4.1 %shard_map.116 = (s32[32]{0:T(128)S(1)}, bf16[2,128,1280]{2,1,0:T(8,128)(2,1)S(1)}, bf16[2,128,1280]{2,1,0:T(8,128)(2,1)S(1)}, bf16[2,1280,128]{2,1,0:T(8,128)(2...) custom-call(s32[1]{0:T(128)} %bitcast.me_ref, ...), custom_call_target="tpu_custom_call" | custom-call | bytes 12582912 | tf_op jit(solution)/shard_map/pallas_call | solution.py:157
  14.5 2.0 %collective-permute-done.8.refs_1_.refs_14_ = bf16[512,256]{1,0:T(8,128)(2,1)S(1)} collective-permute-done((bf16[512,256]{1,0:T(8,128)(2,1)S(1)}, bf16[512,256]{1,0:T(8,128)(2,1)S(1)}, u32[]{:S(2)}, u32[]{:S(2)}) %collective-permute-start.8) | collective-permute-done | bytes 262176 | tf_op jit(solution)/shard_map/ppermute | solution.py:502
  16.5 1.9 %collective-permute-start.11 = (bf16[512,256]{1,0:T(8,128)(2,1)S(1)}, bf16[512,256]{1,0:T(8,128)(2,1)S(1)}, u32[]{:S(2)}, u32[]{:S(2)}) collective-permute-start(bf16[512,256]{1,0:T(8,128)(2,1)S(1)} %collective-permute-done.9.refs_0_.refs_15_), channel_id=1, source_target_pairs={{4,0},{5,1},{8,4},{9,5},{12,8},{13,9},{14,12},{15,13},{10,14},{11,... | collective-permute-start | bytes 786440 | tf_op jit(solution)/shard_map/ppermute | solution.py:502
  18.5 4.1 %shard_map.112 = (s32[32]{0:T(128)S(1)}, bf16[2,128,1280]{2,1,0:T(8,128)(2,1)S(1)}, bf16[2,128,1280]{2,1,0:T(8,128)(2,1)S(1)}, bf16[2,1280,128]{2,1,0:T(8,128)(2...) custom-call(s32[1]{0:T(128)} %bitcast.me_ref, ...), custom_call_target="tpu_custom_call" | custom-call | bytes 12582912 | tf_op jit(solution)/shard_map/pallas_call | solution.py:157
  22.7 1.9 %collective-permute-start.5 = (bf16[512,256]{1,0:T(8,128)(2,1)S(1)}, bf16[512,256]{1,0:T(8,128)(2,1)S(1)}, u32[]{:S(2)}, u32[]{:S(2)}) collective-permute-start(bf16[512,256]{1,0:T(8,128)(2,1)S(1)} %collective-permute-done.3.refs_0_.refs_13_), channel_id=1, source_target_pairs={{4,0},{5,1},{8,4},{9,5},{12,8},{13,9},{14,12},{15,13},{10,14},{11,... | collective-permute-start | bytes 786440 | tf_op jit(solution)/shard_map/ppermute | solution.py:502
  27.8 1.9 %collective-permute-start.13 = (bf16[512,256]{1,0:T(8,128)(2,1)S(1)}, bf16[512,256]{1,0:T(8,128)(2,1)S(1)}, u32[]{:S(2)}, u32[]{:S(2)}) collective-permute-start(bf16[512,256]{1,0:T(8,128)(2,1)S(1)} %collective-permute-done.11.refs_0_.refs_15_), channel_id=1, source_target_pairs={{4,0},{5,1},{8,4},{9,5},{12,8},{13,9},{14,12},{15,13},{10,14},{11,... | collective-permute-start | bytes 786440 | tf_op jit(solution)/shard_map/ppermute | solution.py:502
  31.0 2.3 %collective-permute-done.4.refs_1_.refs_12_ = bf16[512,256]{1,0:T(8,128)(2,1)S(1)} collective-permute-done((bf16[512,256]{1,0:T(8,128)(2,1)S(1)}, bf16[512,256]{1,0:T(8,128)(2,1)S(1)}, u32[]{:S(2)}, u32[]{:S(2)}) %collective-permute-start.4) | collective-permute-done | bytes 262176 | tf_op jit(solution)/shard_map/ppermute | solution.py:502
  41.0 3.5 %collective-permute-done.6.refs_1_.refs_12_ = bf16[512,256]{1,0:T(8,128)(2,1)S(1)} collective-permute-done((bf16[512,256]{1,0:T(8,128)(2,1)S(1)}, bf16[512,256]{1,0:T(8,128)(2,1)S(1)}, u32[]{:S(2)}, u32[]{:S(2)}) %collective-permute-start.6) | collective-permute-done | bytes 262176 | tf_op jit(solution)/shard_map/ppermute | solution.py:502
  46.6 2.3 %shard_map.119 = (f32[2,1,1280]{2,1,0:T(1,128)S(1)}, f32[2,1,1280]{2,1,0:T(1,128)S(1)}) custom-call(s32[32]{0:T(128)S(1)} %get-tuple-element.133.plan, bf16[2,128,1280]{2,1,0:T(8,128)(2,1)S(1)} %get-tuple-element.128.qt_ref.refs_7_.refs_6_, f32[2,1,1280]{2,1,0:T(1,128)S(1)} %get-tuple-element.148.top_in, f32[2,1,1280]{2,1,0:T(1,128)S(1)} %get-tuple-element.149.sum_in, ...), custom_call_target="tpu_custom_call" | custom-call | bytes 8388608 | tf_op jit(solution)/shard_map/pallas_call | solution.py:193
  49.0 2.4 %shard_map.115 = (f32[2,1,1280]{2,1,0:T(1,128)S(1)}, f32[2,1,1280]{2,1,0:T(1,128)S(1)}) custom-call(s32[32]{0:T(128)S(1)} %get-tuple-element.104.plan, bf16[2,128,1280]{2,1,0:T(8,128)(2,1)S(1)} %get-tuple-element.105.qt_ref.refs_0_, f32[2,1,1280]{2,1,0:T(1,128)S(1)} %get-tuple-element.124.top_in, f32[2,1,1280]{2,1,0:T(1,128)S(1)} %get-tuple-element.125.sum_in, ...), custom_call_target="tpu_custom_call" | custom-call | bytes 8388608 | tf_op jit(solution)/shard_map/pallas_call | solution.py:193
  51.4 8.4 %shard_map.120 = (bf16[1,512,256]{2,1,0:T(8,128)(2,1)}, bf16[1,512,256]{2,1,0:T(8,128)(2,1)}, bf16[2,256,256]{2,1,0:T(8,128)(2,1)S(1)}, bf16[2,256,256]{2,1,0:T(...) custom-call(s32[32]{0:T(128)S(1)} %get-tuple-element.104.plan, ...), custom_call_target="tpu_custom_call" | custom-call | flops 8589934592 | bytes 16777216 | tf_op jit(solution)/shard_map/pallas_call | solution.py:395
  59.9 2.0 %collective-permute-start.19 = (bf16[2,256,256]{2,1,0:T(8,128)(2,1)S(1)}, bf16[2,256,256]{2,1,0:T(8,128)(2,1)S(1)}, u32[]{:S(2)}, u32[]{:S(2)}) collective-permute-start(bf16[2,256,256]{2,1,0:T(8,128)(2,1)S(1)} %get-tuple-element.167), channel_id=1, source_target_pairs={{4,0},{5,1},{8,4},{9,5},{12,8},{13,9},{14,12},{15,13},{10,14},{11,... | collective-permute-start | bytes 786440 | tf_op jit(solution)/shard_map/ppermute | solution.py:492
  61.9 8.3 %shard_map.121 = (bf16[2,512,256]{2,1,0:T(8,128)(2,1)S(1)}, bf16[2,512,256]{2,1,0:T(8,128)(2,1)S(1)}, f32[2,2,128,1280]{3,2,1,0:T(8,128)S(1)}) custom-call(s32[32]{0:T(128)S(1)} %get-tuple-element.104.plan, bf16[2,128,1280]{2,1,0:T(8,128)(2,1)S(1)} %get-tuple-element.105.qt_ref.refs_0_, bf16[2,128,1280]{2,1,0:T(8,128)(2,1)S(1)} %get-tuple-element.106.refs_1_, ...), custom_call_target="tpu_custom_call" | custom-call | flops 8589934592 | bytes 16777216 | tf_op jit(solution)/shard_map/pallas_call | solution.py:395
  70.4 2.0 %collective-permute-start.20 = (bf16[512,256]{1,0:T(8,128)(2,1)S(1)}, bf16[512,256]{1,0:T(8,128)(2,1)S(1)}, u32[]{:S(2)}, u32[]{:S(2)}) collective-permute-start(bf16[512,256]{1,0:T(8,128)(2,1)S(1)} %get-tuple-element.172), channel_id=1, source_target_pairs={{0,4},{1,5},{4,8},{5,9},{8,12},{9,13},{12,14},{13,15},{14,10},{15,... | collective-permute-start | bytes 786440 | tf_op jit(solution)/shard_map/ppermute | solution.py:492
  72.6 2.0 %collective-permute-start.24 = (bf16[512,256]{1,0:T(8,128)(2,1)S(1)}, bf16[512,256]{1,0:T(8,128)(2,1)S(1)}, u32[]{:S(2)}, u32[]{:S(2)}) collective-permute-start(bf16[512,256]{1,0:T(8,128)(2,1)S(1)} %get-tuple-element.204), channel_id=1, source_target_pairs={{0,4},{1,5},{4,8},{5,9},{8,12},{9,13},{12,14},{13,15},{14,10},{15,... | collective-permute-start | bytes 786440 | tf_op jit(solution)/shard_map/ppermute | solution.py:492
  74.6 4.6 %shard_map.122 = (bf16[2,512,256]{2,1,0:T(8,128)(2,1)S(1)}, bf16[2,512,256]{2,1,0:T(8,128)(2,1)S(1)}, f32[2,2,128,1280]{3,2,1,0:T(8,128)S(1)}) custom-call(s32[32]{0:T(128)S(1)} %get-tuple-element.104.plan, bf16[2,128,1280]{2,1,0:T(8,128)(2,1)S(1)} %get-tuple-element.105.qt_ref.refs_0_, bf16[2,128,1280]{2,1,0:T(8,128)(2,1)S(1)} %get-tuple-element.106.refs_1_, ...), custom_call_target="tpu_custom_call" | custom-call | flops 8589934592 | bytes 16777216 | tf_op jit(solution)/shard_map/pallas_call | solution.py:395
  80.8 2.4 %collective-permute-start.22 = (bf16[512,256]{1,0:T(8,128)(2,1)S(1)}, bf16[512,256]{1,0:T(8,128)(2,1)S(1)}, u32[]{:S(2)}, u32[]{:S(2)}) collective-permute-start(bf16[512,256]{1,0:T(8,128)(2,1)S(1)} %get-tuple-element.179), channel_id=1, source_target_pairs={{0,4},{1,5},{4,8},{5,9},{8,12},{9,13},{12,14},{13,15},{14,10},{15,... | collective-permute-start | bytes 786440 | tf_op jit(solution)/shard_map/ppermute | solution.py:492
  87.2 4.6 %shard_map.123 = (bf16[2,512,256]{2,1,0:T(8,128)(2,1)S(1)}, bf16[2,512,256]{2,1,0:T(8,128)(2,1)S(1)}, f32[2,2,128,1280]{3,2,1,0:T(8,128)S(1)}) custom-call(s32[32]{0:T(128)S(1)} %get-tuple-element.104.plan, bf16[2,128,1280]{2,1,0:T(8,128)(2,1)S(1)} %get-tuple-element.105.qt_ref.refs_0_, bf16[2,128,1280]{2,1,0:T(8,128)(2,1)S(1)} %get-tuple-element.106.refs_1_, ...), custom_call_target="tpu_custom_call" | custom-call | flops 8589934592 | bytes 16777216 | tf_op jit(solution)/shard_map/pallas_call | solution.py:395
  92.7 2.0 %collective-permute-start.31 = (bf16[512,256]{1,0:T(8,128)(2,1)S(1)}, bf16[512,256]{1,0:T(8,128)(2,1)S(1)}, u32[]{:S(2)}, u32[]{:S(2)}) collective-permute-start(bf16[512,256]{1,0:T(8,128)(2,1)S(1)} %get-tuple-element.191), channel_id=1, source_target_pairs={{4,0},{5,1},{8,4},{9,5},{12,8},{13,9},{14,12},{15,13},{10,14},{11,... | collective-permute-start | bytes 786440 | tf_op jit(solution)/shard_map/ppermute | solution.py:492
  94.7 3.4 %collective-permute-done.29 = bf16[512,256]{1,0:T(8,128)(2,1)S(1)} collective-permute-done((bf16[512,256]{1,0:T(8,128)(2,1)S(1)}, bf16[512,256]{1,0:T(8,128)(2,1)S(1)}, u32[]{:S(2)}, u32[]{:S(2)}) %collective-permute-start.29) | collective-permute-done | bytes 262176 | tf_op jit(solution)/shard_map/ppermute | solution.py:492
  98.3 2.0 %collective-permute-start.26 = (bf16[512,256]{1,0:T(8,128)(2,1)S(1)}, bf16[512,256]{1,0:T(8,128)(2,1)S(1)}, u32[]{:S(2)}, u32[]{:S(2)}) collective-permute-start(bf16[512,256]{1,0:T(8,128)(2,1)S(1)} %get-tuple-element.200), channel_id=1, source_target_pairs={{0,4},{1,5},{4,8},{5,9},{8,12},{9,13},{12,14},{13,15},{14,10},{15,... | collective-permute-start | bytes 786440 | tf_op jit(solution)/shard_map/ppermute | solution.py:492
  100.3 5.9 %shard_map.124 = (bf16[1,512,256]{2,1,0:T(8,128)(2,1)S(1)}, bf16[1,512,256]{2,1,0:T(8,128)(2,1)S(1)}, bf16[256,1280]{1,0:T(8,128)(2,1)S(1)}, bf16[256,1280]{1,0:T(8,128)(2,1)S(1)}) custom-call(s32[32]{0:T(128)S(1)} %get-tuple-element.104.plan, bf16[2,128,1280]{2,1,0:T(8,128)(2,1)S(1)} %get-tuple-element.105.qt_ref.refs_0_, ...), custom_call_target="tpu_custom_call" | custom-call | flops 8589934592 | bytes 16777216 | tf_op jit(solution)/shard_map/pallas_call | solution.py:395
  (99 shorter events, 30.1 us)
Async XLA Ops:
  4.6 9.9 %collective-permute-start.9 = (bf16[512,256]{1,0:T(8,128)(2,1)S(1)}, bf16[512,256]{1,0:T(8,128)(2,1)S(1)}, u32[]{:S(2)}, u32[]{:S(2)}) collective-permute-start(bf16[512,256]{1,0:T(8,128)(2,1)S(1)} %pad_maximum_fusion.3.block.refs_13_), channel_id=1, source_target_pairs={{4,0},{5,1},{8,4},{9,5},{12,8},{13,9},{14,12},{15,13},{10,14},{11,... | collective-permute-start | bytes 786440 | tf_op jit(solution)/shard_map/ppermute | solution.py:502
  7.3 9.2 %collective-permute-start.8 = (bf16[512,256]{1,0:T(8,128)(2,1)S(1)}, bf16[512,256]{1,0:T(8,128)(2,1)S(1)}, u32[]{:S(2)}, u32[]{:S(2)}) collective-permute-start(bf16[512,256]{1,0:T(8,128)(2,1)S(1)} %pad_maximum_fusion.3.block.refs_13_), channel_id=1, source_target_pairs={{0,4},{1,5},{4,8},{5,9},{8,12},{9,13},{12,14},{13,15},{14,10},{15,... | collective-permute-start | bytes 786440 | tf_op jit(solution)/shard_map/ppermute | solution.py:502
  7.4 15.1 %collective-permute-start.3 = (bf16[512,256]{1,0:T(8,128)(2,1)S(1)}, bf16[512,256]{1,0:T(8,128)(2,1)S(1)}, u32[]{:S(2)}, u32[]{:S(2)}) collective-permute-start(bf16[512,256]{1,0:T(8,128)(2,1)S(1)} %pad_maximum_fusion.2.block.refs_12_), channel_id=1, source_target_pairs={{4,0},{5,1},{8,4},{9,5},{12,8},{13,9},{14,12},{15,13},{10,14},{11,... | collective-permute-start | bytes 786440 | tf_op jit(solution)/shard_map/ppermute | solution.py:502
  9.4 13.2 %collective-permute-start.2 = (bf16[512,256]{1,0:T(8,128)(2,1)S(1)}, bf16[512,256]{1,0:T(8,128)(2,1)S(1)}, u32[]{:S(2)}, u32[]{:S(2)}) collective-permute-start(bf16[512,256]{1,0:T(8,128)(2,1)S(1)} %pad_maximum_fusion.2.block.refs_12_), channel_id=1, source_target_pairs={{0,4},{1,5},{4,8},{5,9},{8,12},{9,13},{12,14},{13,15},{14,10},{15,... | collective-permute-start | bytes 786440 | tf_op jit(solution)/shard_map/ppermute | solution.py:502
  16.4 11.2 %collective-permute-start.10 = (bf16[512,256]{1,0:T(8,128)(2,1)S(1)}, bf16[512,256]{1,0:T(8,128)(2,1)S(1)}, u32[]{:S(2)}, u32[]{:S(2)}) collective-permute-start(bf16[512,256]{1,0:T(8,128)(2,1)S(1)} %collective-permute-done.8.refs_1_.refs_14_), channel_id=1, source_target_pairs={{0,4},{1,5},{4,8},{5,9},{8,12},{9,13},{12,14},{13,15},{14,10},{15,... | collective-permute-start | bytes 786440 | tf_op jit(solution)/shard_map/ppermute | solution.py:502
  16.5 11.2 %collective-permute-start.11 = (bf16[512,256]{1,0:T(8,128)(2,1)S(1)}, bf16[512,256]{1,0:T(8,128)(2,1)S(1)}, u32[]{:S(2)}, u32[]{:S(2)}) collective-permute-start(bf16[512,256]{1,0:T(8,128)(2,1)S(1)} %collective-permute-done.9.refs_0_.refs_15_), channel_id=1, source_target_pairs={{4,0},{5,1},{8,4},{9,5},{12,8},{13,9},{14,12},{15,13},{10,14},{11,... | collective-permute-start | bytes 786440 | tf_op jit(solution)/shard_map/ppermute | solution.py:502
  22.6 10.7 %collective-permute-start.4 = (bf16[512,256]{1,0:T(8,128)(2,1)S(1)}, bf16[512,256]{1,0:T(8,128)(2,1)S(1)}, u32[]{:S(2)}, u32[]{:S(2)}) collective-permute-start(bf16[512,256]{1,0:T(8,128)(2,1)S(1)} %collective-permute-done.2.refs_1_.refs_12_), channel_id=1, source_target_pairs={{0,4},{1,5},{4,8},{5,9},{8,12},{9,13},{12,14},{13,15},{14,10},{15,... | collective-permute-start | bytes 786440 | tf_op jit(solution)/shard_map/ppermute | solution.py:502
  22.7 10.6 %collective-permute-start.5 = (bf16[512,256]{1,0:T(8,128)(2,1)S(1)}, bf16[512,256]{1,0:T(8,128)(2,1)S(1)}, u32[]{:S(2)}, u32[]{:S(2)}) collective-permute-start(bf16[512,256]{1,0:T(8,128)(2,1)S(1)} %collective-permute-done.3.refs_0_.refs_13_), channel_id=1, source_target_pairs={{4,0},{5,1},{8,4},{9,5},{12,8},{13,9},{14,12},{15,13},{10,14},{11,... | collective-permute-start | bytes 786440 | tf_op jit(solution)/shard_map/ppermute | solution.py:502
  27.7 11.2 %collective-permute-start.12 = (bf16[512,256]{1,0:T(8,128)(2,1)S(1)}, bf16[512,256]{1,0:T(8,128)(2,1)S(1)}, u32[]{:S(2)}, u32[]{:S(2)}) collective-permute-start(bf16[512,256]{1,0:T(8,128)(2,1)S(1)} %collective-permute-done.10.refs_1_.refs_14_), channel_id=1, source_target_pairs={{0,4},{1,5},{4,8},{5,9},{8,12},{9,13},{12,14},{13,15},{14,10},{15,... | collective-permute-start | bytes 786440 | tf_op jit(solution)/shard_map/ppermute | solution.py:502
  27.8 11.1 %collective-permute-start.13 = (bf16[512,256]{1,0:T(8,128)(2,1)S(1)}, bf16[512,256]{1,0:T(8,128)(2,1)S(1)}, u32[]{:S(2)}, u32[]{:S(2)}) collective-permute-start(bf16[512,256]{1,0:T(8,128)(2,1)S(1)} %collective-permute-done.11.refs_0_.refs_15_), channel_id=1, source_target_pairs={{4,0},{5,1},{8,4},{9,5},{12,8},{13,9},{14,12},{15,13},{10,14},{11,... | collective-permute-start | bytes 786440 | tf_op jit(solution)/shard_map/ppermute | solution.py:502
  33.3 11.2 %collective-permute-start.6 = (bf16[512,256]{1,0:T(8,128)(2,1)S(1)}, bf16[512,256]{1,0:T(8,128)(2,1)S(1)}, u32[]{:S(2)}, u32[]{:S(2)}) collective-permute-start(bf16[512,256]{1,0:T(8,128)(2,1)S(1)} %collective-permute-done.4.refs_1_.refs_12_), channel_id=1, source_target_pairs={{0,4},{1,5},{4,8},{5,9},{8,12},{9,13},{12,14},{13,15},{14,10},{15,... | collective-permute-start | bytes 786440 | tf_op jit(solution)/shard_map/ppermute | solution.py:502
  34.0 10.5 %collective-permute-start.7 = (bf16[512,256]{1,0:T(8,128)(2,1)S(1)}, bf16[512,256]{1,0:T(8,128)(2,1)S(1)}, u32[]{:S(2)}, u32[]{:S(2)}) collective-permute-start(bf16[512,256]{1,0:T(8,128)(2,1)S(1)} %collective-permute-done.5.refs_0_.refs_13_), channel_id=1, source_target_pairs={{4,0},{5,1},{8,4},{9,5},{12,8},{13,9},{14,12},{15,13},{10,14},{11,... | collective-permute-start | bytes 786440 | tf_op jit(solution)/shard_map/ppermute | solution.py:502
  39.0 12.4 %collective-permute-start.17 = (bf16[256,256]{1,0:T(8,128)(2,1)S(1)}, bf16[256,256]{1,0:T(8,128)(2,1)S(1)}, u32[]{:S(2)}, u32[]{:S(2)}) collective-permute-start(bf16[256,256]{1,0:T(8,128)(2,1)S(1)} %slice.69), channel_id=1, source_target_pairs={{4,0},{5,1},{8,4},{9,5},{12,8},{13,9},{14,12},{15,13},{10,14},{11,... | collective-permute-start | bytes 393224 | tf_op jit(solution)/shard_map/ppermute | solution.py:513
  40.7 10.7 %collective-permute-start.16 = (bf16[256,256]{1,0:T(8,128)(2,1)S(1)}, bf16[256,256]{1,0:T(8,128)(2,1)S(1)}, u32[]{:S(2)}, u32[]{:S(2)}) collective-permute-start(bf16[256,256]{1,0:T(8,128)(2,1)S(1)} %slice.68), channel_id=1, source_target_pairs={{0,4},{1,5},{4,8},{5,9},{8,12},{9,13},{12,14},{13,15},{14,10},{15,... | collective-permute-start | bytes 393224 | tf_op jit(solution)/shard_map/ppermute | solution.py:513
  59.8 10.4 %collective-permute-start.18 = (bf16[2,256,256]{2,1,0:T(8,128)(2,1)S(1)}, bf16[2,256,256]{2,1,0:T(8,128)(2,1)S(1)}, u32[]{:S(2)}, u32[]{:S(2)}) collective-permute-start(bf16[2,256,256]{2,1,0:T(8,128)(2,1)S(1)} %get-tuple-element.165), channel_id=1, source_target_pairs={{0,4},{1,5},{4,8},{5,9},{8,12},{9,13},{12,14},{13,15},{14,10},{15,... | collective-permute-start | bytes 786440 | tf_op jit(solution)/shard_map/ppermute | solution.py:492
  59.9 10.4 %collective-permute-start.19 = (bf16[2,256,256]{2,1,0:T(8,128)(2,1)S(1)}, bf16[2,256,256]{2,1,0:T(8,128)(2,1)S(1)}, u32[]{:S(2)}, u32[]{:S(2)}) collective-permute-start(bf16[2,256,256]{2,1,0:T(8,128)(2,1)S(1)} %get-tuple-element.167), channel_id=1, source_target_pairs={{4,0},{5,1},{8,4},{9,5},{12,8},{13,9},{14,12},{15,13},{10,14},{11,... | collective-permute-start | bytes 786440 | tf_op jit(solution)/shard_map/ppermute | solution.py:492
  72.6 12.4 %collective-permute-start.28 = (bf16[512,256]{1,0:T(8,128)(2,1)S(1)}, bf16[512,256]{1,0:T(8,128)(2,1)S(1)}, u32[]{:S(2)}, u32[]{:S(2)}) collective-permute-start(bf16[512,256]{1,0:T(8,128)(2,1)S(1)} %get-tuple-element.203), channel_id=1, source_target_pairs={{4,0},{5,1},{8,4},{9,5},{12,8},{13,9},{14,12},{15,13},{10,14},{11,... | collective-permute-start | bytes 786440 | tf_op jit(solution)/shard_map/ppermute | solution.py:492
  72.6 12.3 %collective-permute-start.24 = (bf16[512,256]{1,0:T(8,128)(2,1)S(1)}, bf16[512,256]{1,0:T(8,128)(2,1)S(1)}, u32[]{:S(2)}, u32[]{:S(2)}) collective-permute-start(bf16[512,256]{1,0:T(8,128)(2,1)S(1)} %get-tuple-element.204), channel_id=1, source_target_pairs={{0,4},{1,5},{4,8},{5,9},{8,12},{9,13},{12,14},{13,15},{14,10},{15,... | collective-permute-start | bytes 786440 | tf_op jit(solution)/shard_map/ppermute | solution.py:492
  80.8 11.0 %collective-permute-start.22 = (bf16[512,256]{1,0:T(8,128)(2,1)S(1)}, bf16[512,256]{1,0:T(8,128)(2,1)S(1)}, u32[]{:S(2)}, u32[]{:S(2)}) collective-permute-start(bf16[512,256]{1,0:T(8,128)(2,1)S(1)} %get-tuple-element.179), channel_id=1, source_target_pairs={{0,4},{1,5},{4,8},{5,9},{8,12},{9,13},{12,14},{13,15},{14,10},{15,... | collective-permute-start | bytes 786440 | tf_op jit(solution)/shard_map/ppermute | solution.py:492
  83.2 9.2 %collective-permute-start.23 = (bf16[512,256]{1,0:T(8,128)(2,1)S(1)}, bf16[512,256]{1,0:T(8,128)(2,1)S(1)}, u32[]{:S(2)}, u32[]{:S(2)}) collective-permute-start(bf16[512,256]{1,0:T(8,128)(2,1)S(1)} %get-tuple-element.181), channel_id=1, source_target_pairs={{4,0},{5,1},{8,4},{9,5},{12,8},{13,9},{14,12},{15,13},{10,14},{11,... | collective-permute-start | bytes 786440 | tf_op jit(solution)/shard_map/ppermute | solution.py:492
  85.1 13.0 %collective-permute-start.29 = (bf16[512,256]{1,0:T(8,128)(2,1)S(1)}, bf16[512,256]{1,0:T(8,128)(2,1)S(1)}, u32[]{:S(2)}, u32[]{:S(2)}) collective-permute-start(bf16[512,256]{1,0:T(8,128)(2,1)S(1)} %get-tuple-element.201), channel_id=1, source_target_pairs={{4,0},{5,1},{8,4},{9,5},{12,8},{13,9},{14,12},{15,13},{10,14},{11,... | collective-permute-start | bytes 786440 | tf_op jit(solution)/shard_map/ppermute | solution.py:492
  85.4 12.6 %collective-permute-start.25 = (bf16[512,256]{1,0:T(8,128)(2,1)S(1)}, bf16[512,256]{1,0:T(8,128)(2,1)S(1)}, u32[]{:S(2)}, u32[]{:S(2)}) collective-permute-start(bf16[512,256]{1,0:T(8,128)(2,1)S(1)} %get-tuple-element.202), channel_id=1, source_target_pairs={{0,4},{1,5},{4,8},{5,9},{8,12},{9,13},{12,14},{13,15},{14,10},{15,... | collective-permute-start | bytes 786440 | tf_op jit(solution)/shard_map/ppermute | solution.py:492
  92.6 13.7 %collective-permute-start.27 = (bf16[512,256]{1,0:T(8,128)(2,1)S(1)}, bf16[512,256]{1,0:T(8,128)(2,1)S(1)}, u32[]{:S(2)}, u32[]{:S(2)}) collective-permute-start(bf16[512,256]{1,0:T(8,128)(2,1)S(1)} %get-tuple-element.190), channel_id=1, source_target_pairs={{0,4},{1,5},{4,8},{5,9},{8,12},{9,13},{12,14},{13,15},{14,10},{15,... | collective-permute-start | bytes 786440 | tf_op jit(solution)/shard_map/ppermute | solution.py:492
  92.7 13.6 %collective-permute-start.31 = (bf16[512,256]{1,0:T(8,128)(2,1)S(1)}, bf16[512,256]{1,0:T(8,128)(2,1)S(1)}, u32[]{:S(2)}, u32[]{:S(2)}) collective-permute-start(bf16[512,256]{1,0:T(8,128)(2,1)S(1)} %get-tuple-element.191), channel_id=1, source_target_pairs={{4,0},{5,1},{8,4},{9,5},{12,8},{13,9},{14,12},{15,13},{10,14},{11,... | collective-permute-start | bytes 786440 | tf_op jit(solution)/shard_map/ppermute | solution.py:492
  (18 other events, 88.4 us)

commit v8 on v7

--- a/solution.py
+++ b/solution.py
@@ -230,25 +230,32 @@
     rows = acc_ref.shape[1]
     slots = stage_ref.shape[0]
 
+    for slot, offset in enumerate(offsets):
+        offset_ref[slot] = offset
+
+    def sees(side, i):
+        return plan[side * 2 * chips + offset_ref[i // 2] * 2 + i % 2]
+
+    def seen(i):
+        return (sees(0, i) > 0) | (sees(1, i) > 0)
+
     pairs = []
-    for head in range(HALF):
-        for slot, offset in enumerate(offsets):
-            offset_ref[slot] = offset
-            if offset == far:
+    for slot, offset in enumerate(offsets):
+        if offset == far:
+            for head in range(HALF):
                 pairs.append((blocks[head][0], kv_ref.at[slot, head, :rows]))
                 pairs.append((blocks[head][1], kv_ref.at[slot, head, rows:]))
-            else:
+            continue
+
+        @pl.when(seen(2 * slot) | seen(2 * slot + 1))
+        def _():
+            for head in range(HALF):
                 pltpu.make_async_copy(
                     blocks[head][slot + first], kv_ref.at[slot, head], kv_sems.at[slot, head]
                 ).start()
+
     copies = run_copies(pairs, sems)
     zero_ref[...] = jnp.zeros_like(zero_ref)
-
-    def sees(side, i):
-        return plan[side * 2 * chips + offset_ref[i // 2] * 2 + i % 2]
-
-    def seen(i):
-        return (sees(0, i) > 0) | (sees(1, i) > 0)
 
     def send(i, sources, sem_of):
         at_block, half = i // 2, i % 2
@@ -301,7 +308,9 @@
         here = pl.ds(pl.multiple_of(half * rows, rows), rows)
 
         if len(offsets) > first:
-            @pl.when((half == 0) & (offset_ref[at_block] != far))
+            either = seen(2 * at_block) | seen(2 * at_block + 1)
+
+            @pl.when((half == 0) & (offset_ref[at_block] != far) & either)
             def _():
                 for head in range(HALF):
                     pltpu.make_async_copy(

time: 112 us -> 113 us (level)
  Pallas kernels: 51.2 us -> 45.7 us
  starting transfers between devices: 33.8 us -> 38.9 us
  waiting for transfers between devices: 21.3 us -> 22.5 us
    ppermute x14, starting transfers between devices: 14.9 us -> 20 us  [shift(): return [lax.ppermute(array, 'leaf', ring) for array in arrays]]
    pallas_call x5, Pallas kernels: 31.9 us -> 28.5 us  [gradients(): pl.pallas_call(functools.partial(grads_kernel, chips, tuple(offsets), fir...]
    pallas_call x6, Pallas kernels: 9.84 us -> 6.67 us  [measure(): pl.pallas_call(functools.partial(measure_kernel, offsets), in_specs=[SMEM...]
    ppermute x6, waiting for transfers between devices: 10.5 us -> 12.1 us  [local(): lax.ppermute(up, 'leaf', right)]
  transfers between devices with their start and end apart: 35 -> 35, of which waited for: 13 -> 15; matrix products, arithmetic and copies ran while one was open for 1% -> 1% of each run, Pallas kernels for 38% -> 32%
where the time goes in v8:
time: 113 us; the launch traced here: 111 us
  Pallas kernels  45.7 us (40%)
  starting transfers between devices  38.9 us (34%)
  waiting for transfers between devices  22.5 us (20%)
  local copies, waits for them, and re-layouts  1.62 us (1%)
  between operations  1.31 us (1%)
    pallas_call x5, Pallas kernels, gradients(): pl.pallas_call(functools.partial(grads_kernel, chips, tuple(offsets), fir...  28.5 us
    ppermute x14, starting transfers between devices, shift(): return [lax.ppermute(array, 'leaf', ring) for array in arrays]  20 us
    ppermute x6, waiting for transfers between devices, local(): lax.ppermute(up, 'leaf', right)  12.1 us
    ppermute x6, starting transfers between devices, local(): lax.ppermute(down, 'leaf', left)  11.9 us
    pallas_call x2, Pallas kernels, prepare(): pl.pallas_call(functools.partial(prepare_kernel, head), in_specs=[SMEM] *...  9.22 us
    ppermute x14, waiting for transfers between devices, shift(): return [lax.ppermute(array, 'leaf', ring) for array in arrays]  6.68 us
    pallas_call x6, Pallas kernels, measure(): pl.pallas_call(functools.partial(measure_kernel, offsets), in_specs=[SMEM...  6.67 us
    ppermute x2, starting transfers between devices, local(): lax.ppermute(down[rows:], 'leaf', left)  3.17 us
  transfers between devices with their start and end apart: 35, of which 15 were waited for; matrix products, arithmetic and copies ran while one was open for 1% of the time, Pallas kernels for 32%

profile of v8, /device:TPU:0, one launch (start us, length us, event | category | flops | bytes accessed | tf_op | source)
XLA Modules:
  0.0 111.1 jit_solution(6646670502080701409)
XLA Ops:
  4.6 2.7 %collective-permute-start.9 = (bf16[512,256]{1,0:T(8,128)(2,1)S(1)}, bf16[512,256]{1,0:T(8,128)(2,1)S(1)}, u32[]{:S(2)}, u32[]{:S(2)}) collective-permute-start(bf16[512,256]{1,0:T(8,128)(2,1)S(1)} %pad_maximum_fusion.3.block.refs_13_), channel_id=1, source_target_pairs={{4,0},{5,1},{8,4},{9,5},{12,8},{13,9},{14,12},{15,13},{10,14},{11,... | collective-permute-start | bytes 786440 | tf_op jit(solution)/shard_map/ppermute | solution.py:511
  7.4 2.0 %collective-permute-start.3 = (bf16[512,256]{1,0:T(8,128)(2,1)S(1)}, bf16[512,256]{1,0:T(8,128)(2,1)S(1)}, u32[]{:S(2)}, u32[]{:S(2)}) collective-permute-start(bf16[512,256]{1,0:T(8,128)(2,1)S(1)} %pad_maximum_fusion.2.block.refs_12_), channel_id=1, source_target_pairs={{4,0},{5,1},{8,4},{9,5},{12,8},{13,9},{14,12},{15,13},{10,14},{11,... | collective-permute-start | bytes 786440 | tf_op jit(solution)/shard_map/ppermute | solution.py:511
  9.5 4.6 %shard_map.116 = (s32[32]{0:T(128)S(1)}, bf16[2,128,1280]{2,1,0:T(8,128)(2,1)S(1)}, bf16[2,128,1280]{2,1,0:T(8,128)(2,1)S(1)}, bf16[2,1280,128]{2,1,0:T(8,128)(2...) custom-call(s32[1]{0:T(128)} %bitcast.me_ref, ...), custom_call_target="tpu_custom_call" | custom-call | bytes 12582912 | tf_op jit(solution)/shard_map/pallas_call | solution.py:157
  14.5 2.0 %collective-permute-done.8.refs_1_.refs_14_ = bf16[512,256]{1,0:T(8,128)(2,1)S(1)} collective-permute-done((bf16[512,256]{1,0:T(8,128)(2,1)S(1)}, bf16[512,256]{1,0:T(8,128)(2,1)S(1)}, u32[]{:S(2)}, u32[]{:S(2)}) %collective-permute-start.8) | collective-permute-done | bytes 262176 | tf_op jit(solution)/shard_map/ppermute | solution.py:511
  16.5 1.9 %collective-permute-start.11 = (bf16[512,256]{1,0:T(8,128)(2,1)S(1)}, bf16[512,256]{1,0:T(8,128)(2,1)S(1)}, u32[]{:S(2)}, u32[]{:S(2)}) collective-permute-start(bf16[512,256]{1,0:T(8,128)(2,1)S(1)} %collective-permute-done.9.refs_0_.refs_15_), channel_id=1, source_target_pairs={{4,0},{5,1},{8,4},{9,5},{12,8},{13,9},{14,12},{15,13},{10,14},{11,... | collective-permute-start | bytes 786440 | tf_op jit(solution)/shard_map/ppermute | solution.py:511
  18.5 4.6 %shard_map.112 = (s32[32]{0:T(128)S(1)}, bf16[2,128,1280]{2,1,0:T(8,128)(2,1)S(1)}, bf16[2,128,1280]{2,1,0:T(8,128)(2,1)S(1)}, bf16[2,1280,128]{2,1,0:T(8,128)(2...) custom-call(s32[1]{0:T(128)} %bitcast.me_ref, ...), custom_call_target="tpu_custom_call" | custom-call | bytes 12582912 | tf_op jit(solution)/shard_map/pallas_call | solution.py:157
  23.2 2.0 %collective-permute-start.5 = (bf16[512,256]{1,0:T(8,128)(2,1)S(1)}, bf16[512,256]{1,0:T(8,128)(2,1)S(1)}, u32[]{:S(2)}, u32[]{:S(2)}) collective-permute-start(bf16[512,256]{1,0:T(8,128)(2,1)S(1)} %collective-permute-done.3.refs_0_.refs_13_), channel_id=1, source_target_pairs={{4,0},{5,1},{8,4},{9,5},{12,8},{13,9},{14,12},{15,13},{10,14},{11,... | collective-permute-start | bytes 786440 | tf_op jit(solution)/shard_map/ppermute | solution.py:511
  27.8 1.9 %collective-permute-start.13 = (bf16[512,256]{1,0:T(8,128)(2,1)S(1)}, bf16[512,256]{1,0:T(8,128)(2,1)S(1)}, u32[]{:S(2)}, u32[]{:S(2)}) collective-permute-start(bf16[512,256]{1,0:T(8,128)(2,1)S(1)} %collective-permute-done.11.refs_0_.refs_15_), channel_id=1, source_target_pairs={{4,0},{5,1},{8,4},{9,5},{12,8},{13,9},{14,12},{15,13},{10,14},{11,... | collective-permute-start | bytes 786440 | tf_op jit(solution)/shard_map/ppermute | solution.py:511
  30.5 2.8 %collective-permute-done.4.refs_1_.refs_12_ = bf16[512,256]{1,0:T(8,128)(2,1)S(1)} collective-permute-done((bf16[512,256]{1,0:T(8,128)(2,1)S(1)}, bf16[512,256]{1,0:T(8,128)(2,1)S(1)}, u32[]{:S(2)}, u32[]{:S(2)}) %collective-permute-start.4) | collective-permute-done | bytes 262176 | tf_op jit(solution)/shard_map/ppermute | solution.py:511
  36.9 2.1 %collective-permute-done.12.refs_1_.refs_14_ = bf16[512,256]{1,0:T(8,128)(2,1)S(1)} collective-permute-done((bf16[512,256]{1,0:T(8,128)(2,1)S(1)}, bf16[512,256]{1,0:T(8,128)(2,1)S(1)}, u32[]{:S(2)}, u32[]{:S(2)}) %collective-permute-start.12) | collective-permute-done | bytes 262176 | tf_op jit(solution)/shard_map/ppermute | solution.py:511
  41.0 3.5 %collective-permute-done.6.refs_1_.refs_12_ = bf16[512,256]{1,0:T(8,128)(2,1)S(1)} collective-permute-done((bf16[512,256]{1,0:T(8,128)(2,1)S(1)}, bf16[512,256]{1,0:T(8,128)(2,1)S(1)}, u32[]{:S(2)}, u32[]{:S(2)}) %collective-permute-start.6) | collective-permute-done | bytes 262176 | tf_op jit(solution)/shard_map/ppermute | solution.py:511
  46.6 1.8 %shard_map.119 = (f32[2,1,1280]{2,1,0:T(1,128)S(1)}, f32[2,1,1280]{2,1,0:T(1,128)S(1)}) custom-call(s32[32]{0:T(128)S(1)} %get-tuple-element.133.plan, bf16[2,128,1280]{2,1,0:T(8,128)(2,1)S(1)} %get-tuple-element.128.qt_ref.refs_7_.refs_6_, f32[2,1,1280]{2,1,0:T(1,128)S(1)} %get-tuple-element.148.top_in, f32[2,1,1280]{2,1,0:T(1,128)S(1)} %get-tuple-element.149.sum_in, ...), custom_call_target="tpu_custom_call" | custom-call | bytes 8388608 | tf_op jit(solution)/shard_map/pallas_call | solution.py:193
  48.5 1.8 %shard_map.115 = (f32[2,1,1280]{2,1,0:T(1,128)S(1)}, f32[2,1,1280]{2,1,0:T(1,128)S(1)}) custom-call(s32[32]{0:T(128)S(1)} %get-tuple-element.104.plan, bf16[2,128,1280]{2,1,0:T(8,128)(2,1)S(1)} %get-tuple-element.105.qt_ref.refs_0_, f32[2,1,1280]{2,1,0:T(1,128)S(1)} %get-tuple-element.124.top_in, f32[2,1,1280]{2,1,0:T(1,128)S(1)} %get-tuple-element.125.sum_in, ...), custom_call_target="tpu_custom_call" | custom-call | bytes 8388608 | tf_op jit(solution)/shard_map/pallas_call | solution.py:193
  51.0 8.4 %shard_map.120 = (bf16[1,512,256]{2,1,0:T(8,128)(2,1)}, bf16[1,512,256]{2,1,0:T(8,128)(2,1)}, bf16[2,256,256]{2,1,0:T(8,128)(2,1)S(1)}, bf16[2,256,256]{2,1,0:T(...) custom-call(s32[32]{0:T(128)S(1)} %get-tuple-element.104.plan, ...), custom_call_target="tpu_custom_call" | custom-call | flops 8589934592 | bytes 16777216 | tf_op jit(solution)/shard_map/pallas_call | solution.py:404
  61.5 6.6 %shard_map.121 = (bf16[2,512,256]{2,1,0:T(8,128)(2,1)S(1)}, bf16[2,512,256]{2,1,0:T(8,128)(2,1)S(1)}, f32[2,2,128,1280]{3,2,1,0:T(8,128)S(1)}) custom-call(s32[32]{0:T(128)S(1)} %get-tuple-element.104.plan, bf16[2,128,1280]{2,1,0:T(8,128)(2,1)S(1)} %get-tuple-element.105.qt_ref.refs_0_, bf16[2,128,1280]{2,1,0:T(8,128)(2,1)S(1)} %get-tuple-element.106.refs_1_, ...), custom_call_target="tpu_custom_call" | custom-call | flops 8589934592 | bytes 16777216 | tf_op jit(solution)/shard_map/pallas_call | solution.py:404
  68.3 2.9 %collective-permute-start.20 = (bf16[512,256]{1,0:T(8,128)(2,1)S(1)}, bf16[512,256]{1,0:T(8,128)(2,1)S(1)}, u32[]{:S(2)}, u32[]{:S(2)}) collective-permute-start(bf16[512,256]{1,0:T(8,128)(2,1)S(1)} %get-tuple-element.172), channel_id=1, source_target_pairs={{0,4},{1,5},{4,8},{5,9},{8,12},{9,13},{12,14},{13,15},{14,10},{15,... | collective-permute-start | bytes 786440 | tf_op jit(solution)/shard_map/ppermute | solution.py:501
  71.3 2.1 %collective-permute-start.24 = (bf16[512,256]{1,0:T(8,128)(2,1)S(1)}, bf16[512,256]{1,0:T(8,128)(2,1)S(1)}, u32[]{:S(2)}, u32[]{:S(2)}) collective-permute-start(bf16[512,256]{1,0:T(8,128)(2,1)S(1)} %get-tuple-element.204), channel_id=1, source_target_pairs={{0,4},{1,5},{4,8},{5,9},{8,12},{9,13},{12,14},{13,15},{14,10},{15,... | collective-permute-start | bytes 786440 | tf_op jit(solution)/shard_map/ppermute | solution.py:501
  73.4 2.7 %shard_map.122 = (bf16[2,512,256]{2,1,0:T(8,128)(2,1)S(1)}, bf16[2,512,256]{2,1,0:T(8,128)(2,1)S(1)}, f32[2,2,128,1280]{3,2,1,0:T(8,128)S(1)}) custom-call(s32[32]{0:T(128)S(1)} %get-tuple-element.104.plan, bf16[2,128,1280]{2,1,0:T(8,128)(2,1)S(1)} %get-tuple-element.105.qt_ref.refs_0_, bf16[2,128,1280]{2,1,0:T(8,128)(2,1)S(1)} %get-tuple-element.106.refs_1_, ...), custom_call_target="tpu_custom_call" | custom-call | flops 8589934592 | bytes 16777216 | tf_op jit(solution)/shard_map/pallas_call | solution.py:404
  82.9 2.3 %collective-permute-start.29 = (bf16[512,256]{1,0:T(8,128)(2,1)S(1)}, bf16[512,256]{1,0:T(8,128)(2,1)S(1)}, u32[]{:S(2)}, u32[]{:S(2)}) collective-permute-start(bf16[512,256]{1,0:T(8,128)(2,1)S(1)} %get-tuple-element.201), channel_id=1, source_target_pairs={{4,0},{5,1},{8,4},{9,5},{12,8},{13,9},{14,12},{15,13},{10,14},{11,... | collective-permute-start | bytes 786440 | tf_op jit(solution)/shard_map/ppermute | solution.py:501
  86.1 2.9 %shard_map.123 = (bf16[2,512,256]{2,1,0:T(8,128)(2,1)S(1)}, bf16[2,512,256]{2,1,0:T(8,128)(2,1)S(1)}, f32[2,2,128,1280]{3,2,1,0:T(8,128)S(1)}) custom-call(s32[32]{0:T(128)S(1)} %get-tuple-element.104.plan, bf16[2,128,1280]{2,1,0:T(8,128)(2,1)S(1)} %get-tuple-element.105.qt_ref.refs_0_, bf16[2,128,1280]{2,1,0:T(8,128)(2,1)S(1)} %get-tuple-element.106.refs_1_, ...), custom_call_target="tpu_custom_call" | custom-call | flops 8589934592 | bytes 16777216 | tf_op jit(solution)/shard_map/pallas_call | solution.py:404
  89.0 2.2 %collective-permute-done.23 = bf16[512,256]{1,0:T(8,128)(2,1)S(1)} collective-permute-done((bf16[512,256]{1,0:T(8,128)(2,1)S(1)}, bf16[512,256]{1,0:T(8,128)(2,1)S(1)}, u32[]{:S(2)}, u32[]{:S(2)}) %collective-permute-start.23) | collective-permute-done | bytes 262176 | tf_op jit(solution)/shard_map/ppermute | solution.py:501
  91.4 5.5 %collective-permute-start.27 = (bf16[512,256]{1,0:T(8,128)(2,1)S(1)}, bf16[512,256]{1,0:T(8,128)(2,1)S(1)}, u32[]{:S(2)}, u32[]{:S(2)}) collective-permute-start(bf16[512,256]{1,0:T(8,128)(2,1)S(1)} %get-tuple-element.190), channel_id=1, source_target_pairs={{0,4},{1,5},{4,8},{5,9},{8,12},{9,13},{12,14},{13,15},{14,10},{15,... | collective-permute-start | bytes 786440 | tf_op jit(solution)/shard_map/ppermute | solution.py:501
  97.2 2.1 %collective-permute-start.26 = (bf16[512,256]{1,0:T(8,128)(2,1)S(1)}, bf16[512,256]{1,0:T(8,128)(2,1)S(1)}, u32[]{:S(2)}, u32[]{:S(2)}) collective-permute-start(bf16[512,256]{1,0:T(8,128)(2,1)S(1)} %get-tuple-element.200), channel_id=1, source_target_pairs={{0,4},{1,5},{4,8},{5,9},{8,12},{9,13},{12,14},{13,15},{14,10},{15,... | collective-permute-start | bytes 786440 | tf_op jit(solution)/shard_map/ppermute | solution.py:501
  99.2 7.8 %shard_map.124 = (bf16[1,512,256]{2,1,0:T(8,128)(2,1)S(1)}, bf16[1,512,256]{2,1,0:T(8,128)(2,1)S(1)}, bf16[256,1280]{1,0:T(8,128)(2,1)S(1)}, bf16[256,1280]{1,0:T(8,128)(2,1)S(1)}) custom-call(s32[32]{0:T(128)S(1)} %get-tuple-element.104.plan, bf16[2,128,1280]{2,1,0:T(8,128)(2,1)S(1)} %get-tuple-element.105.qt_ref.refs_0_, ...), custom_call_target="tpu_custom_call" | custom-call | flops 8589934592 | bytes 16777216 | tf_op jit(solution)/shard_map/pallas_call | solution.py:404
  (99 shorter events, 30.4 us)
Async XLA Ops:
  4.6 9.9 %collective-permute-start.9 = (bf16[512,256]{1,0:T(8,128)(2,1)S(1)}, bf16[512,256]{1,0:T(8,128)(2,1)S(1)}, u32[]{:S(2)}, u32[]{:S(2)}) collective-permute-start(bf16[512,256]{1,0:T(8,128)(2,1)S(1)} %pad_maximum_fusion.3.block.refs_13_), channel_id=1, source_target_pairs={{4,0},{5,1},{8,4},{9,5},{12,8},{13,9},{14,12},{15,13},{10,14},{11,... | collective-permute-start | bytes 786440 | tf_op jit(solution)/shard_map/ppermute | solution.py:511
  7.3 9.2 %collective-permute-start.8 = (bf16[512,256]{1,0:T(8,128)(2,1)S(1)}, bf16[512,256]{1,0:T(8,128)(2,1)S(1)}, u32[]{:S(2)}, u32[]{:S(2)}) collective-permute-start(bf16[512,256]{1,0:T(8,128)(2,1)S(1)} %pad_maximum_fusion.3.block.refs_13_), channel_id=1, source_target_pairs={{0,4},{1,5},{4,8},{5,9},{8,12},{9,13},{12,14},{13,15},{14,10},{15,... | collective-permute-start | bytes 786440 | tf_op jit(solution)/shard_map/ppermute | solution.py:511
  7.4 15.7 %collective-permute-start.3 = (bf16[512,256]{1,0:T(8,128)(2,1)S(1)}, bf16[512,256]{1,0:T(8,128)(2,1)S(1)}, u32[]{:S(2)}, u32[]{:S(2)}) collective-permute-start(bf16[512,256]{1,0:T(8,128)(2,1)S(1)} %pad_maximum_fusion.2.block.refs_12_), channel_id=1, source_target_pairs={{4,0},{5,1},{8,4},{9,5},{12,8},{13,9},{14,12},{15,13},{10,14},{11,... | collective-permute-start | bytes 786440 | tf_op jit(solution)/shard_map/ppermute | solution.py:511
  9.4 13.7 %collective-permute-start.2 = (bf16[512,256]{1,0:T(8,128)(2,1)S(1)}, bf16[512,256]{1,0:T(8,128)(2,1)S(1)}, u32[]{:S(2)}, u32[]{:S(2)}) collective-permute-start(bf16[512,256]{1,0:T(8,128)(2,1)S(1)} %pad_maximum_fusion.2.block.refs_12_), channel_id=1, source_target_pairs={{0,4},{1,5},{4,8},{5,9},{8,12},{9,13},{12,14},{13,15},{14,10},{15,... | collective-permute-start | bytes 786440 | tf_op jit(solution)/shard_map/ppermute | solution.py:511
  16.4 11.2 %collective-permute-start.10 = (bf16[512,256]{1,0:T(8,128)(2,1)S(1)}, bf16[512,256]{1,0:T(8,128)(2,1)S(1)}, u32[]{:S(2)}, u32[]{:S(2)}) collective-permute-start(bf16[512,256]{1,0:T(8,128)(2,1)S(1)} %collective-permute-done.8.refs_1_.refs_14_), channel_id=1, source_target_pairs={{0,4},{1,5},{4,8},{5,9},{8,12},{9,13},{12,14},{13,15},{14,10},{15,... | collective-permute-start | bytes 786440 | tf_op jit(solution)/shard_map/ppermute | solution.py:511
  16.5 11.2 %collective-permute-start.11 = (bf16[512,256]{1,0:T(8,128)(2,1)S(1)}, bf16[512,256]{1,0:T(8,128)(2,1)S(1)}, u32[]{:S(2)}, u32[]{:S(2)}) collective-permute-start(bf16[512,256]{1,0:T(8,128)(2,1)S(1)} %collective-permute-done.9.refs_0_.refs_15_), channel_id=1, source_target_pairs={{4,0},{5,1},{8,4},{9,5},{12,8},{13,9},{14,12},{15,13},{10,14},{11,... | collective-permute-start | bytes 786440 | tf_op jit(solution)/shard_map/ppermute | solution.py:511
  23.1 10.2 %collective-permute-start.4 = (bf16[512,256]{1,0:T(8,128)(2,1)S(1)}, bf16[512,256]{1,0:T(8,128)(2,1)S(1)}, u32[]{:S(2)}, u32[]{:S(2)}) collective-permute-start(bf16[512,256]{1,0:T(8,128)(2,1)S(1)} %collective-permute-done.2.refs_1_.refs_12_), channel_id=1, source_target_pairs={{0,4},{1,5},{4,8},{5,9},{8,12},{9,13},{12,14},{13,15},{14,10},{15,... | collective-permute-start | bytes 786440 | tf_op jit(solution)/shard_map/ppermute | solution.py:511
  23.2 10.1 %collective-permute-start.5 = (bf16[512,256]{1,0:T(8,128)(2,1)S(1)}, bf16[512,256]{1,0:T(8,128)(2,1)S(1)}, u32[]{:S(2)}, u32[]{:S(2)}) collective-permute-start(bf16[512,256]{1,0:T(8,128)(2,1)S(1)} %collective-permute-done.3.refs_0_.refs_13_), channel_id=1, source_target_pairs={{4,0},{5,1},{8,4},{9,5},{12,8},{13,9},{14,12},{15,13},{10,14},{11,... | collective-permute-start | bytes 786440 | tf_op jit(solution)/shard_map/ppermute | solution.py:511
  27.7 11.2 %collective-permute-start.12 = (bf16[512,256]{1,0:T(8,128)(2,1)S(1)}, bf16[512,256]{1,0:T(8,128)(2,1)S(1)}, u32[]{:S(2)}, u32[]{:S(2)}) collective-permute-start(bf16[512,256]{1,0:T(8,128)(2,1)S(1)} %collective-permute-done.10.refs_1_.refs_14_), channel_id=1, source_target_pairs={{0,4},{1,5},{4,8},{5,9},{8,12},{9,13},{12,14},{13,15},{14,10},{15,... | collective-permute-start | bytes 786440 | tf_op jit(solution)/shard_map/ppermute | solution.py:511
  27.8 11.1 %collective-permute-start.13 = (bf16[512,256]{1,0:T(8,128)(2,1)S(1)}, bf16[512,256]{1,0:T(8,128)(2,1)S(1)}, u32[]{:S(2)}, u32[]{:S(2)}) collective-permute-start(bf16[512,256]{1,0:T(8,128)(2,1)S(1)} %collective-permute-done.11.refs_0_.refs_15_), channel_id=1, source_target_pairs={{4,0},{5,1},{8,4},{9,5},{12,8},{13,9},{14,12},{15,13},{10,14},{11,... | collective-permute-start | bytes 786440 | tf_op jit(solution)/shard_map/ppermute | solution.py:511
  33.3 11.2 %collective-permute-start.6 = (bf16[512,256]{1,0:T(8,128)(2,1)S(1)}, bf16[512,256]{1,0:T(8,128)(2,1)S(1)}, u32[]{:S(2)}, u32[]{:S(2)}) collective-permute-start(bf16[512,256]{1,0:T(8,128)(2,1)S(1)} %collective-permute-done.4.refs_1_.refs_12_), channel_id=1, source_target_pairs={{0,4},{1,5},{4,8},{5,9},{8,12},{9,13},{12,14},{13,15},{14,10},{15,... | collective-permute-start | bytes 786440 | tf_op jit(solution)/shard_map/ppermute | solution.py:511
  34.0 10.6 %collective-permute-start.7 = (bf16[512,256]{1,0:T(8,128)(2,1)S(1)}, bf16[512,256]{1,0:T(8,128)(2,1)S(1)}, u32[]{:S(2)}, u32[]{:S(2)}) collective-permute-start(bf16[512,256]{1,0:T(8,128)(2,1)S(1)} %collective-permute-done.5.refs_0_.refs_13_), channel_id=1, source_target_pairs={{4,0},{5,1},{8,4},{9,5},{12,8},{13,9},{14,12},{15,13},{10,14},{11,... | collective-permute-start | bytes 786440 | tf_op jit(solution)/shard_map/ppermute | solution.py:511
  39.0 11.4 %collective-permute-start.17 = (bf16[256,256]{1,0:T(8,128)(2,1)S(1)}, bf16[256,256]{1,0:T(8,128)(2,1)S(1)}, u32[]{:S(2)}, u32[]{:S(2)}) collective-permute-start(bf16[256,256]{1,0:T(8,128)(2,1)S(1)} %slice.69), channel_id=1, source_target_pairs={{4,0},{5,1},{8,4},{9,5},{12,8},{13,9},{14,12},{15,13},{10,14},{11,... | collective-permute-start | bytes 393224 | tf_op jit(solution)/shard_map/ppermute | solution.py:522
  40.7 9.6 %collective-permute-start.16 = (bf16[256,256]{1,0:T(8,128)(2,1)S(1)}, bf16[256,256]{1,0:T(8,128)(2,1)S(1)}, u32[]{:S(2)}, u32[]{:S(2)}) collective-permute-start(bf16[256,256]{1,0:T(8,128)(2,1)S(1)} %slice.68), channel_id=1, source_target_pairs={{0,4},{1,5},{4,8},{5,9},{8,12},{9,13},{12,14},{13,15},{14,10},{15,... | collective-permute-start | bytes 393224 | tf_op jit(solution)/shard_map/ppermute | solution.py:522
  71.2 11.3 %collective-permute-start.28 = (bf16[512,256]{1,0:T(8,128)(2,1)S(1)}, bf16[512,256]{1,0:T(8,128)(2,1)S(1)}, u32[]{:S(2)}, u32[]{:S(2)}) collective-permute-start(bf16[512,256]{1,0:T(8,128)(2,1)S(1)} %get-tuple-element.203), channel_id=1, source_target_pairs={{4,0},{5,1},{8,4},{9,5},{12,8},{13,9},{14,12},{15,13},{10,14},{11,... | collective-permute-start | bytes 786440 | tf_op jit(solution)/shard_map/ppermute | solution.py:501
  71.3 11.5 %collective-permute-start.24 = (bf16[512,256]{1,0:T(8,128)(2,1)S(1)}, bf16[512,256]{1,0:T(8,128)(2,1)S(1)}, u32[]{:S(2)}, u32[]{:S(2)}) collective-permute-start(bf16[512,256]{1,0:T(8,128)(2,1)S(1)} %get-tuple-element.204), channel_id=1, source_target_pairs={{0,4},{1,5},{4,8},{5,9},{8,12},{9,13},{12,14},{13,15},{14,10},{15,... | collective-permute-start | bytes 786440 | tf_op jit(solution)/shard_map/ppermute | solution.py:501
  79.3 9.7 %collective-permute-start.22 = (bf16[512,256]{1,0:T(8,128)(2,1)S(1)}, bf16[512,256]{1,0:T(8,128)(2,1)S(1)}, u32[]{:S(2)}, u32[]{:S(2)}) collective-permute-start(bf16[512,256]{1,0:T(8,128)(2,1)S(1)} %get-tuple-element.179), channel_id=1, source_target_pairs={{0,4},{1,5},{4,8},{5,9},{8,12},{9,13},{12,14},{13,15},{14,10},{15,... | collective-permute-start | bytes 786440 | tf_op jit(solution)/shard_map/ppermute | solution.py:501
  80.2 11.0 %collective-permute-start.23 = (bf16[512,256]{1,0:T(8,128)(2,1)S(1)}, bf16[512,256]{1,0:T(8,128)(2,1)S(1)}, u32[]{:S(2)}, u32[]{:S(2)}) collective-permute-start(bf16[512,256]{1,0:T(8,128)(2,1)S(1)} %get-tuple-element.181), channel_id=1, source_target_pairs={{4,0},{5,1},{8,4},{9,5},{12,8},{13,9},{14,12},{15,13},{10,14},{11,... | collective-permute-start | bytes 786440 | tf_op jit(solution)/shard_map/ppermute | solution.py:501
  82.9 14.0 %collective-permute-start.29 = (bf16[512,256]{1,0:T(8,128)(2,1)S(1)}, bf16[512,256]{1,0:T(8,128)(2,1)S(1)}, u32[]{:S(2)}, u32[]{:S(2)}) collective-permute-start(bf16[512,256]{1,0:T(8,128)(2,1)S(1)} %get-tuple-element.201), channel_id=1, source_target_pairs={{4,0},{5,1},{8,4},{9,5},{12,8},{13,9},{14,12},{15,13},{10,14},{11,... | collective-permute-start | bytes 786440 | tf_op jit(solution)/shard_map/ppermute | solution.py:501
  85.2 11.7 %collective-permute-start.25 = (bf16[512,256]{1,0:T(8,128)(2,1)S(1)}, bf16[512,256]{1,0:T(8,128)(2,1)S(1)}, u32[]{:S(2)}, u32[]{:S(2)}) collective-permute-start(bf16[512,256]{1,0:T(8,128)(2,1)S(1)} %get-tuple-element.202), channel_id=1, source_target_pairs={{0,4},{1,5},{4,8},{5,9},{8,12},{9,13},{12,14},{13,15},{14,10},{15,... | collective-permute-start | bytes 786440 | tf_op jit(solution)/shard_map/ppermute | solution.py:501
  91.4 15.6 %collective-permute-start.27 = (bf16[512,256]{1,0:T(8,128)(2,1)S(1)}, bf16[512,256]{1,0:T(8,128)(2,1)S(1)}, u32[]{:S(2)}, u32[]{:S(2)}) collective-permute-start(bf16[512,256]{1,0:T(8,128)(2,1)S(1)} %get-tuple-element.190), channel_id=1, source_target_pairs={{0,4},{1,5},{4,8},{5,9},{8,12},{9,13},{12,14},{13,15},{14,10},{15,... | collective-permute-start | bytes 786440 | tf_op jit(solution)/shard_map/ppermute | solution.py:501
  96.9 10.1 %collective-permute-start.31 = (bf16[512,256]{1,0:T(8,128)(2,1)S(1)}, bf16[512,256]{1,0:T(8,128)(2,1)S(1)}, u32[]{:S(2)}, u32[]{:S(2)}) collective-permute-start(bf16[512,256]{1,0:T(8,128)(2,1)S(1)} %get-tuple-element.191), channel_id=1, source_target_pairs={{4,0},{5,1},{8,4},{9,5},{12,8},{13,9},{14,12},{15,13},{10,14},{11,... | collective-permute-start | bytes 786440 | tf_op jit(solution)/shard_map/ppermute | solution.py:501
  97.1 10.0 %collective-permute-start.30 = (bf16[512,256]{1,0:T(8,128)(2,1)S(1)}, bf16[512,256]{1,0:T(8,128)(2,1)S(1)}, u32[]{:S(2)}, u32[]{:S(2)}) collective-permute-start(bf16[512,256]{1,0:T(8,128)(2,1)S(1)} %get-tuple-element.199), channel_id=1, source_target_pairs={{4,0},{5,1},{8,4},{9,5},{12,8},{13,9},{14,12},{15,13},{10,14},{11,... | collective-permute-start | bytes 786440 | tf_op jit(solution)/shard_map/ppermute | solution.py:501
  97.2 9.9 %collective-permute-start.26 = (bf16[512,256]{1,0:T(8,128)(2,1)S(1)}, bf16[512,256]{1,0:T(8,128)(2,1)S(1)}, u32[]{:S(2)}, u32[]{:S(2)}) collective-permute-start(bf16[512,256]{1,0:T(8,128)(2,1)S(1)} %get-tuple-element.200), channel_id=1, source_target_pairs={{0,4},{1,5},{4,8},{5,9},{8,12},{9,13},{12,14},{13,15},{14,10},{15,... | collective-permute-start | bytes 786440 | tf_op jit(solution)/shard_map/ppermute | solution.py:501
  (18 other events, 87.4 us)
